TPU v7x, 512 devices: a whole 4x4x16 slice. The times are simulated.
512 devices in a mesh: grp: 16 (over y, x), ep: 32 (over z, core).
Axes of the slice: x: 4, y: 4, z: 16, core: 2. Of those that a mesh axis runs over, the one named last changes fastest.
Arguments:
- tokens: bfloat16 [4096, 4096], P(('grp', 'ep')), may hold values from -6 to 6
- expert_ids: int32 [4096, 8], P(('grp', 'ep')), may hold values from 0 to 63, all different within a row; in each aligned block of 8 rows (0 to 7, 8 to 15, ...) at most 2 rows name the same one
- gate_weights: float32 [4096, 8], P(('grp', 'ep')), may hold values from 0.1 to 1
- w_gate: bfloat16 [32, 4096, 2048], P('ep', None, 'grp'), may hold values from -0.09375 to 0.09375
- w_up: bfloat16 [32, 4096, 2048], P('ep', None, 'grp'), may hold values from -0.09375 to 0.09375
- w_down: bfloat16 [32, 1024, 8192], P('ep', None, 'grp'), may hold values from -0.1875 to 0.1875
- norm_gain: float32 [4096], replicated, may hold values from 0.1 to 1.9
Outputs:
- scored: bfloat16 [4096, 4096], P(('grp', 'ep'))
Inputs may be any that keep to these rules, and one draw needn't show every extreme that they name: `expert_ids`: each row names 8 different experts. Among the 8 rows of one device no expert is named by more than 2 rows, and in some devices' rows an expert is named by exactly 2.
All inputs are finite; a program needn't handle non-finite values.
Results may differ from a plain program's by a relative error of at most 0.0043.
Values may be sent and summed in bfloat16 or wider, within the bound.
No kernel may reach another device: no remote copies, remote signals or barrier semaphores. Data moves between devices by JAX's collectives and lax.ppermute only.
A program may use at most 64 MiB of HBM per device.

v0:
```python
import jax
import jax.numpy as jnp
from jax import lax
from jax.sharding import PartitionSpec as P


def swapped(shard, axis, bit):
    return lax.ppermute(shard, axis, [(i, i ^ 1 << bit) for i in range(lax.axis_size(axis))])


def expert_front(arrived, gate_slice, up_slice):
    gate_part = jnp.einsum("abmd,df->abmf", arrived, gate_slice, preferred_element_type=jnp.float32)
    up_part = jnp.einsum("abmd,df->abmf", arrived, up_slice, preferred_element_type=jnp.float32)
    return (jax.nn.silu(gate_part) * up_part).astype(jnp.bfloat16)


def shards(tokens, expert_ids, gate_weights, w_gate, w_up, w_down, norm_gain):
    tok_rows, width = tokens.shape
    top_count = expert_ids.shape[1]
    n_ep = lax.axis_size("ep")
    n_grp = lax.axis_size("grp")
    experts = 2 * n_ep
    capacity = max(2, 2 * tok_rows * top_count // experts)
    slots = experts * capacity
    span = n_grp // 2
    flat_ids = expert_ids.reshape(-1)
    onehot = (flat_ids[:, None] == jnp.arange(experts, dtype=jnp.int32)[None, :]).astype(jnp.int32)
    earlier = jnp.cumsum(onehot, axis=0) - onehot
    ranking = jnp.sum(earlier * onehot, axis=1)
    slot_ids = jnp.arange(slots, dtype=jnp.int32)
    send_slot = flat_ids % 2 * (n_ep * capacity) + flat_ids // 2 * capacity + ranking
    placing = send_slot.reshape(tok_rows, top_count)[None, :, :] == slot_ids[:, None, None]
    placing = jnp.sum(placing.astype(jnp.float32), axis=2).astype(jnp.bfloat16)
    outgoing = jnp.dot(placing, tokens, preferred_element_type=jnp.float32).astype(jnp.bfloat16)
    outgoing = outgoing.reshape(2, n_ep, capacity, width)
    gate_slice = w_gate[0]
    up_slice = w_up[0]
    arrived = lax.all_to_all(outgoing, "ep", split_axis=1, concat_axis=1, tiled=True)
    fanned = jnp.repeat(arrived, span, axis=0)
    hidden = expert_front(
        lax.all_to_all(fanned, "grp", split_axis=0, concat_axis=0, tiled=True), gate_slice, up_slice
    )
    my_index = lax.axis_index("grp")
    assembled = hidden
    for level in range(span.bit_length() - 1):
        partner = swapped(assembled, "grp", level)
        upper = my_index // (1 << level) % 2
        assembled = jnp.where(
            upper == 0,
            jnp.concatenate([assembled, partner], axis=3),
            jnp.concatenate([partner, assembled], axis=3),
        )
    expert_out = jnp.einsum(
        "abmf,fc->abmc", assembled, w_down[0], preferred_element_type=jnp.float32
    ).astype(jnp.bfloat16)
    returned = lax.all_to_all(expert_out, "grp", split_axis=0, concat_axis=3, tiled=True)
    returned = returned.reshape(n_ep, capacity, 2, width)
    home = lax.all_to_all(returned, "ep", split_axis=0, concat_axis=0, tiled=True)
    back_slot = flat_ids // 2 * (capacity * 2) + ranking * 2 + flat_ids % 2
    matches = back_slot.reshape(tok_rows, top_count)[:, :, None] == slot_ids[None, None, :]
    weight_table = jnp.sum(jnp.where(matches, gate_weights[:, :, None], jnp.float32(0.0)), axis=1)
    combined = jnp.dot(
        weight_table,
        home.reshape(slots, width).astype(jnp.float32),
        precision=lax.Precision.HIGHEST,
    )
    mixed = tokens.astype(jnp.float32) + combined
    factor = lax.rsqrt(jnp.mean(mixed * mixed, axis=1, keepdims=True) + 1e-06)
    return (mixed * factor * norm_gain).astype(jnp.bfloat16)


def solution(mesh):
    placed = (
        P(("grp", "ep"), None),
        P(("grp", "ep"), None),
        P(("grp", "ep"), None),
        P("ep", None, "grp"),
        P("ep", None, "grp"),
        P("ep", None, "grp"),
        P(),
    )
    return jax.shard_map(
        shards, mesh=mesh, in_specs=placed, out_specs=P(("grp", "ep"), None), check_vma=False
    )
```

profile of v0, /device:TPU:1, one launch (start us, length us, event | category | flops | bytes accessed | tf_op | source)
XLA Modules:
  0.0 325.1 jit_solution(393102932788492460)
XLA Ops:
  0.0 0.9 eq.57
  1.3 0.7 add_add_fusion
  2.1 1.3 convolution_convert_fusion
  3.4 0.7 reshape.93
  4.1 1.2 copy.14
  5.3 72.3 %all_to_all.30 = bf16[2,32,2,4096]{3,2,0,1:T(2,128)(2,1)S(1)} all-to-all(bf16[2,32,2,4096]{3,2,0,1:T(2,128)(2,1)S(1)} %copy.14), channel_id=1, replica_groups=mesh['grp'=16,'ep'=32] {'ep'}, dimensions={1} | all-to-all | bytes 2097152 | tf_op jit(solution)/shard_map/all_to_all | solution.py:38
  77.6 0.6 copy.15
  78.2 1.0 broadcast_in_dim.23
  79.2 101.5 %all_to_all.31 = bf16[16,32,2,4096]{3,1,2,0:T(8,128)(2,1)S(1)} all-to-all(bf16[16,32,2,4096]{3,1,2,0:T(8,128)(2,1)S(1)} %bitcast.33), channel_id=1, replica_groups=mesh['grp'=16,'ep'=32] {'grp'}, dimensions={0} | all-to-all | bytes 16777216 | tf_op jit(solution)/shard_map/all_to_all | solution.py:41
  180.7 2.3 fusion.11
  183.1 2.3 fusion.8
  185.4 2.2 collective-permute-start
  187.7 5.6 %collective-permute-done = bf16[16,32,2,128]{3,1,2,0:T(8,128)(2,1)S(1)} collective-permute-done((bf16[16,32,2,128]{3,1,2,0:T(8,128)(2,1)S(1)}, bf16[16,32,2,128]{3,1,2,0:T(8,128)(2,1)S(1)}, u32[]{:S(2)}, u32[]{:S(2)}) %collective-permute-start) | collective-permute-done | bytes 262176 | tf_op jit(solution)/shard_map/ppermute | solution.py:8
  193.5 3.0 collective-permute-start.1
  196.5 10.9 %collective-permute-done.1 = bf16[16,32,2,256]{3,1,2,0:T(8,128)(2,1)S(1)} collective-permute-done((bf16[16,32,2,256]{3,1,2,0:T(8,128)(2,1)S(1)}, bf16[16,32,2,256]{3,1,2,0:T(8,128)(2,1)S(1)}, u32[]{:S(2)}, u32[]{:S(2)}) %collective-permute-start.1) | collective-permute-done | bytes 524320 | tf_op jit(solution)/shard_map/ppermute | solution.py:8
  207.8 2.2 collective-permute-start.2
  210.1 20.6 %collective-permute-done.2 = bf16[16,32,2,512]{3,1,2,0:T(8,128)(2,1)} collective-permute-done((bf16[16,32,2,512]{3,1,2,0:T(8,128)(2,1)S(1)}, bf16[16,32,2,512]{3,1,2,0:T(8,128)(2,1)}, u32[]{:S(2)}, u32[]{:S(2)}) %collective-permute-start.2) | collective-permute-done | bytes 1048608 | tf_op jit(solution)/shard_map/ppermute | solution.py:8
  230.7 2.8 fusion.7
  233.5 18.2 %all_to_all.32 = bf16[16,32,2,512]{3,1,2,0:T(8,128)(2,1)S(1)} all-to-all(bf16[16,32,2,512]{3,1,2,0:T(8,128)(2,1)S(1)} %fusion.7), channel_id=1, replica_groups=mesh['grp'=16,'ep'=32] {'grp'}, dimensions={0} | all-to-all | bytes 2097152 | tf_op jit(solution)/shard_map/all_to_all | solution.py:56
  252.3 1.6 reshape.95
  253.9 13.7 %all-to-all-start.3 = ((bf16[32,2,2,4096]{3,2,1,0:T(2,128)(2,1)}), bf16[32,2,2,4096]{3,2,1,0:T(2,128)(2,1)S(1)}, u32[]{:S(2)}, u32[]{:S(2)}) async-start(bf16[32,2,2,4096]{3,2,1,0:T(2,128)(2,1)} %reshape.95), calls=%async_computation.3 | async-start | bytes 2097152 | tf_op jit(solution)/shard_map/all_to_all | solution.py:58
  267.7 55.6 %all-to-all-done.3 = bf16[32,2,2,4096]{3,2,1,0:T(2,128)(2,1)S(1)} async-done(((bf16[32,2,2,4096]{3,2,1,0:T(2,128)(2,1)}), bf16[32,2,2,4096]{3,2,1,0:T(2,128)(2,1)S(1)}, u32[]{:S(2)}, u32[]{:S(2)}) %all-to-all-start.3) | async-done | bytes 1048608 | tf_op jit(solution)/shard_map/all_to_all | solution.py:58
  323.7 0.6 multiply_reduce_fusion
  324.4 0.7 multiply_convert_fusion
  (23 shorter events, 2.3 us)
Async XLA Ops:
  0.0 230.7 %copy-start = (bf16[1,1024,512]{2,1,0:T(8,128)(2,1)S(1)}, bf16[1,1024,512]{2,1,0:T(8,128)(2,1)}, u32[]{:S(2)}) copy-start(bf16[1,1024,512]{2,1,0:T(8,128)(2,1)} %param.12) | copy-start | bytes 3145732
  79.2 101.5 %copy-start.4 = (bf16[1,4096,128]{2,1,0:T(8,128)(2,1)S(1)}, bf16[1,4096,128]{2,1,0:T(8,128)(2,1)}, u32[]{:S(2)}) copy-start(bf16[1,4096,128]{2,1,0:T(8,128)(2,1)} %param.10) | copy-start | bytes 3145732
  180.7 2.3 copy-start.5
  185.4 7.8 %collective-permute-start = (bf16[16,32,2,128]{3,1,2,0:T(8,128)(2,1)S(1)}, bf16[16,32,2,128]{3,1,2,0:T(8,128)(2,1)S(1)}, u32[]{:S(2)}, u32[]{:S(2)}) collective-permute-start(bf16[16,32,2,128]{3,1,2,0:T(8,128)(2,1)S(1)} %fusion.8), channel_id=1, source_target_pairs={{0,32},{32,0},{64,96},{96,64},{128,160},{160,128},{192,224},{224,1... | collective-permute-start | bytes 786440 | tf_op jit(solution)/shard_map/ppermute | solution.py:8
  193.5 14.0 %collective-permute-start.1 = (bf16[16,32,2,256]{3,1,2,0:T(8,128)(2,1)S(1)}, bf16[16,32,2,256]{3,1,2,0:T(8,128)(2,1)S(1)}, u32[]{:S(2)}, u32[]{:S(2)}) collective-permute-start(bf16[16,32,2,256]{3,1,2,0:T(8,128)(2,1)S(1)} %maximum_select_fusion.5), channel_id=1, source_target_pairs={{0,64},{32,96},{64,0},{96,32},{128,192},{160,224},{192,128},{224,1... | collective-permute-start | bytes 1572872 | tf_op jit(solution)/shard_map/ppermute | solution.py:8
  207.8 22.9 %collective-permute-start.2 = (bf16[16,32,2,512]{3,1,2,0:T(8,128)(2,1)S(1)}, bf16[16,32,2,512]{3,1,2,0:T(8,128)(2,1)}, u32[]{:S(2)}, u32[]{:S(2)}) collective-permute-start(bf16[16,32,2,512]{3,1,2,0:T(8,128)(2,1)S(1)} %maximum_select_fusion.4), channel_id=1, source_target_pairs={{0,128},{32,160},{64,192},{96,224},{128,0},{160,32},{192,64},{224,... | collective-permute-start | bytes 3145736 | tf_op jit(solution)/shard_map/ppermute | solution.py:8
  252.3 15.3 %copy-start.3 = (f32[8,8]{1,0:T(8,128)S(1)}, f32[8,8]{1,0:T(8,128)}, u32[]{:S(2)}) copy-start(f32[8,8]{1,0:T(8,128)} %param.9) | copy-start | bytes 772
  253.9 69.8 %copy-start.1 = (bf16[8,4096]{1,0:T(8,128)(2,1)S(1)}, bf16[8,4096]{1,0:T(8,128)(2,1)}, u32[]{:S(2)}) copy-start(bf16[8,4096]{1,0:T(8,128)(2,1)} %param.7) | copy-start | bytes 196612
  253.9 69.4 %all-to-all-start.3 = ((bf16[32,2,2,4096]{3,2,1,0:T(2,128)(2,1)}), bf16[32,2,2,4096]{3,2,1,0:T(2,128)(2,1)S(1)}, u32[]{:S(2)}, u32[]{:S(2)}) async-start(bf16[32,2,2,4096]{3,2,1,0:T(2,128)(2,1)} %reshape.95), calls=%async_computation.3 | async-start | bytes 2097152 | tf_op jit(solution)/shard_map/all_to_all | solution.py:58
  267.6 56.8 %copy-start.2 = (f32[4096]{0:T(1024)S(1)}, f32[4096]{0:T(1024)}, u32[]{:S(2)}) copy-start(f32[4096]{0:T(1024)} %param.13) | copy-start | bytes 49156
where the time goes:
time: 326 us; the launch traced here: 325 us
  blocking collectives  192 us (59%)
  waiting for transfers between devices  92.7 us (28%)
  starting transfers between devices  21.1 us (6%)
  matrix products  9.42 us (3%)
  local copies, waits for them, and re-layouts  7.06 us (2%)
    all_to_all x1, blocking collectives, shards(): lax.all_to_all(fanned, 'grp', split_axis=0, concat_axis=0, tiled=True)  102 us
    all_to_all x1, blocking collectives, shards(): lax.all_to_all(outgoing, 'ep', split_axis=1, concat_axis=1, tiled=True)  72.3 us
    all_to_all x1, waiting for transfers between devices, shards(): lax.all_to_all(returned, 'ep', split_axis=0, concat_axis=0, tiled=True)  55.6 us
    ppermute x3, waiting for transfers between devices, swapped(): lax.ppermute(shard, axis, [(i, i ^ 1 << bit) for i in range(lax.axis_size...  37.1 us
    all_to_all x1, blocking collectives, shards(): lax.all_to_all(expert_out, 'grp', split_axis=0, concat_axis=3, tiled=True)  18.2 us
    all_to_all x1, starting transfers between devices, shards(): lax.all_to_all(returned, 'ep', split_axis=0, concat_axis=0, tiled=True)  13.7 us
    ppermute x3, starting transfers between devices, swapped(): lax.ppermute(shard, axis, [(i, i ^ 1 << bit) for i in range(lax.axis_size...  7.43 us
  transfers between devices with their start and end apart: 4, of which 4 were waited for; matrix products, arithmetic and copies ran while one was open for 0% of the time, Pallas kernels for 0%

commit v1 on v0

v1 whole, which is shorter than its diff:
```python
import jax
import jax.numpy as jnp
from jax import lax
from jax.sharding import PartitionSpec as P

BF16 = jnp.bfloat16
F32 = jnp.float32


def around(block, chips):
    size = lax.axis_size("ep")
    return lax.ppermute(block, "ep", [(i, (i + 2 * chips) % size) for i in range(size)])


def core_swap(block):
    return lax.ppermute(block, "ep", [(i, i ^ 1) for i in range(lax.axis_size("ep"))])


def pair_swap(block):
    return lax.ppermute(block, "grp", [(i, i ^ 4) for i in range(lax.axis_size("grp"))])


EIGHTS = [[0, 1, 2, 3, 12, 13, 14, 15], [4, 5, 6, 7, 8, 9, 10, 11]]
FOURS = [[4 * y + x for x in range(4)] for y in range(4)]


def gather_column(block):
    n = block.shape[0]
    three = jnp.concatenate([block, around(block, 5), around(block, -5)], 0)
    below2, above2 = around(three, 2), around(three, -2)
    eighth = around(three[2 * n:], -3)
    below1, above1 = around(three, 1), around(three, -1)
    column = jnp.concatenate([three, below1, above1, below2, above2, eighth], 0)
    return column


def scatter_group(column, n):
    sent = column[3 * n:].astype(BF16)
    below1, above1, below2, above2 = (sent[3 * n * i:3 * n * (i + 1)] for i in range(4))
    from_above2, from_below2 = around(below2, -2), around(above2, 2)
    eighth = around(sent[12 * n:], 3)
    from_above1, from_below1 = around(below1, -1), around(above1, 1)
    part = column[:3 * n]
    for other in (from_above2, from_below2, from_above1, from_below1):
        part = part + other.astype(F32)
    below = around(part[n:2 * n].astype(BF16), -5)
    above = around((part[2 * n:] + eighth.astype(F32)).astype(BF16), 5)
    return part[:n] + below.astype(F32) + above.astype(F32)


def shards(tokens, expert_ids, gate_weights, w_gate, w_up, w_down, norm_gain):
    n, width = tokens.shape
    top = expert_ids.shape[1]
    g = lax.axis_index("grp")
    p = lax.axis_index("ep")
    odd_row = g // 4 % 2 == 1

    gate_own, up_own, down_own = w_gate[0], w_up[0], w_down[0]
    gate_other, up_other, down_other = pair_swap(gate_own), pair_swap(up_own), pair_swap(down_own)

    high = lax.reduce_precision(gate_weights, 8, 7)
    low = gate_weights - high
    extra = jnp.concatenate([expert_ids.astype(F32), high, low], 1).astype(BF16)
    extra = jnp.pad(extra, ((0, 0), (0, 128 - 3 * top)))
    column = gather_column(jnp.concatenate([tokens, extra], 1))
    column, gate_other = lax.optimization_barrier((column, gate_other))
    parts = column, core_swap(column)
    half = parts[0].shape[0]
    rows = 2 * half
    slots = rows // 4

    take = (jnp.arange(3 * top)[:, None] == jnp.arange(128)[None, :]).astype(BF16)
    facts = [
        lax.dot_general(take, part[:, width:], (((1,), (1,)), ((), ())), preferred_element_type=F32)
        for part in parts
    ]
    facts = jnp.concatenate(facts, 1).reshape(3, top, rows)

    experts = (2 * p + jnp.arange(2)).astype(F32)
    match = facts[0][None] == experts[:, None, None]
    hit = jnp.any(match, axis=1)
    before = jnp.arange(rows)[:, None] < jnp.arange(rows)[None, :]
    place = jnp.dot(hit.astype(BF16), before.astype(BF16), preferred_element_type=F32)
    place = jnp.where(hit, place, -1.0)
    picks = place[:, None, :] == jnp.arange(slots, dtype=F32)[None, :, None]
    picks = picks.reshape(2 * slots, rows)
    onehot = picks.astype(BF16)
    chosen = jnp.dot(onehot[:, :half], parts[0][:, :width], preferred_element_type=F32)
    chosen = chosen + jnp.dot(onehot[:, half:], parts[1][:, :width], preferred_element_type=F32)
    chosen = chosen.astype(BF16)

    fanned = jnp.broadcast_to(chosen.reshape(2, 1, slots, width), (2, 4, slots, width)).reshape(8, slots, width)
    arrived = lax.all_to_all(fanned, "grp", split_axis=0, concat_axis=0, tiled=True, axis_index_groups=EIGHTS)
    arrived = arrived.reshape(8 * slots, width)

    def front(gate, up):
        a = jnp.dot(arrived, gate, preferred_element_type=F32)
        b = jnp.dot(arrived, up, preferred_element_type=F32)
        return (jax.nn.silu(a) * b).astype(BF16)

    mine, theirs = front(gate_own, up_own), front(gate_other, up_other)
    hidden = jnp.where(odd_row, jnp.concatenate([theirs, mine], 1), jnp.concatenate([mine, theirs], 1))
    hidden, down_other = lax.optimization_barrier((hidden, down_other))
    units = mine.shape[1]
    hidden = jnp.broadcast_to(hidden[None], (4,) + hidden.shape)
    hidden = lax.all_to_all(hidden, "grp", split_axis=0, concat_axis=0, tiled=True, axis_index_groups=FOURS)
    hidden = jnp.concatenate(
        [hidden[x, :, units * at:units * (at + 1)] for at in range(2) for x in range(4)], 1
    )

    out_own = jnp.dot(hidden, down_own, preferred_element_type=F32).astype(BF16)
    out_other = jnp.dot(hidden, down_other, preferred_element_type=F32).astype(BF16)
    out = jnp.where(odd_row, jnp.concatenate([out_other, out_own], 1), jnp.concatenate([out_own, out_other], 1))
    features = out_own.shape[1]
    out = out.reshape(8, slots, 2 * features)
    home = lax.all_to_all(out, "grp", split_axis=0, concat_axis=0, tiled=True, axis_index_groups=EIGHTS)
    home = jnp.concatenate(
        [
            jnp.concatenate(
                [home[4 * of + x, :, features * at:features * (at + 1)] for at in range(2) for x in range(4)], 1
            )
            for of in range(2)
        ],
        0,
    )

    def weight(at):
        summed = jnp.sum(jnp.where(match, facts[at][None], 0.0), axis=1)
        summed = jnp.broadcast_to(summed[:, None], (2, slots, rows)).reshape(2 * slots, rows)
        return jnp.where(picks, summed, 0.0).astype(BF16)

    table = jnp.concatenate([weight(1), weight(2)], 0)
    home = jnp.concatenate([home, home], 0)

    def weighted(at):
        return lax.dot_general(at, home, (((0,), (0,)), ((), ())), preferred_element_type=F32)

    swapped = core_swap(weighted(table[:, half:]).astype(BF16))
    column = weighted(table[:, :half]) + swapped.astype(F32)
    mixed = tokens.astype(F32) + scatter_group(column, n)
    factor = lax.rsqrt(jnp.mean(mixed * mixed, axis=1, keepdims=True) + 1e-06)
    return (mixed * factor * norm_gain).astype(BF16)


def solution(mesh):
    placed = (
        P(("grp", "ep"), None),
        P(("grp", "ep"), None),
        P(("grp", "ep"), None),
        P("ep", None, "grp"),
        P("ep", None, "grp"),
        P("ep", None, "grp"),
        P(),
    )
    return jax.shard_map(
        shards, mesh=mesh, in_specs=placed, out_specs=P(("grp", "ep"), None), check_vma=False
    )
```

time: 326 us -> 246 us (0.75)
  blocking collectives: 192 us -> 27.3 us
  starting transfers between devices: 21.1 us -> 96.6 us
  matrix products: 9.42 us -> 21.5 us
  local copies, waits for them, and re-layouts: 7.06 us -> 3.44 us
  other arithmetic: 2.6 us -> 5.94 us
    all_to_all x3 -> x1, blocking collectives: 192 us -> 27.3 us  [shards(): lax.all_to_all(hidden, 'grp', split_axis=0, concat_axis=0, tiled=True, ax...]
    ppermute x3 -> x19, starting transfers between devices: 7.43 us -> 85.8 us  [the longest x14 66.2 us: around(): lax.ppermute(block, 'ep', [(i, (i + 2 * chips) % size) for i in range(siz...]
    dot_general x5 -> x13, matrix products: 9.42 us -> 21.5 us  [the longest x2 8 us: front(): b = jnp.dot(arrived, up, preferred_element_type=F32)]
    ppermute x3 -> x19, waiting for transfers between devices: 37.1 us -> 27.5 us  [the longest x14 23.1 us: around(): lax.ppermute(block, 'ep', [(i, (i + 2 * chips) % size) for i in range(siz...]
    all_to_all x1 -> x2, waiting for transfers between devices: 55.6 us -> 62.1 us  [the longest x1 45.5 us: shards(): lax.all_to_all(fanned, 'grp', split_axis=0, concat_axis=0, tiled=True, ax...]
    reshape x4 -> x0, local copies, waits for them, and re-layouts: 3.9 us -> none  [the longest x2 1.88 us: shards(): outgoing = outgoing.reshape(2, n_ep, capacity, width)]
    all_to_all x1 -> x2, starting transfers between devices: 13.7 us -> 10.9 us  [the longest x1 6.6 us: shards(): lax.all_to_all(fanned, 'grp', split_axis=0, concat_axis=0, tiled=True, ax...]
  transfers between devices with their start and end apart: 4 -> 21, of which waited for: 4 -> 11; matrix products, arithmetic and copies ran while one was open for 0% -> 7% of each run, Pallas kernels for 0% -> 0%
where the time goes in v1:
time: 246 us; the launch traced here: 245 us
  starting transfers between devices  96.6 us (39%)
  waiting for transfers between devices  89.6 us (36%)
  blocking collectives  27.3 us (11%)
  matrix products  21.5 us (9%)
  other arithmetic  5.94 us (2%)
  local copies, waits for them, and re-layouts  3.44 us (1%)
    ppermute x14, starting transfers between devices, around(): lax.ppermute(block, 'ep', [(i, (i + 2 * chips) % size) for i in range(siz...  66.2 us
    all_to_all x1, waiting for transfers between devices, shards(): lax.all_to_all(fanned, 'grp', split_axis=0, concat_axis=0, tiled=True, ax...  45.5 us
    all_to_all x1, blocking collectives, shards(): lax.all_to_all(hidden, 'grp', split_axis=0, concat_axis=0, tiled=True, ax...  27.3 us
    ppermute x14, waiting for transfers between devices, around(): lax.ppermute(block, 'ep', [(i, (i + 2 * chips) % size) for i in range(siz...  23.1 us
    all_to_all x1, waiting for transfers between devices, shards(): lax.all_to_all(out, 'grp', split_axis=0, concat_axis=0, tiled=True, axis_...  16.5 us
    ppermute x2, starting transfers between devices, core_swap(): lax.ppermute(block, 'ep', [(i, i ^ 1) for i in range(lax.axis_size('ep'))])  11.1 us
    ppermute x3, starting transfers between devices, pair_swap(): lax.ppermute(block, 'grp', [(i, i ^ 4) for i in range(lax.axis_size('grp'...  8.48 us
    dot_general x2, matrix products, front(): b = jnp.dot(arrived, up, preferred_element_type=F32)  8 us
  transfers between devices with their start and end apart: 21, of which 11 were waited for; matrix products, arithmetic and copies ran while one was open for 7% of the time, Pallas kernels for 0%

profile of v1, /device:TPU:1, one launch (start us, length us, event | category | flops | bytes accessed | tf_op | source)
XLA Modules:
  0.0 245.0 jit_solution(17348579396099652398)
XLA Ops:
  2.3 11.0 %collective-permute-start = (bf16[8,4224]{1,0:T(8,128)(2,1)S(1)}, bf16[8,4224]{1,0:T(8,128)(2,1)S(1)}, u32[]{:S(2)}, u32[]{:S(2)}) collective-permute-start(bf16[8,4224]{1,0:T(8,128)(2,1)S(1)} %get-tuple-element.35), channel_id=1, source_target_pairs={{0,10},{1,11},{2,12},{3,13},{4,14},{5,15},{6,16},{7,17},{8,18},{9,... | collective-permute-start | bytes 202760 | tf_op jit(solution)/shard_map/ppermute | solution.py:12
  13.3 5.9 %collective-permute-start.1 = (bf16[8,4224]{1,0:T(8,128)(2,1)S(1)}, bf16[8,4224]{1,0:T(8,128)(2,1)S(1)}, u32[]{:S(2)}, u32[]{:S(2)}) collective-permute-start(bf16[8,4224]{1,0:T(8,128)(2,1)S(1)} %get-tuple-element.35), channel_id=1, source_target_pairs={{0,22},{1,23},{2,24},{3,25},{4,26},{5,27},{6,28},{7,29},{8,30},{9,... | collective-permute-start | bytes 202760 | tf_op jit(solution)/shard_map/ppermute | solution.py:12
  19.2 3.2 %collective-permute-start.7 = (bf16[4096,128]{1,0:T(8,128)(2,1)}, bf16[4096,128]{1,0:T(8,128)(2,1)S(1)}, u32[]{:S(2)}, u32[]{:S(2)}) collective-permute-start(bf16[4096,128]{1,0:T(8,128)(2,1)} %bitcast.136), channel_id=1, source_target_pairs={{0,128},{32,160},{64,192},{96,224},{128,0},{160,32},{192,64},{224,... | collective-permute-start | bytes 3145736 | tf_op jit(solution)/shard_map/ppermute | solution.py:20
  27.8 4.4 %collective-permute-start.3 = (bf16[24,4224]{1,0:T(8,128)(2,1)S(1)}, bf16[24,4224]{1,0:T(8,128)(2,1)S(1)}, u32[]{:S(2)}, u32[]{:S(2)}) collective-permute-start(bf16[24,4224]{1,0:T(8,128)(2,1)S(1)} %pad_maximum_fusion.5), channel_id=1, source_target_pairs={{0,30},{1,31},{2,0},{3,1},{4,2},{5,3},{6,4},{7,5},{8,6},{9,7},{10,... | collective-permute-start | bytes 608264 | tf_op jit(solution)/shard_map/ppermute | solution.py:12
  32.2 9.9 %collective-permute-start.4 = (bf16[24,4224]{1,0:T(8,128)(2,1)S(1)}, bf16[24,4224]{1,0:T(8,128)(2,1)S(1)}, u32[]{:S(2)}, u32[]{:S(2)}) collective-permute-start(bf16[24,4224]{1,0:T(8,128)(2,1)S(1)} %pad_maximum_fusion.5), channel_id=1, source_target_pairs={{0,4},{1,5},{2,6},{3,7},{4,8},{5,9},{6,10},{7,11},{8,12},{9,13},{1... | collective-permute-start | bytes 608264 | tf_op jit(solution)/shard_map/ppermute | solution.py:12
  47.3 5.8 %collective-permute-done.5 = bf16[24,4224]{1,0:T(8,128)(2,1)S(1)} collective-permute-done((bf16[24,4224]{1,0:T(8,128)(2,1)S(1)}, bf16[24,4224]{1,0:T(8,128)(2,1)S(1)}, u32[]{:S(2)}, u32[]{:S(2)}) %collective-permute-start.5) | collective-permute-done | bytes 202784 | tf_op jit(solution)/shard_map/ppermute | solution.py:12
  54.7 8.0 %collective-permute-start.8 = (bf16[128,4224]{1,0:T(8,128)(2,1)S(1)}, bf16[128,4224]{1,0:T(8,128)(2,1)S(1)}, u32[]{:S(2)}, u32[]{:S(2)}) collective-permute-start(bf16[128,4224]{1,0:T(8,128)(2,1)S(1)} %constant_dynamic-update-slice_fusion), channel_id=1, source_target_pairs={{0,1},{1,0},{2,3},{3,2},{4,5},{5,4},{6,7},{7,6},{8,9},{9,8},{10,11... | collective-permute-start | bytes 3244040 | tf_op jit(solution)/shard_map/ppermute | solution.py:16
  68.9 6.6 %all-to-all-start = ((bf16[8,64,4096]{2,1,0:T(8,128)(2,1)}), bf16[8,64,4096]{2,1,0:T(8,128)(2,1)}, u32[]{:S(2)}, u32[]{:S(2)}) async-start(bf16[8,64,4096]{2,1,0:T(8,128)(2,1)} %bitcast.134), calls=%async_computation | async-start | bytes 8388608 | tf_op jit(solution)/shard_map/all_to_all | solution.py:93
  77.5 3.4 %collective-permute-start.10 = (bf16[1024,512]{1,0:T(8,128)(2,1)}, bf16[1024,512]{1,0:T(8,128)(2,1)}, u32[]{:S(2)}, u32[]{:S(2)}) collective-permute-start(bf16[1024,512]{1,0:T(8,128)(2,1)} %bitcast.8), channel_id=1, source_target_pairs={{0,128},{32,160},{64,192},{96,224},{128,0},{160,32},{192,64},{224,... | collective-permute-start | bytes 3145736 | tf_op jit(solution)/shard_map/ppermute | solution.py:20
  80.9 45.5 %all-to-all-done = bf16[8,64,4096]{2,1,0:T(8,128)(2,1)} async-done(((bf16[8,64,4096]{2,1,0:T(8,128)(2,1)}), bf16[8,64,4096]{2,1,0:T(8,128)(2,1)}, u32[]{:S(2)}, u32[]{:S(2)}) %all-to-all-start) | async-done | bytes 4194336 | tf_op jit(solution)/shard_map/all_to_all | solution.py:93
  126.4 3.7 %fusion.45 = f32[512,128]{0,1:T(8,128)S(1)} fusion(bf16[512,4096]{1,0:T(8,128)(2,1)} %bitcast.6, bf16[1,4096,128]{2,1,0:T(8,128)(2,1)S(1)} %copy-done.1), kind=kOutput, calls=%fused_computation.133 | convolution fusion | flops 536870912 | bytes 5505024 | tf_op jit(solution)/shard_map/dot_general | solution.py:97
  130.1 3.7 %fusion.49 = f32[512,128]{0,1:T(8,128)S(1)} fusion(bf16[512,4096]{1,0:T(8,128)(2,1)} %bitcast.6, bf16[4096,128]{1,0:T(8,128)(2,1)S(1)} %collective-permute-done.7), kind=kOutput, calls=%fused_computation.137 | convolution fusion | flops 536870912 | bytes 5505024 | tf_op jit(solution)/shard_map/dot_general | solution.py:97
  133.8 4.0 %fusion.1 = bf16[512,128]{0,1:T(8,128)(2,1)S(1)} fusion(bf16[512,4096]{1,0:T(8,128)(2,1)} %bitcast.6, f32[512,128]{0,1:T(8,128)S(1)} %fusion.45, bf16[1,4096,128]{2,1,0:T(8,128)(2,1)} %param.11), kind=kOutput, calls=%fused_computation.8 | convolution fusion | flops 537264128 | bytes 5636096 | tf_op jit(solution)/shard_map/dot_general | solution.py:98
  137.8 4.0 %multiply_convert_fusion = bf16[512,128]{0,1:T(8,128)(2,1)S(1)} fusion(f32[512,128]{0,1:T(8,128)S(1)} %fusion.49, bf16[512,4096]{1,0:T(8,128)(2,1)} %bitcast.6, bf16[4096,128]{1,0:T(8,128)(2,1)} %collective-permute-done.9), kind=kOutput, calls=%fused_computation.20 | convolution fusion | flops 537264128 | bytes 5636096 | tf_op jit(solution)/shard_map/dot_general | solution.py:98
  142.1 27.3 %all_to_all.15 = bf16[4,512,256]{2,1,0:T(8,128)(2,1)S(1)} all-to-all(bf16[4,512,256]{2,1,0:T(8,128)(2,1)S(1)} %broadcast_in_dim.70), channel_id=1, replica_groups={{0,32,64,96},{128,160,192,224},{256,288,320,352},{384,416,448,480},{1,3..., dimensions={0} | all-to-all | bytes 2097152 | tf_op jit(solution)/shard_map/all_to_all | solution.py:106
  175.0 4.3 %all-to-all-start.2 = ((bf16[8,64,1024]{2,1,0:T(8,128)(2,1)}), bf16[8,64,1024]{2,1,0:T(8,128)(2,1)S(1)}, u32[]{:S(2)}, u32[]{:S(2)}) async-start(bf16[8,64,1024]{2,1,0:T(8,128)(2,1)} %maximum_select_fusion), calls=%async_computation.2 | async-start | bytes 2097152 | tf_op jit(solution)/shard_map/all_to_all | solution.py:116
  179.5 16.5 %all-to-all-done.2 = bf16[8,64,1024]{2,1,0:T(8,128)(2,1)S(1)} async-done(((bf16[8,64,1024]{2,1,0:T(8,128)(2,1)}), bf16[8,64,1024]{2,1,0:T(8,128)(2,1)S(1)}, u32[]{:S(2)}, u32[]{:S(2)}) %all-to-all-start.2) | async-done | bytes 1048608 | tf_op jit(solution)/shard_map/all_to_all | solution.py:116
  196.6 3.1 %collective-permute-start.11 = (bf16[128,4096]{1,0:T(8,128)(2,1)S(1)}, bf16[128,4096]{1,0:T(8,128)(2,1)S(1)}, u32[]{:S(2)}, u32[]{:S(2)}) collective-permute-start(bf16[128,4096]{1,0:T(8,128)(2,1)S(1)} %convolution_convert_fusion), channel_id=1, source_target_pairs={{0,1},{1,0},{2,3},{3,2},{4,5},{5,4},{6,7},{7,6},{8,9},{9,8},{10,11... | collective-permute-start | bytes 3145736 | tf_op jit(solution)/shard_map/ppermute | solution.py:16
  202.6 4.9 %collective-permute-start.15 = (bf16[24,4096]{1,0:T(8,128)(2,1)S(1)}, bf16[24,4096]{1,0:T(8,128)(2,1)S(1)}, u32[]{:S(2)}, u32[]{:S(2)}) collective-permute-start(bf16[24,4096]{1,0:T(8,128)(2,1)S(1)} %get-tuple-element.16), channel_id=1, source_target_pairs={{0,2},{1,3},{2,4},{3,5},{4,6},{5,7},{6,8},{7,9},{8,10},{9,11},{10,... | collective-permute-start | bytes 589832 | tf_op jit(solution)/shard_map/ppermute | solution.py:12
  212.5 4.3 %collective-permute-start.12 = (bf16[24,4096]{1,0:T(8,128)(2,1)S(1)}, bf16[24,4096]{1,0:T(8,128)(2,1)S(1)}, u32[]{:S(2)}, u32[]{:S(2)}) collective-permute-start(bf16[24,4096]{1,0:T(8,128)(2,1)S(1)} %get-tuple-element.15), channel_id=1, source_target_pairs={{0,28},{1,29},{2,30},{3,31},{4,0},{5,1},{6,2},{7,3},{8,4},{9,5},{1... | collective-permute-start | bytes 589832 | tf_op jit(solution)/shard_map/ppermute | solution.py:12
  218.8 5.7 %collective-permute-done.13 = bf16[24,4096]{1,0:T(8,128)(2,1)S(1)} collective-permute-done((bf16[24,4096]{1,0:T(8,128)(2,1)S(1)}, bf16[24,4096]{1,0:T(8,128)(2,1)S(1)}, u32[]{:S(2)}, u32[]{:S(2)}) %collective-permute-start.13) | collective-permute-done | bytes 196640 | tf_op jit(solution)/shard_map/ppermute | solution.py:12
  226.6 6.4 %collective-permute-start.18 = (bf16[8,4096]{1,0:T(8,128)(2,1)S(1)}, bf16[8,4096]{1,0:T(8,128)(2,1)S(1)}, u32[]{:S(2)}, u32[]{:S(2)}) collective-permute-start(bf16[8,4096]{1,0:T(8,128)(2,1)S(1)} %fusion.9), channel_id=1, source_target_pairs={{0,10},{1,11},{2,12},{3,13},{4,14},{5,15},{6,16},{7,17},{8,18},{9,... | collective-permute-start | bytes 196616 | tf_op jit(solution)/shard_map/ppermute | solution.py:12
  233.0 4.9 %collective-permute-start.16 = (bf16[8,4096]{1,0:T(8,128)(2,1)S(1)}, bf16[8,4096]{1,0:T(8,128)(2,1)S(1)}, u32[]{:S(2)}, u32[]{:S(2)}) collective-permute-start(bf16[8,4096]{1,0:T(8,128)(2,1)S(1)} %slice.354), channel_id=1, source_target_pairs={{0,22},{1,23},{2,24},{3,25},{4,26},{5,27},{6,28},{7,29},{8,30},{9,... | collective-permute-start | bytes 196616 | tf_op jit(solution)/shard_map/ppermute | solution.py:12
  237.9 4.2 %collective-permute-done.18 = bf16[8,4096]{1,0:T(8,128)(2,1)S(1)} collective-permute-done((bf16[8,4096]{1,0:T(8,128)(2,1)S(1)}, bf16[8,4096]{1,0:T(8,128)(2,1)S(1)}, u32[]{:S(2)}, u32[]{:S(2)}) %collective-permute-start.18) | collective-permute-done | bytes 65568 | tf_op jit(solution)/shard_map/ppermute | solution.py:12
  (87 shorter events, 43.7 us)
Async XLA Ops:
  2.3 20.1 %collective-permute-start = (bf16[8,4224]{1,0:T(8,128)(2,1)S(1)}, bf16[8,4224]{1,0:T(8,128)(2,1)S(1)}, u32[]{:S(2)}, u32[]{:S(2)}) collective-permute-start(bf16[8,4224]{1,0:T(8,128)(2,1)S(1)} %get-tuple-element.35), channel_id=1, source_target_pairs={{0,10},{1,11},{2,12},{3,13},{4,14},{5,15},{6,16},{7,17},{8,18},{9,... | collective-permute-start | bytes 202760 | tf_op jit(solution)/shard_map/ppermute | solution.py:12
  13.3 11.0 %collective-permute-start.1 = (bf16[8,4224]{1,0:T(8,128)(2,1)S(1)}, bf16[8,4224]{1,0:T(8,128)(2,1)S(1)}, u32[]{:S(2)}, u32[]{:S(2)}) collective-permute-start(bf16[8,4224]{1,0:T(8,128)(2,1)S(1)} %get-tuple-element.35), channel_id=1, source_target_pairs={{0,22},{1,23},{2,24},{3,25},{4,26},{5,27},{6,28},{7,29},{8,30},{9,... | collective-permute-start | bytes 202760 | tf_op jit(solution)/shard_map/ppermute | solution.py:12
  19.2 35.5 %collective-permute-start.7 = (bf16[4096,128]{1,0:T(8,128)(2,1)}, bf16[4096,128]{1,0:T(8,128)(2,1)S(1)}, u32[]{:S(2)}, u32[]{:S(2)}) collective-permute-start(bf16[4096,128]{1,0:T(8,128)(2,1)} %bitcast.136), channel_id=1, source_target_pairs={{0,128},{32,160},{64,192},{96,224},{128,0},{160,32},{192,64},{224,... | collective-permute-start | bytes 3145736 | tf_op jit(solution)/shard_map/ppermute | solution.py:20
  25.2 18.9 %collective-permute-start.2 = (bf16[24,4224]{1,0:T(8,128)(2,1)S(1)}, bf16[24,4224]{1,0:T(8,128)(2,1)S(1)}, u32[]{:S(2)}, u32[]{:S(2)}) collective-permute-start(bf16[24,4224]{1,0:T(8,128)(2,1)S(1)} %pad_maximum_fusion.5), channel_id=1, source_target_pairs={{0,2},{1,3},{2,4},{3,5},{4,6},{5,7},{6,8},{7,9},{8,10},{9,11},{10,... | collective-permute-start | bytes 608264 | tf_op jit(solution)/shard_map/ppermute | solution.py:12
  27.8 19.4 %collective-permute-start.3 = (bf16[24,4224]{1,0:T(8,128)(2,1)S(1)}, bf16[24,4224]{1,0:T(8,128)(2,1)S(1)}, u32[]{:S(2)}, u32[]{:S(2)}) collective-permute-start(bf16[24,4224]{1,0:T(8,128)(2,1)S(1)} %pad_maximum_fusion.5), channel_id=1, source_target_pairs={{0,30},{1,31},{2,0},{3,1},{4,2},{5,3},{6,4},{7,5},{8,6},{9,7},{10,... | collective-permute-start | bytes 608264 | tf_op jit(solution)/shard_map/ppermute | solution.py:12
  32.2 15.0 %collective-permute-start.4 = (bf16[24,4224]{1,0:T(8,128)(2,1)S(1)}, bf16[24,4224]{1,0:T(8,128)(2,1)S(1)}, u32[]{:S(2)}, u32[]{:S(2)}) collective-permute-start(bf16[24,4224]{1,0:T(8,128)(2,1)S(1)} %pad_maximum_fusion.5), channel_id=1, source_target_pairs={{0,4},{1,5},{2,6},{3,7},{4,8},{5,9},{6,10},{7,11},{8,12},{9,13},{1... | collective-permute-start | bytes 608264 | tf_op jit(solution)/shard_map/ppermute | solution.py:12
  42.2 10.9 %collective-permute-start.5 = (bf16[24,4224]{1,0:T(8,128)(2,1)S(1)}, bf16[24,4224]{1,0:T(8,128)(2,1)S(1)}, u32[]{:S(2)}, u32[]{:S(2)}) collective-permute-start(bf16[24,4224]{1,0:T(8,128)(2,1)S(1)} %pad_maximum_fusion.5), channel_id=1, source_target_pairs={{0,28},{1,29},{2,30},{3,31},{4,0},{5,1},{6,2},{7,3},{8,4},{9,5},{1... | collective-permute-start | bytes 608264 | tf_op jit(solution)/shard_map/ppermute | solution.py:12
  44.1 10.6 %collective-permute-start.6 = (bf16[8,4224]{1,0:T(8,128)(2,1)S(1)}, bf16[8,4224]{1,0:T(8,128)(2,1)S(1)}, u32[]{:S(2)}, u32[]{:S(2)}) collective-permute-start(bf16[8,4224]{1,0:T(8,128)(2,1)S(1)} %collective-permute-done.1), channel_id=1, source_target_pairs={{0,26},{1,27},{2,28},{3,29},{4,30},{5,31},{6,0},{7,1},{8,2},{9,3},... | collective-permute-start | bytes 202760 | tf_op jit(solution)/shard_map/ppermute | solution.py:12
  54.7 10.3 %collective-permute-start.8 = (bf16[128,4224]{1,0:T(8,128)(2,1)S(1)}, bf16[128,4224]{1,0:T(8,128)(2,1)S(1)}, u32[]{:S(2)}, u32[]{:S(2)}) collective-permute-start(bf16[128,4224]{1,0:T(8,128)(2,1)S(1)} %constant_dynamic-update-slice_fusion), channel_id=1, source_target_pairs={{0,1},{1,0},{2,3},{3,2},{4,5},{5,4},{6,7},{7,6},{8,9},{9,8},{10,11... | collective-permute-start | bytes 3244040 | tf_op jit(solution)/shard_map/ppermute | solution.py:16
  68.9 57.5 %copy-start.1 = (bf16[1,4096,128]{2,1,0:T(8,128)(2,1)S(1)}, bf16[1,4096,128]{2,1,0:T(8,128)(2,1)}, u32[]{:S(2)}) copy-start(bf16[1,4096,128]{2,1,0:T(8,128)(2,1)} %param.10) | copy-start | bytes 3145732
  68.9 57.5 %all-to-all-start = ((bf16[8,64,4096]{2,1,0:T(8,128)(2,1)}), bf16[8,64,4096]{2,1,0:T(8,128)(2,1)}, u32[]{:S(2)}, u32[]{:S(2)}) async-start(bf16[8,64,4096]{2,1,0:T(8,128)(2,1)} %bitcast.134), calls=%async_computation | async-start | bytes 8388608 | tf_op jit(solution)/shard_map/all_to_all | solution.py:93
  75.5 62.3 %collective-permute-start.9 = (bf16[4096,128]{1,0:T(8,128)(2,1)}, bf16[4096,128]{1,0:T(8,128)(2,1)}, u32[]{:S(2)}, u32[]{:S(2)}) collective-permute-start(bf16[4096,128]{1,0:T(8,128)(2,1)} %bitcast.7), channel_id=1, source_target_pairs={{0,128},{32,160},{64,192},{96,224},{128,0},{160,32},{192,64},{224,... | collective-permute-start | bytes 3145736 | tf_op jit(solution)/shard_map/ppermute | solution.py:20
  77.5 64.4 %collective-permute-start.10 = (bf16[1024,512]{1,0:T(8,128)(2,1)}, bf16[1024,512]{1,0:T(8,128)(2,1)}, u32[]{:S(2)}, u32[]{:S(2)}) collective-permute-start(bf16[1024,512]{1,0:T(8,128)(2,1)} %bitcast.8), channel_id=1, source_target_pairs={{0,128},{32,160},{64,192},{96,224},{128,0},{160,32},{192,64},{224,... | collective-permute-start | bytes 3145736 | tf_op jit(solution)/shard_map/ppermute | solution.py:20
  175.0 21.0 %all-to-all-start.2 = ((bf16[8,64,1024]{2,1,0:T(8,128)(2,1)}), bf16[8,64,1024]{2,1,0:T(8,128)(2,1)S(1)}, u32[]{:S(2)}, u32[]{:S(2)}) async-start(bf16[8,64,1024]{2,1,0:T(8,128)(2,1)} %maximum_select_fusion), calls=%async_computation.2 | async-start | bytes 2097152 | tf_op jit(solution)/shard_map/all_to_all | solution.py:116
  196.6 5.4 %collective-permute-start.11 = (bf16[128,4096]{1,0:T(8,128)(2,1)S(1)}, bf16[128,4096]{1,0:T(8,128)(2,1)S(1)}, u32[]{:S(2)}, u32[]{:S(2)}) collective-permute-start(bf16[128,4096]{1,0:T(8,128)(2,1)S(1)} %convolution_convert_fusion), channel_id=1, source_target_pairs={{0,1},{1,0},{2,3},{3,2},{4,5},{5,4},{6,7},{7,6},{8,9},{9,8},{10,11... | collective-permute-start | bytes 3145736 | tf_op jit(solution)/shard_map/ppermute | solution.py:16
  202.5 41.6 %copy-start = (bf16[8,4096]{1,0:T(8,128)(2,1)S(1)}, bf16[8,4096]{1,0:T(8,128)(2,1)}, u32[]{:S(2)}) copy-start(bf16[8,4096]{1,0:T(8,128)(2,1)} %param.7) | copy-start | bytes 196612
  202.5 41.7 %copy-start.2 = (f32[4096]{0:T(1024)S(1)}, f32[4096]{0:T(1024)}, u32[]{:S(2)}) copy-start(f32[4096]{0:T(1024)} %param.13) | copy-start | bytes 49156
  202.6 16.2 %collective-permute-start.15 = (bf16[24,4096]{1,0:T(8,128)(2,1)S(1)}, bf16[24,4096]{1,0:T(8,128)(2,1)S(1)}, u32[]{:S(2)}, u32[]{:S(2)}) collective-permute-start(bf16[24,4096]{1,0:T(8,128)(2,1)S(1)} %get-tuple-element.16), channel_id=1, source_target_pairs={{0,2},{1,3},{2,4},{3,5},{4,6},{5,7},{6,8},{7,9},{8,10},{9,11},{10,... | collective-permute-start | bytes 589832 | tf_op jit(solution)/shard_map/ppermute | solution.py:12
  207.5 11.3 %collective-permute-start.14 = (bf16[24,4096]{1,0:T(8,128)(2,1)S(1)}, bf16[24,4096]{1,0:T(8,128)(2,1)S(1)}, u32[]{:S(2)}, u32[]{:S(2)}) collective-permute-start(bf16[24,4096]{1,0:T(8,128)(2,1)S(1)} %get-tuple-element.17), channel_id=1, source_target_pairs={{0,30},{1,31},{2,0},{3,1},{4,2},{5,3},{6,4},{7,5},{8,6},{9,7},{10,... | collective-permute-start | bytes 589832 | tf_op jit(solution)/shard_map/ppermute | solution.py:12
  209.4 15.1 %collective-permute-start.13 = (bf16[24,4096]{1,0:T(8,128)(2,1)S(1)}, bf16[24,4096]{1,0:T(8,128)(2,1)S(1)}, u32[]{:S(2)}, u32[]{:S(2)}) collective-permute-start(bf16[24,4096]{1,0:T(8,128)(2,1)S(1)} %get-tuple-element.18), channel_id=1, source_target_pairs={{0,4},{1,5},{2,6},{3,7},{4,8},{5,9},{6,10},{7,11},{8,12},{9,13},{1... | collective-permute-start | bytes 589832 | tf_op jit(solution)/shard_map/ppermute | solution.py:12
  212.5 13.9 %collective-permute-start.12 = (bf16[24,4096]{1,0:T(8,128)(2,1)S(1)}, bf16[24,4096]{1,0:T(8,128)(2,1)S(1)}, u32[]{:S(2)}, u32[]{:S(2)}) collective-permute-start(bf16[24,4096]{1,0:T(8,128)(2,1)S(1)} %get-tuple-element.15), channel_id=1, source_target_pairs={{0,28},{1,29},{2,30},{3,31},{4,0},{5,1},{6,2},{7,3},{8,4},{9,5},{1... | collective-permute-start | bytes 589832 | tf_op jit(solution)/shard_map/ppermute | solution.py:12
  216.8 9.7 %collective-permute-start.17 = (bf16[8,4096]{1,0:T(8,128)(2,1)S(1)}, bf16[8,4096]{1,0:T(8,128)(2,1)S(1)}, u32[]{:S(2)}, u32[]{:S(2)}) collective-permute-start(bf16[8,4096]{1,0:T(8,128)(2,1)S(1)} %slice.229), channel_id=1, source_target_pairs={{0,6},{1,7},{2,8},{3,9},{4,10},{5,11},{6,12},{7,13},{8,14},{9,15},... | collective-permute-start | bytes 196616 | tf_op jit(solution)/shard_map/ppermute | solution.py:12
  226.6 15.5 %collective-permute-start.18 = (bf16[8,4096]{1,0:T(8,128)(2,1)S(1)}, bf16[8,4096]{1,0:T(8,128)(2,1)S(1)}, u32[]{:S(2)}, u32[]{:S(2)}) collective-permute-start(bf16[8,4096]{1,0:T(8,128)(2,1)S(1)} %fusion.9), channel_id=1, source_target_pairs={{0,10},{1,11},{2,12},{3,13},{4,14},{5,15},{6,16},{7,17},{8,18},{9,... | collective-permute-start | bytes 196616 | tf_op jit(solution)/shard_map/ppermute | solution.py:12
  233.0 11.1 %collective-permute-start.16 = (bf16[8,4096]{1,0:T(8,128)(2,1)S(1)}, bf16[8,4096]{1,0:T(8,128)(2,1)S(1)}, u32[]{:S(2)}, u32[]{:S(2)}) collective-permute-start(bf16[8,4096]{1,0:T(8,128)(2,1)S(1)} %slice.354), channel_id=1, source_target_pairs={{0,22},{1,23},{2,24},{3,25},{4,26},{5,27},{6,28},{7,29},{8,30},{9,... | collective-permute-start | bytes 196616 | tf_op jit(solution)/shard_map/ppermute | solution.py:12

commit v2 on v1

--- a/solution.py
+++ b/solution.py
@@ -1,6 +1,8 @@
 import jax
 import jax.numpy as jnp
 from jax import lax
+from jax.experimental import pallas as pl
+from jax.experimental.pallas import tpu as pltpu
 from jax.sharding import PartitionSpec as P
 
 BF16 = jnp.bfloat16
@@ -27,25 +29,134 @@
 def gather_column(block):
     n = block.shape[0]
     three = jnp.concatenate([block, around(block, 5), around(block, -5)], 0)
-    below2, above2 = around(three, 2), around(three, -2)
+    below1, above1 = around(three, 1), around(three, -1)
     eighth = around(three[2 * n:], -3)
-    below1, above1 = around(three, 1), around(three, -1)
-    column = jnp.concatenate([three, below1, above1, below2, above2, eighth], 0)
-    return column
+    below2, above2 = around(below1, 1), around(above1, -1)
+    return jnp.concatenate([three, below1, above1, below2, above2, eighth], 0)
 
 
 def scatter_group(column, n):
-    sent = column[3 * n:].astype(BF16)
-    below1, above1, below2, above2 = (sent[3 * n * i:3 * n * (i + 1)] for i in range(4))
-    from_above2, from_below2 = around(below2, -2), around(above2, 2)
-    eighth = around(sent[12 * n:], 3)
-    from_above1, from_below1 = around(below1, -1), around(above1, 1)
-    part = column[:3 * n]
-    for other in (from_above2, from_below2, from_above1, from_below1):
-        part = part + other.astype(F32)
+    below1, above1, below2, above2 = (column[3 * n * i:3 * n * (i + 1)] for i in range(1, 5))
+    below1 = below1 + around(below2.astype(BF16), -1).astype(F32)
+    above1 = above1 + around(above2.astype(BF16), 1).astype(F32)
+    eighth = around(column[15 * n:].astype(BF16), 3).astype(F32)
+    part = column[:3 * n] + around(below1.astype(BF16), -1).astype(F32) + around(above1.astype(BF16), 1).astype(F32)
     below = around(part[n:2 * n].astype(BF16), -5)
-    above = around((part[2 * n:] + eighth.astype(F32)).astype(BF16), 5)
+    above = around((part[2 * n:] + eighth).astype(BF16), 5)
     return part[:n] + below.astype(F32) + above.astype(F32)
+
+
+def whole(shape):
+    return pl.BlockSpec(shape, lambda k: (0,) * len(shape))
+
+
+def pick_rows(onehot, near, other, width):
+    picked, half = onehot.shape[0], near.shape[0]
+    slots, block = picked // 2, 512
+
+    def kernel(onehot_ref, near_ref, other_ref, out_ref):
+        rows = jnp.dot(onehot_ref[:, :half], near_ref[...], preferred_element_type=F32)
+        rows = rows + jnp.dot(onehot_ref[:, half:], other_ref[...], preferred_element_type=F32)
+        rows = rows.astype(BF16)
+        for at in range(8):
+            start = at // 4 * slots
+            out_ref[at] = rows[start:start + slots]
+
+    return pl.pallas_call(
+        kernel,
+        grid=(width // block,),
+        in_specs=[
+            whole(onehot.shape),
+            pl.BlockSpec((half, block), lambda k: (0, k)),
+            pl.BlockSpec((half, block), lambda k: (0, k)),
+        ],
+        out_specs=pl.BlockSpec((8, slots, block), lambda k: (0, 0, k)),
+        out_shape=jax.ShapeDtypeStruct((8, slots, width), BF16),
+        name="pick_rows",
+    )(onehot, near, other)
+
+
+def front(odd, rows, gates, ups):
+    count, width = rows.shape
+    units, block = gates[0].shape[1], 512
+    steps = width // block
+
+    def kernel(odd_ref, rows_ref, gate_own, gate_other, up_own, up_other, out_ref, total):
+        k = pl.program_id(0)
+
+        @pl.when(k == 0)
+        def _():
+            total[...] = jnp.zeros_like(total)
+
+        weights = jnp.concatenate([gate_own[...], gate_other[...], up_own[...], up_other[...]], 1)
+        total[...] += jnp.dot(rows_ref[...], weights, preferred_element_type=F32)
+
+        @pl.when(k == steps - 1)
+        def _():
+            gate, up = total[:, :2 * units], total[:, 2 * units:]
+            hidden = gate / (1.0 + jnp.exp(-gate)) * up
+            low, high = hidden[:, :units], hidden[:, units:]
+            swap = odd_ref[0] == 1
+            first, second = jnp.where(swap, high, low).astype(BF16), jnp.where(swap, low, high).astype(BF16)
+            for at in range(4):
+                out_ref[at, :, :units] = first
+                out_ref[at, :, units:] = second
+
+    weight = pl.BlockSpec((block, units), lambda k: (k, 0))
+    return pl.pallas_call(
+        kernel,
+        grid=(steps,),
+        in_specs=[
+            pl.BlockSpec(memory_space=pltpu.SMEM),
+            pl.BlockSpec((count, block), lambda k: (0, k)),
+            weight, weight, weight, weight,
+        ],
+        out_specs=whole((4, count, 2 * units)),
+        out_shape=jax.ShapeDtypeStruct((4, count, 2 * units), BF16),
+        scratch_shapes=[pltpu.VMEM((count, 4 * units), F32)],
+        name="front",
+    )(odd, rows, *gates, *ups)
+
+
+def back(odd, hidden, own, other, slots):
+    parts, count, units = hidden.shape
+    features = own.shape[1]
+    half = units // 2
+    own, other = (w.reshape(2, own.shape[0] // 2, features) for w in (own, other))
+
+    def kernel(odd_ref, hidden_ref, own_ref, other_ref, out_ref, total):
+        k = pl.program_id(0)
+
+        @pl.when(k == 0)
+        def _():
+            total[...] = jnp.zeros_like(total)
+
+        weights = [jnp.concatenate([w[0], w[1]], 0) for w in (own_ref, other_ref)]
+        total[...] += jnp.dot(hidden_ref[0], jnp.concatenate(weights, 1), preferred_element_type=F32)
+
+        @pl.when(k == parts - 1)
+        def _():
+            low, high = total[:, :features], total[:, features:]
+            swap = odd_ref[0] == 1
+            shape = (count // slots, slots, features)
+            out_ref[:, :, :features] = jnp.where(swap, high, low).astype(BF16).reshape(shape)
+            out_ref[:, :, features:] = jnp.where(swap, low, high).astype(BF16).reshape(shape)
+
+    weight = pl.BlockSpec((2, half, features), lambda k: (0, k, 0))
+    out = (count // slots, slots, 2 * features)
+    return pl.pallas_call(
+        kernel,
+        grid=(parts,),
+        in_specs=[
+            pl.BlockSpec(memory_space=pltpu.SMEM),
+            pl.BlockSpec((1, count, units), lambda k: (k, 0, 0)),
+            weight, weight,
+        ],
+        out_specs=whole(out),
+        out_shape=jax.ShapeDtypeStruct(out, BF16),
+        scratch_shapes=[pltpu.VMEM((count, 2 * features), F32)],
+        name="back",
+    )(odd, hidden, own, other)
 
 
 def shards(tokens, expert_ids, gate_weights, w_gate, w_up, w_down, norm_gain):
@@ -53,7 +164,7 @@
     top = expert_ids.shape[1]
     g = lax.axis_index("grp")
     p = lax.axis_index("ep")
-    odd_row = g // 4 % 2 == 1
+    odd = (g // 4 % 2).astype(jnp.int32).reshape(1)
 
     gate_own, up_own, down_own = w_gate[0], w_up[0], w_down[0]
     gate_other, up_other, down_other = pair_swap(gate_own), pair_swap(up_own), pair_swap(down_own)
@@ -63,7 +174,7 @@
     extra = jnp.concatenate([expert_ids.astype(F32), high, low], 1).astype(BF16)
     extra = jnp.pad(extra, ((0, 0), (0, 128 - 3 * top)))
     column = gather_column(jnp.concatenate([tokens, extra], 1))
-    column, gate_other = lax.optimization_barrier((column, gate_other))
+    column, gate_other, up_other = lax.optimization_barrier((column, gate_other, up_other))
     parts = column, core_swap(column)
     half = parts[0].shape[0]
     rows = 2 * half
@@ -85,34 +196,17 @@
     picks = place[:, None, :] == jnp.arange(slots, dtype=F32)[None, :, None]
     picks = picks.reshape(2 * slots, rows)
     onehot = picks.astype(BF16)
-    chosen = jnp.dot(onehot[:, :half], parts[0][:, :width], preferred_element_type=F32)
-    chosen = chosen + jnp.dot(onehot[:, half:], parts[1][:, :width], preferred_element_type=F32)
-    chosen = chosen.astype(BF16)
-
-    fanned = jnp.broadcast_to(chosen.reshape(2, 1, slots, width), (2, 4, slots, width)).reshape(8, slots, width)
+    fanned = pick_rows(onehot, parts[0], parts[1], width)
+
     arrived = lax.all_to_all(fanned, "grp", split_axis=0, concat_axis=0, tiled=True, axis_index_groups=EIGHTS)
     arrived = arrived.reshape(8 * slots, width)
 
-    def front(gate, up):
-        a = jnp.dot(arrived, gate, preferred_element_type=F32)
-        b = jnp.dot(arrived, up, preferred_element_type=F32)
-        return (jax.nn.silu(a) * b).astype(BF16)
-
-    mine, theirs = front(gate_own, up_own), front(gate_other, up_other)
-    hidden = jnp.where(odd_row, jnp.concatenate([theirs, mine], 1), jnp.concatenate([mine, theirs], 1))
+    hidden = front(odd, arrived, (gate_own, gate_other), (up_own, up_other))
     hidden, down_other = lax.optimization_barrier((hidden, down_other))
-    units = mine.shape[1]
-    hidden = jnp.broadcast_to(hidden[None], (4,) + hidden.shape)
     hidden = lax.all_to_all(hidden, "grp", split_axis=0, concat_axis=0, tiled=True, axis_index_groups=FOURS)
-    hidden = jnp.concatenate(
-        [hidden[x, :, units * at:units * (at + 1)] for at in range(2) for x in range(4)], 1
-    )
-
-    out_own = jnp.dot(hidden, down_own, preferred_element_type=F32).astype(BF16)
-    out_other = jnp.dot(hidden, down_other, preferred_element_type=F32).astype(BF16)
-    out = jnp.where(odd_row, jnp.concatenate([out_other, out_own], 1), jnp.concatenate([out_own, out_other], 1))
-    features = out_own.shape[1]
-    out = out.reshape(8, slots, 2 * features)
+
+    features = down_own.shape[1]
+    out = back(odd, hidden, down_own, down_other, slots)
     home = lax.all_to_all(out, "grp", split_axis=0, concat_axis=0, tiled=True, axis_index_groups=EIGHTS)
     home = jnp.concatenate(
         [

time: 246 us -> 258 us (1.049)
  the two profiles are of different devices: /device:TPU:1 before, /device:TPU:96 now
where the time goes in v2:
time: 258 us; the launch traced here: 256 us
  waiting for transfers between devices  119 us (46%)
  starting transfers between devices  79.6 us (31%)
  blocking collectives  29.7 us (12%)
  Pallas kernels  20.6 us (8%)
  other arithmetic  5.24 us (2%)
    ppermute x14, starting transfers between devices, around(): lax.ppermute(block, 'ep', [(i, (i + 2 * chips) % size) for i in range(siz...  56.4 us
    all_to_all x1, waiting for transfers between devices, shards(): lax.all_to_all(fanned, 'grp', split_axis=0, concat_axis=0, tiled=True, ax...  48.9 us
    ppermute x14, waiting for transfers between devices, around(): lax.ppermute(block, 'ep', [(i, (i + 2 * chips) % size) for i in range(siz...  39.1 us
    all_to_all x1, blocking collectives, shards(): lax.all_to_all(hidden, 'grp', split_axis=0, concat_axis=0, tiled=True, ax...  29.7 us
    all_to_all x1, waiting for transfers between devices, shards(): lax.all_to_all(out, 'grp', split_axis=0, concat_axis=0, tiled=True, axis_...  14.7 us
    ppermute x3, waiting for transfers between devices, pair_swap(): lax.ppermute(block, 'grp', [(i, i ^ 4) for i in range(lax.axis_size('grp'...  11.2 us
    pallas_call x1, Pallas kernels, front(): pl.pallas_call(kernel, grid=(steps,), in_specs=[pl.BlockSpec(memory_space...  8.66 us
    ppermute x3, starting transfers between devices, pair_swap(): lax.ppermute(block, 'grp', [(i, i ^ 4) for i in range(lax.axis_size('grp'...  7.89 us
  transfers between devices with their start and end apart: 21, of which 15 were waited for; matrix products, arithmetic and copies ran while one was open for 1% of the time, Pallas kernels for 3%

profile of v2, /device:TPU:96, one launch (start us, length us, event | category | flops | bytes accessed | tf_op | source)
XLA Modules:
  0.0 256.3 jit_solution(12274276745622701425)
XLA Ops:
  2.3 11.7 %collective-permute-start = (bf16[8,4224]{1,0:T(8,128)(2,1)S(1)}, bf16[8,4224]{1,0:T(8,128)(2,1)S(1)}, u32[]{:S(2)}, u32[]{:S(2)}) collective-permute-start(bf16[8,4224]{1,0:T(8,128)(2,1)S(1)} %get-tuple-element.37), channel_id=1, source_target_pairs={{0,10},{1,11},{2,12},{3,13},{4,14},{5,15},{6,16},{7,17},{8,18},{9,... | collective-permute-start | bytes 202760 | tf_op jit(solution)/shard_map/ppermute | solution.py:14
  15.9 3.5 %collective-permute-start.7 = (bf16[4096,128]{1,0:T(8,128)(2,1)}, bf16[4096,128]{1,0:T(8,128)(2,1)S(1)}, u32[]{:S(2)}, u32[]{:S(2)}) collective-permute-start(bf16[4096,128]{1,0:T(8,128)(2,1)} %bitcast.88), channel_id=1, source_target_pairs={{0,128},{32,160},{64,192},{96,224},{128,0},{160,32},{192,64},{224,... | collective-permute-start | bytes 3145736 | tf_op jit(solution)/shard_map/ppermute | solution.py:22
  21.8 8.3 %collective-permute-done.1 = bf16[8,4224]{1,0:T(8,128)(2,1)S(1)} collective-permute-done((bf16[8,4224]{1,0:T(8,128)(2,1)S(1)}, bf16[8,4224]{1,0:T(8,128)(2,1)S(1)}, u32[]{:S(2)}, u32[]{:S(2)}) %collective-permute-start.1) | collective-permute-done | bytes 67616 | tf_op jit(solution)/shard_map/ppermute | solution.py:14
  33.0 3.8 %collective-permute-start.3 = (bf16[24,4224]{1,0:T(8,128)(2,1)S(1)}, bf16[24,4224]{1,0:T(8,128)(2,1)S(1)}, u32[]{:S(2)}, u32[]{:S(2)}) collective-permute-start(bf16[24,4224]{1,0:T(8,128)(2,1)S(1)} %pad_maximum_fusion.5), channel_id=1, source_target_pairs={{0,30},{1,31},{2,0},{3,1},{4,2},{5,3},{6,4},{7,5},{8,6},{9,7},{10,... | collective-permute-start | bytes 608264 | tf_op jit(solution)/shard_map/ppermute | solution.py:14
  39.6 3.4 %collective-permute-start.4 = (bf16[24,4224]{1,0:T(8,128)(2,1)S(1)}, bf16[24,4224]{1,0:T(8,128)(2,1)S(1)}, u32[]{:S(2)}, u32[]{:S(2)}) collective-permute-start(bf16[24,4224]{1,0:T(8,128)(2,1)S(1)} %collective-permute-done.2), channel_id=1, source_target_pairs={{0,2},{1,3},{2,4},{3,5},{4,6},{5,7},{6,8},{7,9},{8,10},{9,11},{10,... | collective-permute-start | bytes 608264 | tf_op jit(solution)/shard_map/ppermute | solution.py:14
  47.4 6.5 %collective-permute-done.5 = bf16[24,4224]{1,0:T(8,128)(2,1)S(1)} collective-permute-done((bf16[24,4224]{1,0:T(8,128)(2,1)S(1)}, bf16[24,4224]{1,0:T(8,128)(2,1)S(1)}, u32[]{:S(2)}, u32[]{:S(2)}) %collective-permute-start.5) | collective-permute-done | bytes 202784 | tf_op jit(solution)/shard_map/ppermute | solution.py:14
  54.0 11.2 %collective-permute-done.8.up_other = bf16[4096,128]{1,0:T(8,128)(2,1)} collective-permute-done((bf16[4096,128]{1,0:T(8,128)(2,1)}, bf16[4096,128]{1,0:T(8,128)(2,1)}, u32[]{:S(2)}, u32[]{:S(2)}) %collective-permute-start.8) | collective-permute-done | bytes 1048608 | tf_op jit(solution)/shard_map/ppermute | solution.py:22
  70.9 7.1 %pick_rows.1 = bf16[8,64,4096]{2,1,0:T(8,128)(2,1)} custom-call(bf16[128,256]{1,0:T(8,128)(2,1)} %fusion.9.onehot_ref, bf16[128,4224]{1,0:T(8,128)(2,1)} %copy-done, bf16[128,4224]{1,0:T(8,128)(2,1)} %copy-done.1), custom_call_target="tpu_custom_call" | custom-call | tf_op jit(solution)/shard_map/pick_rows/pallas_call | solution.py:65
  78.0 6.9 %all-to-all-start = ((bf16[8,64,4096]{2,1,0:T(8,128)(2,1)}), bf16[8,64,4096]{2,1,0:T(8,128)(2,1)}, u32[]{:S(2)}, u32[]{:S(2)}) async-start(bf16[8,64,4096]{2,1,0:T(8,128)(2,1)} %pick_rows.1), calls=%async_computation | async-start | bytes 8388608 | tf_op jit(solution)/shard_map/all_to_all | solution.py:201
  87.0 48.9 %all-to-all-done = bf16[8,64,4096]{2,1,0:T(8,128)(2,1)} async-done(((bf16[8,64,4096]{2,1,0:T(8,128)(2,1)}), bf16[8,64,4096]{2,1,0:T(8,128)(2,1)}, u32[]{:S(2)}, u32[]{:S(2)}) %all-to-all-start) | async-done | bytes 4194336 | tf_op jit(solution)/shard_map/all_to_all | solution.py:201
  135.9 8.7 %front.1 = bf16[4,512,256]{2,1,0:T(8,128)(2,1)} custom-call(s32[1]{0:T(128)} %bitcast.5.odd_ref, bf16[512,4096]{1,0:T(8,128)(2,1)} %bitcast.6.rows_ref, bf16[4096,128]{1,0:T(8,128)(2,1)} %bitcast.89, bf16[4096,128]{1,0:T(8,128)(2,1)} %copy-done.3, bf16[4096,128]{1,0:T(8,128)(2,1)} %bitcast.91, bf16[4096,128]{1,0:T(8,128)(2,1)} %collective-permute-done.8.up_other), custom_call_target="tpu_custom_call" | custom-call | tf_op jit(solution)/shard_map/front/pallas_call | solution.py:106
  144.6 29.7 %all_to_all.15.hidden_ref = bf16[4,512,256]{2,1,0:T(8,128)(2,1)} all-to-all(bf16[4,512,256]{2,1,0:T(8,128)(2,1)} %front.1), channel_id=1, replica_groups={{0,32,64,96},{128,160,192,224},{256,288,320,352},{384,416,448,480},{1,3..., dimensions={0} | all-to-all | bytes 2097152 | tf_op jit(solution)/shard_map/all_to_all | solution.py:206
  174.2 4.9 %back.1 = bf16[8,64,1024]{2,1,0:T(8,128)(2,1)} custom-call(s32[1]{0:T(128)} %bitcast.5.odd_ref, bf16[4,512,256]{2,1,0:T(8,128)(2,1)} %all_to_all.15.hidden_ref, bf16[2,512,512]{2,1,0:T(8,128)(2,1)} %bitcast.92, bf16[2,512,512]{2,1,0:T(8,128)(2,1)} %bitcast.94), custom_call_target="tpu_custom_call" | custom-call | tf_op jit(solution)/shard_map/back/pallas_call | solution.py:147
  179.2 4.6 %all-to-all-start.2 = ((bf16[8,64,1024]{2,1,0:T(8,128)(2,1)}), bf16[8,64,1024]{2,1,0:T(8,128)(2,1)S(1)}, u32[]{:S(2)}, u32[]{:S(2)}) async-start(bf16[8,64,1024]{2,1,0:T(8,128)(2,1)} %back.1), calls=%async_computation.2 | async-start | bytes 2097152 | tf_op jit(solution)/shard_map/all_to_all | solution.py:210
  183.9 14.7 %all-to-all-done.2 = bf16[8,64,1024]{2,1,0:T(8,128)(2,1)S(1)} async-done(((bf16[8,64,1024]{2,1,0:T(8,128)(2,1)}), bf16[8,64,1024]{2,1,0:T(8,128)(2,1)S(1)}, u32[]{:S(2)}, u32[]{:S(2)}) %all-to-all-start.2) | async-done | bytes 1048608 | tf_op jit(solution)/shard_map/all_to_all | solution.py:210
  206.2 5.1 %collective-permute-start.14 = (bf16[24,4096]{1,0:T(8,128)(2,1)S(1)}, bf16[24,4096]{1,0:T(8,128)(2,1)S(1)}, u32[]{:S(2)}, u32[]{:S(2)}) collective-permute-start(bf16[24,4096]{1,0:T(8,128)(2,1)S(1)} %get-tuple-element.20), channel_id=1, source_target_pairs={{0,2},{1,3},{2,4},{3,5},{4,6},{5,7},{6,8},{7,9},{8,10},{9,11},{10,... | collective-permute-start | bytes 589832 | tf_op jit(solution)/shard_map/ppermute | solution.py:14
  211.4 3.0 %collective-permute-done.12 = bf16[24,4096]{1,0:T(8,128)(2,1)S(1)} collective-permute-done((bf16[24,4096]{1,0:T(8,128)(2,1)S(1)}, bf16[24,4096]{1,0:T(8,128)(2,1)S(1)}, u32[]{:S(2)}, u32[]{:S(2)}) %collective-permute-start.12) | collective-permute-done | bytes 196640 | tf_op jit(solution)/shard_map/ppermute | solution.py:14
  215.6 5.6 %collective-permute-start.15 = (bf16[24,4096]{1,0:T(8,128)(2,1)S(1)}, bf16[24,4096]{1,0:T(8,128)(2,1)S(1)}, u32[]{:S(2)}, u32[]{:S(2)}) collective-permute-start(bf16[24,4096]{1,0:T(8,128)(2,1)S(1)} %get-tuple-element.18), channel_id=1, source_target_pairs={{0,2},{1,3},{2,4},{3,5},{4,6},{5,7},{6,8},{7,9},{8,10},{9,11},{10,... | collective-permute-start | bytes 589832 | tf_op jit(solution)/shard_map/ppermute | solution.py:14
  223.2 4.2 %collective-permute-start.17 = (bf16[8,4096]{1,0:T(8,128)(2,1)S(1)}, bf16[8,4096]{1,0:T(8,128)(2,1)S(1)}, u32[]{:S(2)}, u32[]{:S(2)}) collective-permute-start(bf16[8,4096]{1,0:T(8,128)(2,1)S(1)} %slice.166), channel_id=1, source_target_pairs={{0,6},{1,7},{2,8},{3,9},{4,10},{5,11},{6,12},{7,13},{8,14},{9,15},... | collective-permute-start | bytes 196616 | tf_op jit(solution)/shard_map/ppermute | solution.py:14
  227.3 2.7 %collective-permute-done.13 = bf16[24,4096]{1,0:T(8,128)(2,1)S(1)} collective-permute-done((bf16[24,4096]{1,0:T(8,128)(2,1)S(1)}, bf16[24,4096]{1,0:T(8,128)(2,1)S(1)}, u32[]{:S(2)}, u32[]{:S(2)}) %collective-permute-start.13) | collective-permute-done | bytes 196640 | tf_op jit(solution)/shard_map/ppermute | solution.py:14
  230.1 3.5 %collective-permute-done.17 = bf16[8,4096]{1,0:T(8,128)(2,1)S(1)} collective-permute-done((bf16[8,4096]{1,0:T(8,128)(2,1)S(1)}, bf16[8,4096]{1,0:T(8,128)(2,1)S(1)}, u32[]{:S(2)}, u32[]{:S(2)}) %collective-permute-start.17) | collective-permute-done | bytes 65568 | tf_op jit(solution)/shard_map/ppermute | solution.py:14
  233.6 8.7 %collective-permute-start.18 = (bf16[8,4096]{1,0:T(8,128)(2,1)S(1)}, bf16[8,4096]{1,0:T(8,128)(2,1)S(1)}, u32[]{:S(2)}, u32[]{:S(2)}) collective-permute-start(bf16[8,4096]{1,0:T(8,128)(2,1)S(1)} %fusion.4), channel_id=1, source_target_pairs={{0,10},{1,11},{2,12},{3,13},{4,14},{5,15},{6,16},{7,17},{8,18},{9,... | collective-permute-start | bytes 196616 | tf_op jit(solution)/shard_map/ppermute | solution.py:14
  244.2 3.1 %collective-permute-done.18 = bf16[8,4096]{1,0:T(8,128)(2,1)S(1)} collective-permute-done((bf16[8,4096]{1,0:T(8,128)(2,1)S(1)}, bf16[8,4096]{1,0:T(8,128)(2,1)S(1)}, u32[]{:S(2)}, u32[]{:S(2)}) %collective-permute-start.18) | collective-permute-done | bytes 65568 | tf_op jit(solution)/shard_map/ppermute | solution.py:14
  247.4 8.0 %collective-permute-done.16 = bf16[8,4096]{1,0:T(8,128)(2,1)S(1)} collective-permute-done((bf16[8,4096]{1,0:T(8,128)(2,1)S(1)}, bf16[8,4096]{1,0:T(8,128)(2,1)S(1)}, u32[]{:S(2)}, u32[]{:S(2)}) %collective-permute-start.16) | collective-permute-done | bytes 65568 | tf_op jit(solution)/shard_map/ppermute | solution.py:14
  (78 shorter events, 38.3 us)
Async XLA Ops:
  2.3 19.5 %collective-permute-start = (bf16[8,4224]{1,0:T(8,128)(2,1)S(1)}, bf16[8,4224]{1,0:T(8,128)(2,1)S(1)}, u32[]{:S(2)}, u32[]{:S(2)}) collective-permute-start(bf16[8,4224]{1,0:T(8,128)(2,1)S(1)} %get-tuple-element.37), channel_id=1, source_target_pairs={{0,10},{1,11},{2,12},{3,13},{4,14},{5,15},{6,16},{7,17},{8,18},{9,... | collective-permute-start | bytes 202760 | tf_op jit(solution)/shard_map/ppermute | solution.py:14
  14.0 16.1 %collective-permute-start.1 = (bf16[8,4224]{1,0:T(8,128)(2,1)S(1)}, bf16[8,4224]{1,0:T(8,128)(2,1)S(1)}, u32[]{:S(2)}, u32[]{:S(2)}) collective-permute-start(bf16[8,4224]{1,0:T(8,128)(2,1)S(1)} %get-tuple-element.37), channel_id=1, source_target_pairs={{0,22},{1,23},{2,24},{3,25},{4,26},{5,27},{6,28},{7,29},{8,30},{9,... | collective-permute-start | bytes 202760 | tf_op jit(solution)/shard_map/ppermute | solution.py:14
  15.9 38.1 %collective-permute-start.7 = (bf16[4096,128]{1,0:T(8,128)(2,1)}, bf16[4096,128]{1,0:T(8,128)(2,1)S(1)}, u32[]{:S(2)}, u32[]{:S(2)}) collective-permute-start(bf16[4096,128]{1,0:T(8,128)(2,1)} %bitcast.88), channel_id=1, source_target_pairs={{0,128},{32,160},{64,192},{96,224},{128,0},{160,32},{192,64},{224,... | collective-permute-start | bytes 3145736 | tf_op jit(solution)/shard_map/ppermute | solution.py:22
  19.4 45.8 %collective-permute-start.8 = (bf16[4096,128]{1,0:T(8,128)(2,1)}, bf16[4096,128]{1,0:T(8,128)(2,1)}, u32[]{:S(2)}, u32[]{:S(2)}) collective-permute-start(bf16[4096,128]{1,0:T(8,128)(2,1)} %bitcast.90), channel_id=1, source_target_pairs={{0,128},{32,160},{64,192},{96,224},{128,0},{160,32},{192,64},{224,... | collective-permute-start | bytes 3145736 | tf_op jit(solution)/shard_map/ppermute | solution.py:22
  31.0 8.7 %collective-permute-start.2 = (bf16[24,4224]{1,0:T(8,128)(2,1)S(1)}, bf16[24,4224]{1,0:T(8,128)(2,1)S(1)}, u32[]{:S(2)}, u32[]{:S(2)}) collective-permute-start(bf16[24,4224]{1,0:T(8,128)(2,1)S(1)} %pad_maximum_fusion.5), channel_id=1, source_target_pairs={{0,2},{1,3},{2,4},{3,5},{4,6},{5,7},{6,8},{7,9},{8,10},{9,11},{10,... | collective-permute-start | bytes 608264 | tf_op jit(solution)/shard_map/ppermute | solution.py:14
  33.0 12.1 %collective-permute-start.3 = (bf16[24,4224]{1,0:T(8,128)(2,1)S(1)}, bf16[24,4224]{1,0:T(8,128)(2,1)S(1)}, u32[]{:S(2)}, u32[]{:S(2)}) collective-permute-start(bf16[24,4224]{1,0:T(8,128)(2,1)S(1)} %pad_maximum_fusion.5), channel_id=1, source_target_pairs={{0,30},{1,31},{2,0},{3,1},{4,2},{5,3},{6,4},{7,5},{8,6},{9,7},{10,... | collective-permute-start | bytes 608264 | tf_op jit(solution)/shard_map/ppermute | solution.py:14
  36.8 17.1 %collective-permute-start.6 = (bf16[8,4224]{1,0:T(8,128)(2,1)S(1)}, bf16[8,4224]{1,0:T(8,128)(2,1)S(1)}, u32[]{:S(2)}, u32[]{:S(2)}) collective-permute-start(bf16[8,4224]{1,0:T(8,128)(2,1)S(1)} %collective-permute-done.1), channel_id=1, source_target_pairs={{0,26},{1,27},{2,28},{3,29},{4,30},{5,31},{6,0},{7,1},{8,2},{9,3},... | collective-permute-start | bytes 202760 | tf_op jit(solution)/shard_map/ppermute | solution.py:14
  39.6 7.8 %collective-permute-start.4 = (bf16[24,4224]{1,0:T(8,128)(2,1)S(1)}, bf16[24,4224]{1,0:T(8,128)(2,1)S(1)}, u32[]{:S(2)}, u32[]{:S(2)}) collective-permute-start(bf16[24,4224]{1,0:T(8,128)(2,1)S(1)} %collective-permute-done.2), channel_id=1, source_target_pairs={{0,2},{1,3},{2,4},{3,5},{4,6},{5,7},{6,8},{7,9},{8,10},{9,11},{10,... | collective-permute-start | bytes 608264 | tf_op jit(solution)/shard_map/ppermute | solution.py:14
  45.1 8.8 %collective-permute-start.5 = (bf16[24,4224]{1,0:T(8,128)(2,1)S(1)}, bf16[24,4224]{1,0:T(8,128)(2,1)S(1)}, u32[]{:S(2)}, u32[]{:S(2)}) collective-permute-start(bf16[24,4224]{1,0:T(8,128)(2,1)S(1)} %collective-permute-done.3), channel_id=1, source_target_pairs={{0,30},{1,31},{2,0},{3,1},{4,2},{5,3},{6,4},{7,5},{8,6},{9,7},{10,... | collective-permute-start | bytes 608264 | tf_op jit(solution)/shard_map/ppermute | solution.py:14
  65.2 4.6 %collective-permute-start.9 = (bf16[128,4224]{1,0:T(8,128)(2,1)S(1)}, bf16[128,4224]{1,0:T(8,128)(2,1)S(1)}, u32[]{:S(2)}, u32[]{:S(2)}) collective-permute-start(bf16[128,4224]{1,0:T(8,128)(2,1)S(1)} %constant_dynamic-update-slice_fusion.near_ref), channel_id=1, source_target_pairs={{0,1},{1,0},{2,3},{3,2},{4,5},{5,4},{6,7},{7,6},{8,9},{9,8},{10,11... | collective-permute-start | bytes 3244040 | tf_op jit(solution)/shard_map/ppermute | solution.py:18
  78.0 57.9 %all-to-all-start = ((bf16[8,64,4096]{2,1,0:T(8,128)(2,1)}), bf16[8,64,4096]{2,1,0:T(8,128)(2,1)}, u32[]{:S(2)}, u32[]{:S(2)}) async-start(bf16[8,64,4096]{2,1,0:T(8,128)(2,1)} %pick_rows.1), calls=%async_computation | async-start | bytes 8388608 | tf_op jit(solution)/shard_map/all_to_all | solution.py:201
  84.9 59.7 %collective-permute-start.10 = (bf16[1024,512]{1,0:T(8,128)(2,1)S(1)}, bf16[1024,512]{1,0:T(8,128)(2,1)S(1)}, u32[]{:S(2)}, u32[]{:S(2)}) collective-permute-start(bf16[1024,512]{1,0:T(8,128)(2,1)S(1)} %bitcast.93), channel_id=1, source_target_pairs={{0,128},{32,160},{64,192},{96,224},{128,0},{160,32},{192,64},{224,... | collective-permute-start | bytes 3145736 | tf_op jit(solution)/shard_map/ppermute | solution.py:22
  144.6 29.7 %copy-start.4 = (bf16[1024,512]{1,0:T(8,128)(2,1)}, bf16[1024,512]{1,0:T(8,128)(2,1)S(1)}, u32[]{:S(2)}) copy-start(bf16[1024,512]{1,0:T(8,128)(2,1)S(1)} %collective-permute-done.10) | copy-start | bytes 3145732
  179.2 19.4 %all-to-all-start.2 = ((bf16[8,64,1024]{2,1,0:T(8,128)(2,1)}), bf16[8,64,1024]{2,1,0:T(8,128)(2,1)S(1)}, u32[]{:S(2)}, u32[]{:S(2)}) async-start(bf16[8,64,1024]{2,1,0:T(8,128)(2,1)} %back.1), calls=%async_computation.2 | async-start | bytes 2097152 | tf_op jit(solution)/shard_map/all_to_all | solution.py:210
  199.2 4.6 %collective-permute-start.11 = (bf16[128,4096]{1,0:T(8,128)(2,1)S(1)}, bf16[128,4096]{1,0:T(8,128)(2,1)S(1)}, u32[]{:S(2)}, u32[]{:S(2)}) collective-permute-start(bf16[128,4096]{1,0:T(8,128)(2,1)S(1)} %convolution_convert_fusion), channel_id=1, source_target_pairs={{0,1},{1,0},{2,3},{3,2},{4,5},{5,4},{6,7},{7,6},{8,9},{9,8},{10,11... | collective-permute-start | bytes 3145736 | tf_op jit(solution)/shard_map/ppermute | solution.py:18
  204.2 51.1 %copy-start.5 = (bf16[8,4096]{1,0:T(8,128)(2,1)S(1)}, bf16[8,4096]{1,0:T(8,128)(2,1)}, u32[]{:S(2)}) copy-start(bf16[8,4096]{1,0:T(8,128)(2,1)} %param.7) | copy-start | bytes 196612
  204.3 51.3 %copy-start.6 = (f32[4096]{0:T(1024)S(1)}, f32[4096]{0:T(1024)}, u32[]{:S(2)}) copy-start(f32[4096]{0:T(1024)} %param.13) | copy-start | bytes 49156
  204.3 10.0 %collective-permute-start.12 = (bf16[24,4096]{1,0:T(8,128)(2,1)S(1)}, bf16[24,4096]{1,0:T(8,128)(2,1)S(1)}, u32[]{:S(2)}, u32[]{:S(2)}) collective-permute-start(bf16[24,4096]{1,0:T(8,128)(2,1)S(1)} %get-tuple-element.19), channel_id=1, source_target_pairs={{0,30},{1,31},{2,0},{3,1},{4,2},{5,3},{6,4},{7,5},{8,6},{9,7},{10,... | collective-permute-start | bytes 589832 | tf_op jit(solution)/shard_map/ppermute | solution.py:14
  206.2 9.3 %collective-permute-start.14 = (bf16[24,4096]{1,0:T(8,128)(2,1)S(1)}, bf16[24,4096]{1,0:T(8,128)(2,1)S(1)}, u32[]{:S(2)}, u32[]{:S(2)}) collective-permute-start(bf16[24,4096]{1,0:T(8,128)(2,1)S(1)} %get-tuple-element.20), channel_id=1, source_target_pairs={{0,2},{1,3},{2,4},{3,5},{4,6},{5,7},{6,8},{7,9},{8,10},{9,11},{10,... | collective-permute-start | bytes 589832 | tf_op jit(solution)/shard_map/ppermute | solution.py:14
  215.6 11.7 %collective-permute-start.15 = (bf16[24,4096]{1,0:T(8,128)(2,1)S(1)}, bf16[24,4096]{1,0:T(8,128)(2,1)S(1)}, u32[]{:S(2)}, u32[]{:S(2)}) collective-permute-start(bf16[24,4096]{1,0:T(8,128)(2,1)S(1)} %get-tuple-element.18), channel_id=1, source_target_pairs={{0,2},{1,3},{2,4},{3,5},{4,6},{5,7},{6,8},{7,9},{8,10},{9,11},{10,... | collective-permute-start | bytes 589832 | tf_op jit(solution)/shard_map/ppermute | solution.py:14
  221.2 8.8 %collective-permute-start.13 = (bf16[24,4096]{1,0:T(8,128)(2,1)S(1)}, bf16[24,4096]{1,0:T(8,128)(2,1)S(1)}, u32[]{:S(2)}, u32[]{:S(2)}) collective-permute-start(bf16[24,4096]{1,0:T(8,128)(2,1)S(1)} %get-tuple-element.17), channel_id=1, source_target_pairs={{0,30},{1,31},{2,0},{3,1},{4,2},{5,3},{6,4},{7,5},{8,6},{9,7},{10,... | collective-permute-start | bytes 589832 | tf_op jit(solution)/shard_map/ppermute | solution.py:14
  223.2 10.4 %collective-permute-start.17 = (bf16[8,4096]{1,0:T(8,128)(2,1)S(1)}, bf16[8,4096]{1,0:T(8,128)(2,1)S(1)}, u32[]{:S(2)}, u32[]{:S(2)}) collective-permute-start(bf16[8,4096]{1,0:T(8,128)(2,1)S(1)} %slice.166), channel_id=1, source_target_pairs={{0,6},{1,7},{2,8},{3,9},{4,10},{5,11},{6,12},{7,13},{8,14},{9,15},... | collective-permute-start | bytes 196616 | tf_op jit(solution)/shard_map/ppermute | solution.py:14
  233.6 13.8 %collective-permute-start.18 = (bf16[8,4096]{1,0:T(8,128)(2,1)S(1)}, bf16[8,4096]{1,0:T(8,128)(2,1)S(1)}, u32[]{:S(2)}, u32[]{:S(2)}) collective-permute-start(bf16[8,4096]{1,0:T(8,128)(2,1)S(1)} %fusion.4), channel_id=1, source_target_pairs={{0,10},{1,11},{2,12},{3,13},{4,14},{5,15},{6,16},{7,17},{8,18},{9,... | collective-permute-start | bytes 196616 | tf_op jit(solution)/shard_map/ppermute | solution.py:14
  242.3 13.1 %collective-permute-start.16 = (bf16[8,4096]{1,0:T(8,128)(2,1)S(1)}, bf16[8,4096]{1,0:T(8,128)(2,1)S(1)}, u32[]{:S(2)}, u32[]{:S(2)}) collective-permute-start(bf16[8,4096]{1,0:T(8,128)(2,1)S(1)} %slice.261), channel_id=1, source_target_pairs={{0,22},{1,23},{2,24},{3,25},{4,26},{5,27},{6,28},{7,29},{8,30},{9,... | collective-permute-start | bytes 196616 | tf_op jit(solution)/shard_map/ppermute | solution.py:14
  (4 other events, 49.0 us)

commit v3 on v2

--- a/solution.py
+++ b/solution.py
@@ -36,13 +36,16 @@
 
 
 def scatter_group(column, n):
-    below1, above1, below2, above2 = (column[3 * n * i:3 * n * (i + 1)] for i in range(1, 5))
-    below1 = below1 + around(below2.astype(BF16), -1).astype(F32)
-    above1 = above1 + around(above2.astype(BF16), 1).astype(F32)
-    eighth = around(column[15 * n:].astype(BF16), 3).astype(F32)
-    part = column[:3 * n] + around(below1.astype(BF16), -1).astype(F32) + around(above1.astype(BF16), 1).astype(F32)
+    sent = column[3 * n:].astype(BF16)
+    below1, above1, below2, above2 = (sent[3 * n * i:3 * n * (i + 1)] for i in range(4))
+    from_above2, from_below2 = around(below2, -2), around(above2, 2)
+    eighth = around(sent[12 * n:], 3)
+    from_above1, from_below1 = around(below1, -1), around(above1, 1)
+    part = column[:3 * n]
+    for other in (from_above2, from_below2, from_above1, from_below1):
+        part = part + other.astype(F32)
     below = around(part[n:2 * n].astype(BF16), -5)
-    above = around((part[2 * n:] + eighth).astype(BF16), 5)
+    above = around((part[2 * n:] + eighth.astype(F32)).astype(BF16), 5)
     return part[:n] + below.astype(F32) + above.astype(F32)
 
 
@@ -50,45 +53,20 @@
     return pl.BlockSpec(shape, lambda k: (0,) * len(shape))
 
 
-def pick_rows(onehot, near, other, width):
-    picked, half = onehot.shape[0], near.shape[0]
-    slots, block = picked // 2, 512
-
-    def kernel(onehot_ref, near_ref, other_ref, out_ref):
-        rows = jnp.dot(onehot_ref[:, :half], near_ref[...], preferred_element_type=F32)
-        rows = rows + jnp.dot(onehot_ref[:, half:], other_ref[...], preferred_element_type=F32)
-        rows = rows.astype(BF16)
-        for at in range(8):
-            start = at // 4 * slots
-            out_ref[at] = rows[start:start + slots]
-
-    return pl.pallas_call(
-        kernel,
-        grid=(width // block,),
-        in_specs=[
-            whole(onehot.shape),
-            pl.BlockSpec((half, block), lambda k: (0, k)),
-            pl.BlockSpec((half, block), lambda k: (0, k)),
-        ],
-        out_specs=pl.BlockSpec((8, slots, block), lambda k: (0, 0, k)),
-        out_shape=jax.ShapeDtypeStruct((8, slots, width), BF16),
-        name="pick_rows",
-    )(onehot, near, other)
-
-
 def front(odd, rows, gates, ups):
     count, width = rows.shape
-    units, block = gates[0].shape[1], 512
+    units, block = gates[0].shape[1], 1024
     steps = width // block
 
-    def kernel(odd_ref, rows_ref, gate_own, gate_other, up_own, up_other, out_ref, total):
+    def kernel(odd_ref, rows_ref, gate_own, gate_other, up_own, up_first, up_last, out_ref, total):
         k = pl.program_id(0)
 
         @pl.when(k == 0)
         def _():
             total[...] = jnp.zeros_like(total)
 
-        weights = jnp.concatenate([gate_own[...], gate_other[...], up_own[...], up_other[...]], 1)
+        up_other = jnp.where(k < steps // 2, up_first[...], up_last[...])
+        weights = jnp.concatenate([gate_own[...], gate_other[...], up_own[...], up_other], 1)
         total[...] += jnp.dot(rows_ref[...], weights, preferred_element_type=F32)
 
         @pl.when(k == steps - 1)
@@ -109,7 +87,9 @@
         in_specs=[
             pl.BlockSpec(memory_space=pltpu.SMEM),
             pl.BlockSpec((count, block), lambda k: (0, k)),
-            weight, weight, weight, weight,
+            weight, weight, weight,
+            pl.BlockSpec((block, units), lambda k: (jnp.minimum(k, steps // 2 - 1), 0)),
+            pl.BlockSpec((block, units), lambda k: (jnp.maximum(k - steps // 2, 0), 0)),
         ],
         out_specs=whole((4, count, 2 * units)),
         out_shape=jax.ShapeDtypeStruct((4, count, 2 * units), BF16),
@@ -121,7 +101,7 @@
 def back(odd, hidden, own, other, slots):
     parts, count, units = hidden.shape
     features = own.shape[1]
-    half = units // 2
+    half, steps = units // 2, parts // 2
     own, other = (w.reshape(2, own.shape[0] // 2, features) for w in (own, other))
 
     def kernel(odd_ref, hidden_ref, own_ref, other_ref, out_ref, total):
@@ -131,10 +111,14 @@
         def _():
             total[...] = jnp.zeros_like(total)
 
-        weights = [jnp.concatenate([w[0], w[1]], 0) for w in (own_ref, other_ref)]
-        total[...] += jnp.dot(hidden_ref[0], jnp.concatenate(weights, 1), preferred_element_type=F32)
-
-        @pl.when(k == parts - 1)
+        weights = [
+            jnp.concatenate([w[at, j * half:(j + 1) * half] for j in range(2) for at in range(2)], 0)
+            for w in (own_ref, other_ref)
+        ]
+        rows = jnp.concatenate([hidden_ref[0], hidden_ref[1]], 1)
+        total[...] += jnp.dot(rows, jnp.concatenate(weights, 1), preferred_element_type=F32)
+
+        @pl.when(k == steps - 1)
         def _():
             low, high = total[:, :features], total[:, features:]
             swap = odd_ref[0] == 1
@@ -142,14 +126,14 @@
             out_ref[:, :, :features] = jnp.where(swap, high, low).astype(BF16).reshape(shape)
             out_ref[:, :, features:] = jnp.where(swap, low, high).astype(BF16).reshape(shape)
 
-    weight = pl.BlockSpec((2, half, features), lambda k: (0, k, 0))
+    weight = pl.BlockSpec((2, 2 * half, features), lambda k: (0, k, 0))
     out = (count // slots, slots, 2 * features)
     return pl.pallas_call(
         kernel,
-        grid=(parts,),
+        grid=(steps,),
         in_specs=[
             pl.BlockSpec(memory_space=pltpu.SMEM),
-            pl.BlockSpec((1, count, units), lambda k: (k, 0, 0)),
+            pl.BlockSpec((2, count, units), lambda k: (k, 0, 0)),
             weight, weight,
         ],
         out_specs=whole(out),
@@ -167,14 +151,15 @@
     odd = (g // 4 % 2).astype(jnp.int32).reshape(1)
 
     gate_own, up_own, down_own = w_gate[0], w_up[0], w_down[0]
-    gate_other, up_other, down_other = pair_swap(gate_own), pair_swap(up_own), pair_swap(down_own)
+    middle = width // 2
+    gate_other, up_first, up_last = pair_swap(gate_own), pair_swap(up_own[:middle]), pair_swap(up_own[middle:])
 
     high = lax.reduce_precision(gate_weights, 8, 7)
     low = gate_weights - high
     extra = jnp.concatenate([expert_ids.astype(F32), high, low], 1).astype(BF16)
     extra = jnp.pad(extra, ((0, 0), (0, 128 - 3 * top)))
     column = gather_column(jnp.concatenate([tokens, extra], 1))
-    column, gate_other, up_other = lax.optimization_barrier((column, gate_other, up_other))
+    column, gate_other, up_first = lax.optimization_barrier((column, gate_other, up_first))
     parts = column, core_swap(column)
     half = parts[0].shape[0]
     rows = 2 * half
@@ -196,13 +181,18 @@
     picks = place[:, None, :] == jnp.arange(slots, dtype=F32)[None, :, None]
     picks = picks.reshape(2 * slots, rows)
     onehot = picks.astype(BF16)
-    fanned = pick_rows(onehot, parts[0], parts[1], width)
+    chosen = jnp.dot(onehot[:, :half], parts[0][:, :width], preferred_element_type=F32)
+    chosen = chosen + jnp.dot(onehot[:, half:], parts[1][:, :width], preferred_element_type=F32)
+    chosen = chosen.astype(BF16).reshape(2, 1, slots, width)
+    fanned = jnp.broadcast_to(chosen, (2, 4, slots, width)).reshape(8, slots, width)
+    fanned, up_last = lax.optimization_barrier((fanned, up_last))
 
     arrived = lax.all_to_all(fanned, "grp", split_axis=0, concat_axis=0, tiled=True, axis_index_groups=EIGHTS)
+    arrived, down_own = lax.optimization_barrier((arrived, down_own))
+    down_other = pair_swap(down_own)
     arrived = arrived.reshape(8 * slots, width)
 
-    hidden = front(odd, arrived, (gate_own, gate_other), (up_own, up_other))
-    hidden, down_other = lax.optimization_barrier((hidden, down_other))
+    hidden = front(odd, arrived, (gate_own, gate_other), (up_own, up_first, up_last))
     hidden = lax.all_to_all(hidden, "grp", split_axis=0, concat_axis=0, tiled=True, axis_index_groups=FOURS)
 
     features = down_own.shape[1]

time: 258 us -> 240 us (0.930)
  the two profiles are of different devices: /device:TPU:96 before, /device:TPU:32 now
where the time goes in v3:
time: 240 us; the launch traced here: 239 us
  starting transfers between devices  83.3 us (35%)
  blocking collectives  75.6 us (31%)
  waiting for transfers between devices  57.6 us (24%)
  Pallas kernels  10.8 us (4%)
  local copies, waits for them, and re-layouts  4.76 us (2%)
  other arithmetic  3.77 us (2%)
    ppermute x14, starting transfers between devices, around(): lax.ppermute(block, 'ep', [(i, (i + 2 * chips) % size) for i in range(siz...  64.7 us
    all_to_all x1, blocking collectives, shards(): lax.all_to_all(fanned, 'grp', split_axis=0, concat_axis=0, tiled=True, ax...  57.3 us
    ppermute x14, waiting for transfers between devices, around(): lax.ppermute(block, 'ep', [(i, (i + 2 * chips) % size) for i in range(siz...  26.8 us
    all_to_all x1, blocking collectives, shards(): lax.all_to_all(hidden, 'grp', split_axis=0, concat_axis=0, tiled=True, ax...  18.4 us
    all_to_all x1, waiting for transfers between devices, shards(): lax.all_to_all(out, 'grp', split_axis=0, concat_axis=0, tiled=True, axis_...  14.4 us
    ppermute x4, waiting for transfers between devices, pair_swap(): lax.ppermute(block, 'grp', [(i, i ^ 4) for i in range(lax.axis_size('grp'...  13.7 us
    ppermute x4, starting transfers between devices, pair_swap(): lax.ppermute(block, 'grp', [(i, i ^ 4) for i in range(lax.axis_size('grp'...  11.2 us
    pallas_call x1, Pallas kernels, front(): pl.pallas_call(kernel, grid=(steps,), in_specs=[pl.BlockSpec(memory_space...  6.73 us
  transfers between devices with their start and end apart: 21, of which 12 were waited for; matrix products, arithmetic and copies ran while one was open for 2% of the time, Pallas kernels for 3%

profile of v3, /device:TPU:32, one launch (start us, length us, event | category | flops | bytes accessed | tf_op | source)
XLA Modules:
  0.0 238.6 jit_solution(4718276021631647893)
XLA Ops:
  2.3 10.5 %collective-permute-start = (bf16[8,4224]{1,0:T(8,128)(2,1)S(1)}, bf16[8,4224]{1,0:T(8,128)(2,1)S(1)}, u32[]{:S(2)}, u32[]{:S(2)}) collective-permute-start(bf16[8,4224]{1,0:T(8,128)(2,1)S(1)} %get-tuple-element.43), channel_id=1, source_target_pairs={{0,10},{1,11},{2,12},{3,13},{4,14},{5,15},{6,16},{7,17},{8,18},{9,... | collective-permute-start | bytes 202760 | tf_op jit(solution)/shard_map/ppermute | solution.py:14
  12.8 3.8 %collective-permute-start.1 = (bf16[8,4224]{1,0:T(8,128)(2,1)S(1)}, bf16[8,4224]{1,0:T(8,128)(2,1)S(1)}, u32[]{:S(2)}, u32[]{:S(2)}) collective-permute-start(bf16[8,4224]{1,0:T(8,128)(2,1)S(1)} %get-tuple-element.43), channel_id=1, source_target_pairs={{0,22},{1,23},{2,24},{3,25},{4,26},{5,27},{6,28},{7,29},{8,30},{9,... | collective-permute-start | bytes 202760 | tf_op jit(solution)/shard_map/ppermute | solution.py:14
  16.6 3.5 %collective-permute-start.7 = (bf16[4096,128]{1,0:T(8,128)(2,1)}, bf16[4096,128]{1,0:T(8,128)(2,1)S(1)}, u32[]{:S(2)}, u32[]{:S(2)}) collective-permute-start(bf16[4096,128]{1,0:T(8,128)(2,1)} %bitcast.96), channel_id=1, source_target_pairs={{0,128},{32,160},{64,192},{96,224},{128,0},{160,32},{192,64},{224,... | collective-permute-start | bytes 3145736 | tf_op jit(solution)/shard_map/ppermute | solution.py:22
  24.7 3.2 %collective-permute-start.2 = (bf16[24,4224]{1,0:T(8,128)(2,1)S(1)}, bf16[24,4224]{1,0:T(8,128)(2,1)S(1)}, u32[]{:S(2)}, u32[]{:S(2)}) collective-permute-start(bf16[24,4224]{1,0:T(8,128)(2,1)S(1)} %pad_maximum_fusion.5), channel_id=1, source_target_pairs={{0,2},{1,3},{2,4},{3,5},{4,6},{5,7},{6,8},{7,9},{8,10},{9,11},{10,... | collective-permute-start | bytes 608264 | tf_op jit(solution)/shard_map/ppermute | solution.py:14
  27.9 3.6 %collective-permute-start.3 = (bf16[24,4224]{1,0:T(8,128)(2,1)S(1)}, bf16[24,4224]{1,0:T(8,128)(2,1)S(1)}, u32[]{:S(2)}, u32[]{:S(2)}) collective-permute-start(bf16[24,4224]{1,0:T(8,128)(2,1)S(1)} %pad_maximum_fusion.5), channel_id=1, source_target_pairs={{0,30},{1,31},{2,0},{3,1},{4,2},{5,3},{6,4},{7,5},{8,6},{9,7},{10,... | collective-permute-start | bytes 608264 | tf_op jit(solution)/shard_map/ppermute | solution.py:14
  31.5 7.6 %collective-permute-start.6 = (bf16[8,4224]{1,0:T(8,128)(2,1)S(1)}, bf16[8,4224]{1,0:T(8,128)(2,1)S(1)}, u32[]{:S(2)}, u32[]{:S(2)}) collective-permute-start(bf16[8,4224]{1,0:T(8,128)(2,1)S(1)} %collective-permute-done.1), channel_id=1, source_target_pairs={{0,26},{1,27},{2,28},{3,29},{4,30},{5,31},{6,0},{7,1},{8,2},{9,3},... | collective-permute-start | bytes 202760 | tf_op jit(solution)/shard_map/ppermute | solution.py:14
  39.2 2.9 %collective-permute-start.4 = (bf16[24,4224]{1,0:T(8,128)(2,1)S(1)}, bf16[24,4224]{1,0:T(8,128)(2,1)S(1)}, u32[]{:S(2)}, u32[]{:S(2)}) collective-permute-start(bf16[24,4224]{1,0:T(8,128)(2,1)S(1)} %collective-permute-done.2), channel_id=1, source_target_pairs={{0,2},{1,3},{2,4},{3,5},{4,6},{5,7},{6,8},{7,9},{8,10},{9,11},{10,... | collective-permute-start | bytes 608264 | tf_op jit(solution)/shard_map/ppermute | solution.py:14
  46.8 5.3 %collective-permute-done.5 = bf16[24,4224]{1,0:T(8,128)(2,1)S(1)} collective-permute-done((bf16[24,4224]{1,0:T(8,128)(2,1)S(1)}, bf16[24,4224]{1,0:T(8,128)(2,1)S(1)}, u32[]{:S(2)}, u32[]{:S(2)}) %collective-permute-start.5) | collective-permute-done | bytes 202784 | tf_op jit(solution)/shard_map/ppermute | solution.py:14
  57.3 3.5 %collective-permute-start.10 = (bf16[2048,128]{1,0:T(8,128)(2,1)}, bf16[2048,128]{1,0:T(8,128)(2,1)}, u32[]{:S(2)}, u32[]{:S(2)}) collective-permute-start(bf16[2048,128]{1,0:T(8,128)(2,1)} %get-tuple-element.41), channel_id=1, source_target_pairs={{0,128},{32,160},{64,192},{96,224},{128,0},{160,32},{192,64},{224,... | collective-permute-start | bytes 1572872 | tf_op jit(solution)/shard_map/ppermute | solution.py:22
  62.4 11.4 %collective-permute-done.10.up_last = bf16[2048,128]{1,0:T(8,128)(2,1)} collective-permute-done((bf16[2048,128]{1,0:T(8,128)(2,1)}, bf16[2048,128]{1,0:T(8,128)(2,1)}, u32[]{:S(2)}, u32[]{:S(2)}) %collective-permute-start.10) | collective-permute-done | bytes 524320 | tf_op jit(solution)/shard_map/ppermute | solution.py:22
  74.3 57.3 %all_to_all.15 = bf16[8,64,4096]{2,1,0:T(8,128)(2,1)} all-to-all(bf16[8,64,4096]{2,1,0:T(8,128)(2,1)S(1)} %bitcast.93), channel_id=1, replica_groups={{0,32,64,96,384,416,448,480},{128,160,192,224,256,288,320,352},{1,33,65..., dimensions={0} | all-to-all | bytes 8388608 | tf_op jit(solution)/shard_map/all_to_all | solution.py:190
  133.6 6.7 %front.1 = bf16[4,512,256]{2,1,0:T(8,128)(2,1)} custom-call(s32[1]{0:T(128)} %bitcast.5.odd_ref, bf16[512,4096]{1,0:T(8,128)(2,1)} %bitcast.92, bf16[4096,128]{1,0:T(8,128)(2,1)} %bitcast.97, bf16[4096,128]{1,0:T(8,128)(2,1)} %copy-done.1, bf16[4096,128]{1,0:T(8,128)(2,1)} %bitcast.94, bf16[2048,128]{1,0:T(8,128)(2,1)} %copy-done.4, ...), custom_call_target="tpu_custom_call" | custom-call | tf_op jit(solution)/shard_map/front/pallas_call | solution.py:84
  140.3 18.4 %all_to_all.16.hidden_ref = bf16[4,512,256]{2,1,0:T(8,128)(2,1)} all-to-all(bf16[4,512,256]{2,1,0:T(8,128)(2,1)} %front.1), channel_id=1, replica_groups={{0,32,64,96},{128,160,192,224},{256,288,320,352},{384,416,448,480},{1,3..., dimensions={0} | all-to-all | bytes 2097152 | tf_op jit(solution)/shard_map/all_to_all | solution.py:196
  159.6 4.1 %back.1 = bf16[8,64,1024]{2,1,0:T(8,128)(2,1)} custom-call(s32[1]{0:T(128)} %bitcast.5.odd_ref, bf16[4,512,256]{2,1,0:T(8,128)(2,1)} %all_to_all.16.hidden_ref, bf16[2,512,512]{2,1,0:T(8,128)(2,1)} %bitcast.98, bf16[2,512,512]{2,1,0:T(8,128)(2,1)} %bitcast.100), custom_call_target="tpu_custom_call" | custom-call | tf_op jit(solution)/shard_map/back/pallas_call | solution.py:131
  163.7 3.6 %all-to-all-start.2 = ((bf16[8,64,1024]{2,1,0:T(8,128)(2,1)}), bf16[8,64,1024]{2,1,0:T(8,128)(2,1)S(1)}, u32[]{:S(2)}, u32[]{:S(2)}) async-start(bf16[8,64,1024]{2,1,0:T(8,128)(2,1)} %back.1), calls=%async_computation.2 | async-start | bytes 2097152 | tf_op jit(solution)/shard_map/all_to_all | solution.py:200
  167.5 14.4 %all-to-all-done.2 = bf16[8,64,1024]{2,1,0:T(8,128)(2,1)S(1)} async-done(((bf16[8,64,1024]{2,1,0:T(8,128)(2,1)}), bf16[8,64,1024]{2,1,0:T(8,128)(2,1)S(1)}, u32[]{:S(2)}, u32[]{:S(2)}) %all-to-all-start.2) | async-done | bytes 1048608 | tf_op jit(solution)/shard_map/all_to_all | solution.py:200
  187.6 2.9 %collective-permute-start.16 = (bf16[24,4096]{1,0:T(8,128)(2,1)S(1)}, bf16[24,4096]{1,0:T(8,128)(2,1)S(1)}, u32[]{:S(2)}, u32[]{:S(2)}) collective-permute-start(bf16[24,4096]{1,0:T(8,128)(2,1)S(1)} %get-tuple-element.22), channel_id=1, source_target_pairs={{0,2},{1,3},{2,4},{3,5},{4,6},{5,7},{6,8},{7,9},{8,10},{9,11},{10,... | collective-permute-start | bytes 589832 | tf_op jit(solution)/shard_map/ppermute | solution.py:14
  190.5 3.1 %collective-permute-start.15 = (bf16[24,4096]{1,0:T(8,128)(2,1)S(1)}, bf16[24,4096]{1,0:T(8,128)(2,1)S(1)}, u32[]{:S(2)}, u32[]{:S(2)}) collective-permute-start(bf16[24,4096]{1,0:T(8,128)(2,1)S(1)} %get-tuple-element.23), channel_id=1, source_target_pairs={{0,30},{1,31},{2,0},{3,1},{4,2},{5,3},{6,4},{7,5},{8,6},{9,7},{10,... | collective-permute-start | bytes 589832 | tf_op jit(solution)/shard_map/ppermute | solution.py:14
  193.7 4.4 %collective-permute-start.14 = (bf16[24,4096]{1,0:T(8,128)(2,1)S(1)}, bf16[24,4096]{1,0:T(8,128)(2,1)S(1)}, u32[]{:S(2)}, u32[]{:S(2)}) collective-permute-start(bf16[24,4096]{1,0:T(8,128)(2,1)S(1)} %get-tuple-element.24), channel_id=1, source_target_pairs={{0,4},{1,5},{2,6},{3,7},{4,8},{5,9},{6,10},{7,11},{8,12},{9,13},{1... | collective-permute-start | bytes 589832 | tf_op jit(solution)/shard_map/ppermute | solution.py:14
  198.0 4.5 %collective-permute-start.13 = (bf16[24,4096]{1,0:T(8,128)(2,1)S(1)}, bf16[24,4096]{1,0:T(8,128)(2,1)S(1)}, u32[]{:S(2)}, u32[]{:S(2)}) collective-permute-start(bf16[24,4096]{1,0:T(8,128)(2,1)S(1)} %get-tuple-element.21), channel_id=1, source_target_pairs={{0,28},{1,29},{2,30},{3,31},{4,0},{5,1},{6,2},{7,3},{8,4},{9,5},{1... | collective-permute-start | bytes 589832 | tf_op jit(solution)/shard_map/ppermute | solution.py:14
  202.5 5.2 %collective-permute-start.18 = (bf16[8,4096]{1,0:T(8,128)(2,1)S(1)}, bf16[8,4096]{1,0:T(8,128)(2,1)S(1)}, u32[]{:S(2)}, u32[]{:S(2)}) collective-permute-start(bf16[8,4096]{1,0:T(8,128)(2,1)S(1)} %slice.205), channel_id=1, source_target_pairs={{0,6},{1,7},{2,8},{3,9},{4,10},{5,11},{6,12},{7,13},{8,14},{9,15},... | collective-permute-start | bytes 196616 | tf_op jit(solution)/shard_map/ppermute | solution.py:14
  213.6 8.2 %collective-permute-start.19 = (bf16[8,4096]{1,0:T(8,128)(2,1)S(1)}, bf16[8,4096]{1,0:T(8,128)(2,1)S(1)}, u32[]{:S(2)}, u32[]{:S(2)}) collective-permute-start(bf16[8,4096]{1,0:T(8,128)(2,1)S(1)} %fusion.8), channel_id=1, source_target_pairs={{0,10},{1,11},{2,12},{3,13},{4,14},{5,15},{6,16},{7,17},{8,18},{9,... | collective-permute-start | bytes 196616 | tf_op jit(solution)/shard_map/ppermute | solution.py:14
  221.8 3.0 %collective-permute-start.17 = (bf16[8,4096]{1,0:T(8,128)(2,1)S(1)}, bf16[8,4096]{1,0:T(8,128)(2,1)S(1)}, u32[]{:S(2)}, u32[]{:S(2)}) collective-permute-start(bf16[8,4096]{1,0:T(8,128)(2,1)S(1)} %slice.308), channel_id=1, source_target_pairs={{0,22},{1,23},{2,24},{3,25},{4,26},{5,27},{6,28},{7,29},{8,30},{9,... | collective-permute-start | bytes 196616 | tf_op jit(solution)/shard_map/ppermute | solution.py:14
  226.7 10.9 %collective-permute-done.17 = bf16[8,4096]{1,0:T(8,128)(2,1)S(1)} collective-permute-done((bf16[8,4096]{1,0:T(8,128)(2,1)S(1)}, bf16[8,4096]{1,0:T(8,128)(2,1)S(1)}, u32[]{:S(2)}, u32[]{:S(2)}) %collective-permute-start.17) | collective-permute-done | bytes 65568 | tf_op jit(solution)/shard_map/ppermute | solution.py:14
  (79 shorter events, 36.3 us)
Async XLA Ops:
  0.0 24.7 %copy-start.3 = (bf16[8,4096]{1,0:T(8,128)(2,1)S(1)}, bf16[8,4096]{1,0:T(8,128)(2,1)}, u32[]{:S(2)}) copy-start(bf16[8,4096]{1,0:T(8,128)(2,1)} %param.7) | copy-start | bytes 196612
  2.3 22.1 %collective-permute-start = (bf16[8,4224]{1,0:T(8,128)(2,1)S(1)}, bf16[8,4224]{1,0:T(8,128)(2,1)S(1)}, u32[]{:S(2)}, u32[]{:S(2)}) collective-permute-start(bf16[8,4224]{1,0:T(8,128)(2,1)S(1)} %get-tuple-element.43), channel_id=1, source_target_pairs={{0,10},{1,11},{2,12},{3,13},{4,14},{5,15},{6,16},{7,17},{8,18},{9,... | collective-permute-start | bytes 202760 | tf_op jit(solution)/shard_map/ppermute | solution.py:14
  12.8 11.9 %collective-permute-start.1 = (bf16[8,4224]{1,0:T(8,128)(2,1)S(1)}, bf16[8,4224]{1,0:T(8,128)(2,1)S(1)}, u32[]{:S(2)}, u32[]{:S(2)}) collective-permute-start(bf16[8,4224]{1,0:T(8,128)(2,1)S(1)} %get-tuple-element.43), channel_id=1, source_target_pairs={{0,22},{1,23},{2,24},{3,25},{4,26},{5,27},{6,28},{7,29},{8,30},{9,... | collective-permute-start | bytes 202760 | tf_op jit(solution)/shard_map/ppermute | solution.py:14
  16.6 38.8 %collective-permute-start.7 = (bf16[4096,128]{1,0:T(8,128)(2,1)}, bf16[4096,128]{1,0:T(8,128)(2,1)S(1)}, u32[]{:S(2)}, u32[]{:S(2)}) collective-permute-start(bf16[4096,128]{1,0:T(8,128)(2,1)} %bitcast.96), channel_id=1, source_target_pairs={{0,128},{32,160},{64,192},{96,224},{128,0},{160,32},{192,64},{224,... | collective-permute-start | bytes 3145736 | tf_op jit(solution)/shard_map/ppermute | solution.py:22
  22.1 32.4 %collective-permute-start.8 = (bf16[2048,128]{1,0:T(8,128)(2,1)S(1)}, bf16[2048,128]{1,0:T(8,128)(2,1)S(1)}, u32[]{:S(2)}, u32[]{:S(2)}) collective-permute-start(bf16[2048,128]{1,0:T(8,128)(2,1)S(1)} %get-tuple-element.42), channel_id=1, source_target_pairs={{0,128},{32,160},{64,192},{96,224},{128,0},{160,32},{192,64},{224,... | collective-permute-start | bytes 1572872 | tf_op jit(solution)/shard_map/ppermute | solution.py:22
  24.7 14.5 %collective-permute-start.2 = (bf16[24,4224]{1,0:T(8,128)(2,1)S(1)}, bf16[24,4224]{1,0:T(8,128)(2,1)S(1)}, u32[]{:S(2)}, u32[]{:S(2)}) collective-permute-start(bf16[24,4224]{1,0:T(8,128)(2,1)S(1)} %pad_maximum_fusion.5), channel_id=1, source_target_pairs={{0,2},{1,3},{2,4},{3,5},{4,6},{5,7},{6,8},{7,9},{8,10},{9,11},{10,... | collective-permute-start | bytes 608264 | tf_op jit(solution)/shard_map/ppermute | solution.py:14
  27.9 16.6 %collective-permute-start.3 = (bf16[24,4224]{1,0:T(8,128)(2,1)S(1)}, bf16[24,4224]{1,0:T(8,128)(2,1)S(1)}, u32[]{:S(2)}, u32[]{:S(2)}) collective-permute-start(bf16[24,4224]{1,0:T(8,128)(2,1)S(1)} %pad_maximum_fusion.5), channel_id=1, source_target_pairs={{0,30},{1,31},{2,0},{3,1},{4,2},{5,3},{6,4},{7,5},{8,6},{9,7},{10,... | collective-permute-start | bytes 608264 | tf_op jit(solution)/shard_map/ppermute | solution.py:14
  31.5 20.6 %collective-permute-start.6 = (bf16[8,4224]{1,0:T(8,128)(2,1)S(1)}, bf16[8,4224]{1,0:T(8,128)(2,1)S(1)}, u32[]{:S(2)}, u32[]{:S(2)}) collective-permute-start(bf16[8,4224]{1,0:T(8,128)(2,1)S(1)} %collective-permute-done.1), channel_id=1, source_target_pairs={{0,26},{1,27},{2,28},{3,29},{4,30},{5,31},{6,0},{7,1},{8,2},{9,3},... | collective-permute-start | bytes 202760 | tf_op jit(solution)/shard_map/ppermute | solution.py:14
  39.2 7.6 %collective-permute-start.4 = (bf16[24,4224]{1,0:T(8,128)(2,1)S(1)}, bf16[24,4224]{1,0:T(8,128)(2,1)S(1)}, u32[]{:S(2)}, u32[]{:S(2)}) collective-permute-start(bf16[24,4224]{1,0:T(8,128)(2,1)S(1)} %collective-permute-done.2), channel_id=1, source_target_pairs={{0,2},{1,3},{2,4},{3,5},{4,6},{5,7},{6,8},{7,9},{8,10},{9,11},{10,... | collective-permute-start | bytes 608264 | tf_op jit(solution)/shard_map/ppermute | solution.py:14
  44.5 7.6 %collective-permute-start.5 = (bf16[24,4224]{1,0:T(8,128)(2,1)S(1)}, bf16[24,4224]{1,0:T(8,128)(2,1)S(1)}, u32[]{:S(2)}, u32[]{:S(2)}) collective-permute-start(bf16[24,4224]{1,0:T(8,128)(2,1)S(1)} %collective-permute-done.3), channel_id=1, source_target_pairs={{0,30},{1,31},{2,0},{3,1},{4,2},{5,3},{6,4},{7,5},{8,6},{9,7},{10,... | collective-permute-start | bytes 608264 | tf_op jit(solution)/shard_map/ppermute | solution.py:14
  55.4 5.6 %collective-permute-start.9 = (bf16[128,4224]{1,0:T(8,128)(2,1)S(1)}, bf16[128,4224]{1,0:T(8,128)(2,1)S(1)}, u32[]{:S(2)}, u32[]{:S(2)}) collective-permute-start(bf16[128,4224]{1,0:T(8,128)(2,1)S(1)} %constant_dynamic-update-slice_fusion), channel_id=1, source_target_pairs={{0,1},{1,0},{2,3},{3,2},{4,5},{5,4},{6,7},{7,6},{8,9},{9,8},{10,11... | collective-permute-start | bytes 3244040 | tf_op jit(solution)/shard_map/ppermute | solution.py:18
  57.3 16.5 %collective-permute-start.10 = (bf16[2048,128]{1,0:T(8,128)(2,1)}, bf16[2048,128]{1,0:T(8,128)(2,1)}, u32[]{:S(2)}, u32[]{:S(2)}) collective-permute-start(bf16[2048,128]{1,0:T(8,128)(2,1)} %get-tuple-element.41), channel_id=1, source_target_pairs={{0,128},{32,160},{64,192},{96,224},{128,0},{160,32},{192,64},{224,... | collective-permute-start | bytes 1572872 | tf_op jit(solution)/shard_map/ppermute | solution.py:22
  74.3 57.3 %copy-start = (bf16[1,1024,512]{2,1,0:T(8,128)(2,1)S(1)}, bf16[1,1024,512]{2,1,0:T(8,128)(2,1)}, u32[]{:S(2)}) copy-start(bf16[1,1024,512]{2,1,0:T(8,128)(2,1)} %param.12) | copy-start | bytes 3145732
  131.6 27.0 %collective-permute-start.11 = (bf16[1024,512]{1,0:T(8,128)(2,1)S(1)}, bf16[1024,512]{1,0:T(8,128)(2,1)S(1)}, u32[]{:S(2)}, u32[]{:S(2)}) collective-permute-start(bf16[1024,512]{1,0:T(8,128)(2,1)S(1)} %bitcast.99), channel_id=1, source_target_pairs={{0,128},{32,160},{64,192},{96,224},{128,0},{160,32},{192,64},{224,... | collective-permute-start | bytes 3145736 | tf_op jit(solution)/shard_map/ppermute | solution.py:22
  163.7 18.2 %all-to-all-start.2 = ((bf16[8,64,1024]{2,1,0:T(8,128)(2,1)}), bf16[8,64,1024]{2,1,0:T(8,128)(2,1)S(1)}, u32[]{:S(2)}, u32[]{:S(2)}) async-start(bf16[8,64,1024]{2,1,0:T(8,128)(2,1)} %back.1), calls=%async_computation.2 | async-start | bytes 2097152 | tf_op jit(solution)/shard_map/all_to_all | solution.py:200
  182.5 4.6 %collective-permute-start.12 = (bf16[128,4096]{1,0:T(8,128)(2,1)S(1)}, bf16[128,4096]{1,0:T(8,128)(2,1)S(1)}, u32[]{:S(2)}, u32[]{:S(2)}) collective-permute-start(bf16[128,4096]{1,0:T(8,128)(2,1)S(1)} %convolution_convert_fusion), channel_id=1, source_target_pairs={{0,1},{1,0},{2,3},{3,2},{4,5},{5,4},{6,7},{7,6},{8,9},{9,8},{10,11... | collective-permute-start | bytes 3145736 | tf_op jit(solution)/shard_map/ppermute | solution.py:18
  187.5 50.3 %copy-start.5 = (f32[4096]{0:T(1024)S(1)}, f32[4096]{0:T(1024)}, u32[]{:S(2)}) copy-start(f32[4096]{0:T(1024)} %param.13) | copy-start | bytes 49156
  187.6 20.2 %collective-permute-start.16 = (bf16[24,4096]{1,0:T(8,128)(2,1)S(1)}, bf16[24,4096]{1,0:T(8,128)(2,1)S(1)}, u32[]{:S(2)}, u32[]{:S(2)}) collective-permute-start(bf16[24,4096]{1,0:T(8,128)(2,1)S(1)} %get-tuple-element.22), channel_id=1, source_target_pairs={{0,2},{1,3},{2,4},{3,5},{4,6},{5,7},{6,8},{7,9},{8,10},{9,11},{10,... | collective-permute-start | bytes 589832 | tf_op jit(solution)/shard_map/ppermute | solution.py:14
  190.5 17.3 %collective-permute-start.15 = (bf16[24,4096]{1,0:T(8,128)(2,1)S(1)}, bf16[24,4096]{1,0:T(8,128)(2,1)S(1)}, u32[]{:S(2)}, u32[]{:S(2)}) collective-permute-start(bf16[24,4096]{1,0:T(8,128)(2,1)S(1)} %get-tuple-element.23), channel_id=1, source_target_pairs={{0,30},{1,31},{2,0},{3,1},{4,2},{5,3},{6,4},{7,5},{8,6},{9,7},{10,... | collective-permute-start | bytes 589832 | tf_op jit(solution)/shard_map/ppermute | solution.py:14
  193.7 14.1 %collective-permute-start.14 = (bf16[24,4096]{1,0:T(8,128)(2,1)S(1)}, bf16[24,4096]{1,0:T(8,128)(2,1)S(1)}, u32[]{:S(2)}, u32[]{:S(2)}) collective-permute-start(bf16[24,4096]{1,0:T(8,128)(2,1)S(1)} %get-tuple-element.24), channel_id=1, source_target_pairs={{0,4},{1,5},{2,6},{3,7},{4,8},{5,9},{6,10},{7,11},{8,12},{9,13},{1... | collective-permute-start | bytes 589832 | tf_op jit(solution)/shard_map/ppermute | solution.py:14
  198.0 12.6 %collective-permute-start.13 = (bf16[24,4096]{1,0:T(8,128)(2,1)S(1)}, bf16[24,4096]{1,0:T(8,128)(2,1)S(1)}, u32[]{:S(2)}, u32[]{:S(2)}) collective-permute-start(bf16[24,4096]{1,0:T(8,128)(2,1)S(1)} %get-tuple-element.21), channel_id=1, source_target_pairs={{0,28},{1,29},{2,30},{3,31},{4,0},{5,1},{6,2},{7,3},{8,4},{9,5},{1... | collective-permute-start | bytes 589832 | tf_op jit(solution)/shard_map/ppermute | solution.py:14
  202.5 11.1 %collective-permute-start.18 = (bf16[8,4096]{1,0:T(8,128)(2,1)S(1)}, bf16[8,4096]{1,0:T(8,128)(2,1)S(1)}, u32[]{:S(2)}, u32[]{:S(2)}) collective-permute-start(bf16[8,4096]{1,0:T(8,128)(2,1)S(1)} %slice.205), channel_id=1, source_target_pairs={{0,6},{1,7},{2,8},{3,9},{4,10},{5,11},{6,12},{7,13},{8,14},{9,15},... | collective-permute-start | bytes 196616 | tf_op jit(solution)/shard_map/ppermute | solution.py:14
  213.6 13.1 %collective-permute-start.19 = (bf16[8,4096]{1,0:T(8,128)(2,1)S(1)}, bf16[8,4096]{1,0:T(8,128)(2,1)S(1)}, u32[]{:S(2)}, u32[]{:S(2)}) collective-permute-start(bf16[8,4096]{1,0:T(8,128)(2,1)S(1)} %fusion.8), channel_id=1, source_target_pairs={{0,10},{1,11},{2,12},{3,13},{4,14},{5,15},{6,16},{7,17},{8,18},{9,... | collective-permute-start | bytes 196616 | tf_op jit(solution)/shard_map/ppermute | solution.py:14
  221.8 15.9 %collective-permute-start.17 = (bf16[8,4096]{1,0:T(8,128)(2,1)S(1)}, bf16[8,4096]{1,0:T(8,128)(2,1)S(1)}, u32[]{:S(2)}, u32[]{:S(2)}) collective-permute-start(bf16[8,4096]{1,0:T(8,128)(2,1)S(1)} %slice.308), channel_id=1, source_target_pairs={{0,22},{1,23},{2,24},{3,25},{4,26},{5,27},{6,28},{7,29},{8,30},{9,... | collective-permute-start | bytes 196616 | tf_op jit(solution)/shard_map/ppermute | solution.py:14
  (3 other events, 8.9 us)

commit v4 on v3

--- a/solution.py
+++ b/solution.py
@@ -53,20 +53,41 @@
     return pl.BlockSpec(shape, lambda k: (0,) * len(shape))
 
 
+def with_facts(tokens, ids, weights):
+    n, width = tokens.shape
+    top = ids.shape[1]
+
+    def kernel(tokens_ref, ids_ref, weights_ref, out_ref):
+        out_ref[:, :width] = tokens_ref[...]
+        named = ids_ref[...].astype(F32).astype(BF16)
+        high = weights_ref[...].astype(BF16)
+        low = (weights_ref[...] - high.astype(F32)).astype(BF16)
+        lane = lax.broadcasted_iota(jnp.int32, (top, 128), 1)
+        row = lax.broadcasted_iota(jnp.int32, (top, 128), 0)
+        facts = jnp.zeros((n, 128), F32)
+        for at, part in enumerate((named, high, low)):
+            place = jnp.where(lane == row + at * top, 1.0, 0.0).astype(BF16)
+            facts = facts + jnp.dot(part, place, preferred_element_type=F32)
+        out_ref[:, width:] = facts.astype(BF16)
+
+    return pl.pallas_call(
+        kernel, out_shape=jax.ShapeDtypeStruct((n, width + 128), BF16), name="with_facts"
+    )(tokens, ids, weights)
+
+
 def front(odd, rows, gates, ups):
     count, width = rows.shape
     units, block = gates[0].shape[1], 1024
     steps = width // block
 
-    def kernel(odd_ref, rows_ref, gate_own, gate_other, up_own, up_first, up_last, out_ref, total):
+    def kernel(odd_ref, rows_ref, gate_own, gate_other, up_own, up_other, out_ref, total):
         k = pl.program_id(0)
 
         @pl.when(k == 0)
         def _():
             total[...] = jnp.zeros_like(total)
 
-        up_other = jnp.where(k < steps // 2, up_first[...], up_last[...])
-        weights = jnp.concatenate([gate_own[...], gate_other[...], up_own[...], up_other], 1)
+        weights = jnp.concatenate([gate_own[...], gate_other[...], up_own[...], up_other[...]], 1)
         total[...] += jnp.dot(rows_ref[...], weights, preferred_element_type=F32)
 
         @pl.when(k == steps - 1)
@@ -87,9 +108,7 @@
         in_specs=[
             pl.BlockSpec(memory_space=pltpu.SMEM),
             pl.BlockSpec((count, block), lambda k: (0, k)),
-            weight, weight, weight,
-            pl.BlockSpec((block, units), lambda k: (jnp.minimum(k, steps // 2 - 1), 0)),
-            pl.BlockSpec((block, units), lambda k: (jnp.maximum(k - steps // 2, 0), 0)),
+            weight, weight, weight, weight,
         ],
         out_specs=whole((4, count, 2 * units)),
         out_shape=jax.ShapeDtypeStruct((4, count, 2 * units), BF16),
@@ -151,15 +170,9 @@
     odd = (g // 4 % 2).astype(jnp.int32).reshape(1)
 
     gate_own, up_own, down_own = w_gate[0], w_up[0], w_down[0]
-    middle = width // 2
-    gate_other, up_first, up_last = pair_swap(gate_own), pair_swap(up_own[:middle]), pair_swap(up_own[middle:])
-
-    high = lax.reduce_precision(gate_weights, 8, 7)
-    low = gate_weights - high
-    extra = jnp.concatenate([expert_ids.astype(F32), high, low], 1).astype(BF16)
-    extra = jnp.pad(extra, ((0, 0), (0, 128 - 3 * top)))
-    column = gather_column(jnp.concatenate([tokens, extra], 1))
-    column, gate_other, up_first = lax.optimization_barrier((column, gate_other, up_first))
+    gate_other, up_other, down_other = pair_swap(gate_own), pair_swap(up_own), pair_swap(down_own)
+
+    column = gather_column(with_facts(tokens, expert_ids, gate_weights))
     parts = column, core_swap(column)
     half = parts[0].shape[0]
     rows = 2 * half
@@ -185,14 +198,12 @@
     chosen = chosen + jnp.dot(onehot[:, half:], parts[1][:, :width], preferred_element_type=F32)
     chosen = chosen.astype(BF16).reshape(2, 1, slots, width)
     fanned = jnp.broadcast_to(chosen, (2, 4, slots, width)).reshape(8, slots, width)
-    fanned, up_last = lax.optimization_barrier((fanned, up_last))
 
     arrived = lax.all_to_all(fanned, "grp", split_axis=0, concat_axis=0, tiled=True, axis_index_groups=EIGHTS)
-    arrived, down_own = lax.optimization_barrier((arrived, down_own))
-    down_other = pair_swap(down_own)
     arrived = arrived.reshape(8 * slots, width)
 
-    hidden = front(odd, arrived, (gate_own, gate_other), (up_own, up_first, up_last))
+    hidden = front(odd, arrived, (gate_own, gate_other), (up_own, up_other))
+    hidden, down_other = lax.optimization_barrier((hidden, down_other))
     hidden = lax.all_to_all(hidden, "grp", split_axis=0, concat_axis=0, tiled=True, axis_index_groups=FOURS)
 
     features = down_own.shape[1]

time: 240 us -> 236 us (0.983)
  the two profiles are of different devices: /device:TPU:32 before, /device:TPU:1 now
where the time goes in v4:
time: 236 us; the launch traced here: 234 us
  waiting for transfers between devices  101 us (43%)
  starting transfers between devices  94.2 us (40%)
  blocking collectives  17.6 us (7%)
  Pallas kernels  12.3 us (5%)
  local copies, waits for them, and re-layouts  3.83 us (2%)
    ppermute x14, starting transfers between devices, around(): lax.ppermute(block, 'ep', [(i, (i + 2 * chips) % size) for i in range(siz...  67.8 us
    ppermute x3, waiting for transfers between devices, pair_swap(): lax.ppermute(block, 'grp', [(i, i ^ 4) for i in range(lax.axis_size('grp'...  54.7 us
    ppermute x14, waiting for transfers between devices, around(): lax.ppermute(block, 'ep', [(i, (i + 2 * chips) % size) for i in range(siz...  22.9 us
    all_to_all x1, blocking collectives, shards(): lax.all_to_all(hidden, 'grp', split_axis=0, concat_axis=0, tiled=True, ax...  17.6 us
    all_to_all x1, waiting for transfers between devices, shards(): lax.all_to_all(out, 'grp', split_axis=0, concat_axis=0, tiled=True, axis_...  16.5 us
    ppermute x2, starting transfers between devices, core_swap(): lax.ppermute(block, 'ep', [(i, i ^ 1) for i in range(lax.axis_size('ep'))])  8.27 us
    ppermute x3, starting transfers between devices, pair_swap(): lax.ppermute(block, 'grp', [(i, i ^ 4) for i in range(lax.axis_size('grp'...  7.21 us
    all_to_all x1, starting transfers between devices, shards(): lax.all_to_all(fanned, 'grp', split_axis=0, concat_axis=0, tiled=True, ax...  6.73 us
  transfers between devices with their start and end apart: 21, of which 15 were waited for; matrix products, arithmetic and copies ran while one was open for 1% of the time, Pallas kernels for 3%

profile of v4, /device:TPU:1, one launch (start us, length us, event | category | flops | bytes accessed | tf_op | source)
XLA Modules:
  0.0 233.7 jit_solution(15617349953505299737)
XLA Ops:
  1.6 11.0 %collective-permute-start = (bf16[8,4224]{1,0:T(8,128)(2,1)}, bf16[8,4224]{1,0:T(8,128)(2,1)S(1)}, u32[]{:S(2)}, u32[]{:S(2)}) collective-permute-start(bf16[8,4224]{1,0:T(8,128)(2,1)} %with_facts.1), channel_id=1, source_target_pairs={{0,10},{1,11},{2,12},{3,13},{4,14},{5,15},{6,16},{7,17},{8,18},{9,... | collective-permute-start | bytes 202760 | tf_op jit(solution)/shard_map/ppermute | solution.py:14
  12.6 5.9 %collective-permute-start.1 = (bf16[8,4224]{1,0:T(8,128)(2,1)}, bf16[8,4224]{1,0:T(8,128)(2,1)S(1)}, u32[]{:S(2)}, u32[]{:S(2)}) collective-permute-start(bf16[8,4224]{1,0:T(8,128)(2,1)} %with_facts.1), channel_id=1, source_target_pairs={{0,22},{1,23},{2,24},{3,25},{4,26},{5,27},{6,28},{7,29},{8,30},{9,... | collective-permute-start | bytes 202760 | tf_op jit(solution)/shard_map/ppermute | solution.py:14
  19.4 4.6 %collective-permute-done.1 = bf16[8,4224]{1,0:T(8,128)(2,1)S(1)} collective-permute-done((bf16[8,4224]{1,0:T(8,128)(2,1)}, bf16[8,4224]{1,0:T(8,128)(2,1)S(1)}, u32[]{:S(2)}, u32[]{:S(2)}) %collective-permute-start.1) | collective-permute-done | bytes 67616 | tf_op jit(solution)/shard_map/ppermute | solution.py:14
  27.4 4.5 %collective-permute-start.3 = (bf16[24,4224]{1,0:T(8,128)(2,1)S(1)}, bf16[24,4224]{1,0:T(8,128)(2,1)S(1)}, u32[]{:S(2)}, u32[]{:S(2)}) collective-permute-start(bf16[24,4224]{1,0:T(8,128)(2,1)S(1)} %pad_maximum_fusion.5), channel_id=1, source_target_pairs={{0,30},{1,31},{2,0},{3,1},{4,2},{5,3},{6,4},{7,5},{8,6},{9,7},{10,... | collective-permute-start | bytes 608264 | tf_op jit(solution)/shard_map/ppermute | solution.py:14
  31.9 7.4 %collective-permute-start.6 = (bf16[8,4224]{1,0:T(8,128)(2,1)S(1)}, bf16[8,4224]{1,0:T(8,128)(2,1)S(1)}, u32[]{:S(2)}, u32[]{:S(2)}) collective-permute-start(bf16[8,4224]{1,0:T(8,128)(2,1)S(1)} %collective-permute-done.1), channel_id=1, source_target_pairs={{0,26},{1,27},{2,28},{3,29},{4,30},{5,31},{6,0},{7,1},{8,2},{9,3},... | collective-permute-start | bytes 202760 | tf_op jit(solution)/shard_map/ppermute | solution.py:14
  39.3 3.4 %collective-permute-start.4 = (bf16[24,4224]{1,0:T(8,128)(2,1)S(1)}, bf16[24,4224]{1,0:T(8,128)(2,1)S(1)}, u32[]{:S(2)}, u32[]{:S(2)}) collective-permute-start(bf16[24,4224]{1,0:T(8,128)(2,1)S(1)} %collective-permute-done.2), channel_id=1, source_target_pairs={{0,2},{1,3},{2,4},{3,5},{4,6},{5,7},{6,8},{7,9},{8,10},{9,11},{10,... | collective-permute-start | bytes 608264 | tf_op jit(solution)/shard_map/ppermute | solution.py:14
  42.7 3.1 %collective-permute-start.5 = (bf16[24,4224]{1,0:T(8,128)(2,1)S(1)}, bf16[24,4224]{1,0:T(8,128)(2,1)S(1)}, u32[]{:S(2)}, u32[]{:S(2)}) collective-permute-start(bf16[24,4224]{1,0:T(8,128)(2,1)S(1)} %collective-permute-done.3), channel_id=1, source_target_pairs={{0,30},{1,31},{2,0},{3,1},{4,2},{5,3},{6,4},{7,5},{8,6},{9,7},{10,... | collective-permute-start | bytes 608264 | tf_op jit(solution)/shard_map/ppermute | solution.py:14
  47.3 3.3 %collective-permute-done.5 = bf16[24,4224]{1,0:T(8,128)(2,1)S(1)} collective-permute-done((bf16[24,4224]{1,0:T(8,128)(2,1)S(1)}, bf16[24,4224]{1,0:T(8,128)(2,1)S(1)}, u32[]{:S(2)}, u32[]{:S(2)}) %collective-permute-start.5) | collective-permute-done | bytes 202784 | tf_op jit(solution)/shard_map/ppermute | solution.py:14
  50.7 5.1 %collective-permute-start.7 = (bf16[128,4224]{1,0:T(8,128)(2,1)S(1)}, bf16[128,4224]{1,0:T(8,128)(2,1)S(1)}, u32[]{:S(2)}, u32[]{:S(2)}) collective-permute-start(bf16[128,4224]{1,0:T(8,128)(2,1)S(1)} %constant_dynamic-update-slice_fusion), channel_id=1, source_target_pairs={{0,1},{1,0},{2,3},{3,2},{4,5},{5,4},{6,7},{7,6},{8,9},{9,8},{10,11... | collective-permute-start | bytes 3244040 | tf_op jit(solution)/shard_map/ppermute | solution.py:18
  62.1 6.7 %all-to-all-start = ((bf16[8,64,4096]{2,1,0:T(8,128)(2,1)}), bf16[8,64,4096]{2,1,0:T(8,128)(2,1)}, u32[]{:S(2)}, u32[]{:S(2)}) async-start(bf16[8,64,4096]{2,1,0:T(8,128)(2,1)} %bitcast.88), calls=%async_computation | async-start | bytes 8388608 | tf_op jit(solution)/shard_map/all_to_all | solution.py:202
  70.8 3.4 %collective-permute-start.9 = (bf16[4096,128]{1,0:T(8,128)(2,1)S(1)}, bf16[4096,128]{1,0:T(8,128)(2,1)}, u32[]{:S(2)}, u32[]{:S(2)}) collective-permute-start(bf16[4096,128]{1,0:T(8,128)(2,1)S(1)} %bitcast.93), channel_id=1, source_target_pairs={{0,128},{32,160},{64,192},{96,224},{128,0},{160,32},{192,64},{224,... | collective-permute-start | bytes 3145736 | tf_op jit(solution)/shard_map/ppermute | solution.py:22
  76.1 18.8 %collective-permute-done.8.gate_other = bf16[4096,128]{1,0:T(8,128)(2,1)} collective-permute-done((bf16[4096,128]{1,0:T(8,128)(2,1)S(1)}, bf16[4096,128]{1,0:T(8,128)(2,1)}, u32[]{:S(2)}, u32[]{:S(2)}) %collective-permute-start.8) | collective-permute-done | bytes 1048608 | tf_op jit(solution)/shard_map/ppermute | solution.py:22
  94.9 22.5 %collective-permute-done.9.up_other = bf16[4096,128]{1,0:T(8,128)(2,1)} collective-permute-done((bf16[4096,128]{1,0:T(8,128)(2,1)S(1)}, bf16[4096,128]{1,0:T(8,128)(2,1)}, u32[]{:S(2)}, u32[]{:S(2)}) %collective-permute-start.9) | collective-permute-done | bytes 1048608 | tf_op jit(solution)/shard_map/ppermute | solution.py:22
  119.7 6.7 %front.1 = bf16[4,512,256]{2,1,0:T(8,128)(2,1)} custom-call(s32[1]{0:T(128)} %bitcast.3.odd_ref, bf16[512,4096]{1,0:T(8,128)(2,1)} %bitcast.6.rows_ref, bf16[4096,128]{1,0:T(8,128)(2,1)} %bitcast.90, bf16[4096,128]{1,0:T(8,128)(2,1)} %collective-permute-done.8.gate_other, bf16[4096,128]{1,0:T(8,128)(2,1)} %bitcast.92, ...), custom_call_target="tpu_custom_call" | custom-call | tf_op jit(solution)/shard_map/front/pallas_call | solution.py:105
  126.3 13.5 %collective-permute-done.10 = bf16[1024,512]{1,0:T(8,128)(2,1)} collective-permute-done((bf16[1024,512]{1,0:T(8,128)(2,1)S(1)}, bf16[1024,512]{1,0:T(8,128)(2,1)}, u32[]{:S(2)}, u32[]{:S(2)}) %collective-permute-start.10) | collective-permute-done | bytes 1048608 | tf_op jit(solution)/shard_map/ppermute | solution.py:22
  139.8 17.6 %all_to_all.15.hidden_ref = bf16[4,512,256]{2,1,0:T(8,128)(2,1)} all-to-all(bf16[4,512,256]{2,1,0:T(8,128)(2,1)} %front.1), channel_id=1, replica_groups={{0,32,64,96},{128,160,192,224},{256,288,320,352},{384,416,448,480},{1,3..., dimensions={0} | all-to-all | bytes 2097152 | tf_op jit(solution)/shard_map/all_to_all | solution.py:207
  157.4 4.1 %back.1 = bf16[8,64,1024]{2,1,0:T(8,128)(2,1)} custom-call(s32[1]{0:T(128)} %bitcast.3.odd_ref, bf16[4,512,256]{2,1,0:T(8,128)(2,1)} %all_to_all.15.hidden_ref, bf16[2,512,512]{2,1,0:T(8,128)(2,1)} %bitcast.94, bf16[2,512,512]{2,1,0:T(8,128)(2,1)} %bitcast.11.other_ref), custom_call_target="tpu_custom_call" | custom-call | tf_op jit(solution)/shard_map/back/pallas_call | solution.py:150
  161.5 4.2 %all-to-all-start.2 = ((bf16[8,64,1024]{2,1,0:T(8,128)(2,1)}), bf16[8,64,1024]{2,1,0:T(8,128)(2,1)S(1)}, u32[]{:S(2)}, u32[]{:S(2)}) async-start(bf16[8,64,1024]{2,1,0:T(8,128)(2,1)} %back.1), calls=%async_computation.2 | async-start | bytes 2097152 | tf_op jit(solution)/shard_map/all_to_all | solution.py:211
  165.8 16.5 %all-to-all-done.2 = bf16[8,64,1024]{2,1,0:T(8,128)(2,1)S(1)} async-done(((bf16[8,64,1024]{2,1,0:T(8,128)(2,1)}), bf16[8,64,1024]{2,1,0:T(8,128)(2,1)S(1)}, u32[]{:S(2)}, u32[]{:S(2)}) %all-to-all-start.2) | async-done | bytes 1048608 | tf_op jit(solution)/shard_map/all_to_all | solution.py:211
  188.9 3.7 %collective-permute-start.15 = (bf16[24,4096]{1,0:T(8,128)(2,1)S(1)}, bf16[24,4096]{1,0:T(8,128)(2,1)S(1)}, u32[]{:S(2)}, u32[]{:S(2)}) collective-permute-start(bf16[24,4096]{1,0:T(8,128)(2,1)S(1)} %get-tuple-element.12), channel_id=1, source_target_pairs={{0,2},{1,3},{2,4},{3,5},{4,6},{5,7},{6,8},{7,9},{8,10},{9,11},{10,... | collective-permute-start | bytes 589832 | tf_op jit(solution)/shard_map/ppermute | solution.py:14
  195.4 5.0 %collective-permute-start.13 = (bf16[24,4096]{1,0:T(8,128)(2,1)S(1)}, bf16[24,4096]{1,0:T(8,128)(2,1)S(1)}, u32[]{:S(2)}, u32[]{:S(2)}) collective-permute-start(bf16[24,4096]{1,0:T(8,128)(2,1)S(1)} %get-tuple-element.14), channel_id=1, source_target_pairs={{0,4},{1,5},{2,6},{3,7},{4,8},{5,9},{6,10},{7,11},{8,12},{9,13},{1... | collective-permute-start | bytes 589832 | tf_op jit(solution)/shard_map/ppermute | solution.py:14
  202.8 4.9 %collective-permute-start.17 = (bf16[8,4096]{1,0:T(8,128)(2,1)S(1)}, bf16[8,4096]{1,0:T(8,128)(2,1)S(1)}, u32[]{:S(2)}, u32[]{:S(2)}) collective-permute-start(bf16[8,4096]{1,0:T(8,128)(2,1)S(1)} %slice.191), channel_id=1, source_target_pairs={{0,6},{1,7},{2,8},{3,9},{4,10},{5,11},{6,12},{7,13},{8,14},{9,15},... | collective-permute-start | bytes 196616 | tf_op jit(solution)/shard_map/ppermute | solution.py:14
  213.8 8.5 %collective-permute-start.18 = (bf16[8,4096]{1,0:T(8,128)(2,1)S(1)}, bf16[8,4096]{1,0:T(8,128)(2,1)S(1)}, u32[]{:S(2)}, u32[]{:S(2)}) collective-permute-start(bf16[8,4096]{1,0:T(8,128)(2,1)S(1)} %fusion.8), channel_id=1, source_target_pairs={{0,10},{1,11},{2,12},{3,13},{4,14},{5,15},{6,16},{7,17},{8,18},{9,... | collective-permute-start | bytes 196616 | tf_op jit(solution)/shard_map/ppermute | solution.py:14
  225.5 7.4 %collective-permute-done.16 = bf16[8,4096]{1,0:T(8,128)(2,1)S(1)} collective-permute-done((bf16[8,4096]{1,0:T(8,128)(2,1)S(1)}, bf16[8,4096]{1,0:T(8,128)(2,1)S(1)}, u32[]{:S(2)}, u32[]{:S(2)}) %collective-permute-start.16) | collective-permute-done | bytes 65568 | tf_op jit(solution)/shard_map/ppermute | solution.py:14
  (73 shorter events, 41.8 us)
Async XLA Ops:
  1.6 17.8 %collective-permute-start = (bf16[8,4224]{1,0:T(8,128)(2,1)}, bf16[8,4224]{1,0:T(8,128)(2,1)S(1)}, u32[]{:S(2)}, u32[]{:S(2)}) collective-permute-start(bf16[8,4224]{1,0:T(8,128)(2,1)} %with_facts.1), channel_id=1, source_target_pairs={{0,10},{1,11},{2,12},{3,13},{4,14},{5,15},{6,16},{7,17},{8,18},{9,... | collective-permute-start | bytes 202760 | tf_op jit(solution)/shard_map/ppermute | solution.py:14
  12.6 11.3 %collective-permute-start.1 = (bf16[8,4224]{1,0:T(8,128)(2,1)}, bf16[8,4224]{1,0:T(8,128)(2,1)S(1)}, u32[]{:S(2)}, u32[]{:S(2)}) collective-permute-start(bf16[8,4224]{1,0:T(8,128)(2,1)} %with_facts.1), channel_id=1, source_target_pairs={{0,22},{1,23},{2,24},{3,25},{4,26},{5,27},{6,28},{7,29},{8,30},{9,... | collective-permute-start | bytes 202760 | tf_op jit(solution)/shard_map/ppermute | solution.py:14
  24.8 14.5 %collective-permute-start.2 = (bf16[24,4224]{1,0:T(8,128)(2,1)S(1)}, bf16[24,4224]{1,0:T(8,128)(2,1)S(1)}, u32[]{:S(2)}, u32[]{:S(2)}) collective-permute-start(bf16[24,4224]{1,0:T(8,128)(2,1)S(1)} %pad_maximum_fusion.5), channel_id=1, source_target_pairs={{0,2},{1,3},{2,4},{3,5},{4,6},{5,7},{6,8},{7,9},{8,10},{9,11},{10,... | collective-permute-start | bytes 608264 | tf_op jit(solution)/shard_map/ppermute | solution.py:14
  27.4 15.3 %collective-permute-start.3 = (bf16[24,4224]{1,0:T(8,128)(2,1)S(1)}, bf16[24,4224]{1,0:T(8,128)(2,1)S(1)}, u32[]{:S(2)}, u32[]{:S(2)}) collective-permute-start(bf16[24,4224]{1,0:T(8,128)(2,1)S(1)} %pad_maximum_fusion.5), channel_id=1, source_target_pairs={{0,30},{1,31},{2,0},{3,1},{4,2},{5,3},{6,4},{7,5},{8,6},{9,7},{10,... | collective-permute-start | bytes 608264 | tf_op jit(solution)/shard_map/ppermute | solution.py:14
  31.9 18.8 %collective-permute-start.6 = (bf16[8,4224]{1,0:T(8,128)(2,1)S(1)}, bf16[8,4224]{1,0:T(8,128)(2,1)S(1)}, u32[]{:S(2)}, u32[]{:S(2)}) collective-permute-start(bf16[8,4224]{1,0:T(8,128)(2,1)S(1)} %collective-permute-done.1), channel_id=1, source_target_pairs={{0,26},{1,27},{2,28},{3,29},{4,30},{5,31},{6,0},{7,1},{8,2},{9,3},... | collective-permute-start | bytes 202760 | tf_op jit(solution)/shard_map/ppermute | solution.py:14
  39.3 8.0 %collective-permute-start.4 = (bf16[24,4224]{1,0:T(8,128)(2,1)S(1)}, bf16[24,4224]{1,0:T(8,128)(2,1)S(1)}, u32[]{:S(2)}, u32[]{:S(2)}) collective-permute-start(bf16[24,4224]{1,0:T(8,128)(2,1)S(1)} %collective-permute-done.2), channel_id=1, source_target_pairs={{0,2},{1,3},{2,4},{3,5},{4,6},{5,7},{6,8},{7,9},{8,10},{9,11},{10,... | collective-permute-start | bytes 608264 | tf_op jit(solution)/shard_map/ppermute | solution.py:14
  42.7 7.9 %collective-permute-start.5 = (bf16[24,4224]{1,0:T(8,128)(2,1)S(1)}, bf16[24,4224]{1,0:T(8,128)(2,1)S(1)}, u32[]{:S(2)}, u32[]{:S(2)}) collective-permute-start(bf16[24,4224]{1,0:T(8,128)(2,1)S(1)} %collective-permute-done.3), channel_id=1, source_target_pairs={{0,30},{1,31},{2,0},{3,1},{4,2},{5,3},{6,4},{7,5},{8,6},{9,7},{10,... | collective-permute-start | bytes 608264 | tf_op jit(solution)/shard_map/ppermute | solution.py:14
  50.7 7.5 %collective-permute-start.7 = (bf16[128,4224]{1,0:T(8,128)(2,1)S(1)}, bf16[128,4224]{1,0:T(8,128)(2,1)S(1)}, u32[]{:S(2)}, u32[]{:S(2)}) collective-permute-start(bf16[128,4224]{1,0:T(8,128)(2,1)S(1)} %constant_dynamic-update-slice_fusion), channel_id=1, source_target_pairs={{0,1},{1,0},{2,3},{3,2},{4,5},{5,4},{6,7},{7,6},{8,9},{9,8},{10,11... | collective-permute-start | bytes 3244040 | tf_op jit(solution)/shard_map/ppermute | solution.py:18
  62.1 12.1 %copy-start.2 = (bf16[1,1024,512]{2,1,0:T(8,128)(2,1)S(1)}, bf16[1,1024,512]{2,1,0:T(8,128)(2,1)}, u32[]{:S(2)}) copy-start(bf16[1,1024,512]{2,1,0:T(8,128)(2,1)} %param.12) | copy-start | bytes 3145732
  62.1 57.6 %all-to-all-start = ((bf16[8,64,4096]{2,1,0:T(8,128)(2,1)}), bf16[8,64,4096]{2,1,0:T(8,128)(2,1)}, u32[]{:S(2)}, u32[]{:S(2)}) async-start(bf16[8,64,4096]{2,1,0:T(8,128)(2,1)} %bitcast.88), calls=%async_computation | async-start | bytes 8388608 | tf_op jit(solution)/shard_map/all_to_all | solution.py:202
  68.8 26.0 %collective-permute-start.8 = (bf16[4096,128]{1,0:T(8,128)(2,1)S(1)}, bf16[4096,128]{1,0:T(8,128)(2,1)}, u32[]{:S(2)}, u32[]{:S(2)}) collective-permute-start(bf16[4096,128]{1,0:T(8,128)(2,1)S(1)} %bitcast.91), channel_id=1, source_target_pairs={{0,128},{32,160},{64,192},{96,224},{128,0},{160,32},{192,64},{224,... | collective-permute-start | bytes 3145736 | tf_op jit(solution)/shard_map/ppermute | solution.py:22
  70.8 46.6 %collective-permute-start.9 = (bf16[4096,128]{1,0:T(8,128)(2,1)S(1)}, bf16[4096,128]{1,0:T(8,128)(2,1)}, u32[]{:S(2)}, u32[]{:S(2)}) collective-permute-start(bf16[4096,128]{1,0:T(8,128)(2,1)S(1)} %bitcast.93), channel_id=1, source_target_pairs={{0,128},{32,160},{64,192},{96,224},{128,0},{160,32},{192,64},{224,... | collective-permute-start | bytes 3145736 | tf_op jit(solution)/shard_map/ppermute | solution.py:22
  74.1 65.7 %collective-permute-start.10 = (bf16[1024,512]{1,0:T(8,128)(2,1)S(1)}, bf16[1024,512]{1,0:T(8,128)(2,1)}, u32[]{:S(2)}, u32[]{:S(2)}) collective-permute-start(bf16[1024,512]{1,0:T(8,128)(2,1)S(1)} %bitcast.95), channel_id=1, source_target_pairs={{0,128},{32,160},{64,192},{96,224},{128,0},{160,32},{192,64},{224,... | collective-permute-start | bytes 3145736 | tf_op jit(solution)/shard_map/ppermute | solution.py:22
  161.5 20.8 %all-to-all-start.2 = ((bf16[8,64,1024]{2,1,0:T(8,128)(2,1)}), bf16[8,64,1024]{2,1,0:T(8,128)(2,1)S(1)}, u32[]{:S(2)}, u32[]{:S(2)}) async-start(bf16[8,64,1024]{2,1,0:T(8,128)(2,1)} %back.1), calls=%async_computation.2 | async-start | bytes 2097152 | tf_op jit(solution)/shard_map/all_to_all | solution.py:211
  182.9 5.4 %collective-permute-start.11 = (bf16[128,4096]{1,0:T(8,128)(2,1)S(1)}, bf16[128,4096]{1,0:T(8,128)(2,1)S(1)}, u32[]{:S(2)}, u32[]{:S(2)}) collective-permute-start(bf16[128,4096]{1,0:T(8,128)(2,1)S(1)} %convolution_convert_fusion), channel_id=1, source_target_pairs={{0,1},{1,0},{2,3},{3,2},{4,5},{5,4},{6,7},{7,6},{8,9},{9,8},{10,11... | collective-permute-start | bytes 3145736 | tf_op jit(solution)/shard_map/ppermute | solution.py:18
  188.8 44.0 %copy-start.3 = (bf16[8,4096]{1,0:T(8,128)(2,1)S(1)}, bf16[8,4096]{1,0:T(8,128)(2,1)}, u32[]{:S(2)}) copy-start(bf16[8,4096]{1,0:T(8,128)(2,1)} %tokens_ref.1) | copy-start | bytes 196612
  188.8 44.2 %copy-start.4 = (f32[4096]{0:T(1024)S(1)}, f32[4096]{0:T(1024)}, u32[]{:S(2)}) copy-start(f32[4096]{0:T(1024)} %param.13) | copy-start | bytes 49156
  188.9 18.9 %collective-permute-start.15 = (bf16[24,4096]{1,0:T(8,128)(2,1)S(1)}, bf16[24,4096]{1,0:T(8,128)(2,1)S(1)}, u32[]{:S(2)}, u32[]{:S(2)}) collective-permute-start(bf16[24,4096]{1,0:T(8,128)(2,1)S(1)} %get-tuple-element.12), channel_id=1, source_target_pairs={{0,2},{1,3},{2,4},{3,5},{4,6},{5,7},{6,8},{7,9},{8,10},{9,11},{10,... | collective-permute-start | bytes 589832 | tf_op jit(solution)/shard_map/ppermute | solution.py:14
  192.6 15.2 %collective-permute-start.14 = (bf16[24,4096]{1,0:T(8,128)(2,1)S(1)}, bf16[24,4096]{1,0:T(8,128)(2,1)S(1)}, u32[]{:S(2)}, u32[]{:S(2)}) collective-permute-start(bf16[24,4096]{1,0:T(8,128)(2,1)S(1)} %get-tuple-element.13), channel_id=1, source_target_pairs={{0,30},{1,31},{2,0},{3,1},{4,2},{5,3},{6,4},{7,5},{8,6},{9,7},{10,... | collective-permute-start | bytes 589832 | tf_op jit(solution)/shard_map/ppermute | solution.py:14
  195.4 14.9 %collective-permute-start.13 = (bf16[24,4096]{1,0:T(8,128)(2,1)S(1)}, bf16[24,4096]{1,0:T(8,128)(2,1)S(1)}, u32[]{:S(2)}, u32[]{:S(2)}) collective-permute-start(bf16[24,4096]{1,0:T(8,128)(2,1)S(1)} %get-tuple-element.14), channel_id=1, source_target_pairs={{0,4},{1,5},{2,6},{3,7},{4,8},{5,9},{6,10},{7,11},{8,12},{9,13},{1... | collective-permute-start | bytes 589832 | tf_op jit(solution)/shard_map/ppermute | solution.py:14
  200.4 12.8 %collective-permute-start.12 = (bf16[24,4096]{1,0:T(8,128)(2,1)S(1)}, bf16[24,4096]{1,0:T(8,128)(2,1)S(1)}, u32[]{:S(2)}, u32[]{:S(2)}) collective-permute-start(bf16[24,4096]{1,0:T(8,128)(2,1)S(1)} %get-tuple-element.11), channel_id=1, source_target_pairs={{0,28},{1,29},{2,30},{3,31},{4,0},{5,1},{6,2},{7,3},{8,4},{9,5},{1... | collective-permute-start | bytes 589832 | tf_op jit(solution)/shard_map/ppermute | solution.py:14
  202.8 10.9 %collective-permute-start.17 = (bf16[8,4096]{1,0:T(8,128)(2,1)S(1)}, bf16[8,4096]{1,0:T(8,128)(2,1)S(1)}, u32[]{:S(2)}, u32[]{:S(2)}) collective-permute-start(bf16[8,4096]{1,0:T(8,128)(2,1)S(1)} %slice.191), channel_id=1, source_target_pairs={{0,6},{1,7},{2,8},{3,9},{4,10},{5,11},{6,12},{7,13},{8,14},{9,15},... | collective-permute-start | bytes 196616 | tf_op jit(solution)/shard_map/ppermute | solution.py:14
  213.8 11.7 %collective-permute-start.18 = (bf16[8,4096]{1,0:T(8,128)(2,1)S(1)}, bf16[8,4096]{1,0:T(8,128)(2,1)S(1)}, u32[]{:S(2)}, u32[]{:S(2)}) collective-permute-start(bf16[8,4096]{1,0:T(8,128)(2,1)S(1)} %fusion.8), channel_id=1, source_target_pairs={{0,10},{1,11},{2,12},{3,13},{4,14},{5,15},{6,16},{7,17},{8,18},{9,... | collective-permute-start | bytes 196616 | tf_op jit(solution)/shard_map/ppermute | solution.py:14
  222.3 10.5 %collective-permute-start.16 = (bf16[8,4096]{1,0:T(8,128)(2,1)S(1)}, bf16[8,4096]{1,0:T(8,128)(2,1)S(1)}, u32[]{:S(2)}, u32[]{:S(2)}) collective-permute-start(bf16[8,4096]{1,0:T(8,128)(2,1)S(1)} %slice.292), channel_id=1, source_target_pairs={{0,22},{1,23},{2,24},{3,25},{4,26},{5,27},{6,28},{7,29},{8,30},{9,... | collective-permute-start | bytes 196616 | tf_op jit(solution)/shard_map/ppermute | solution.py:14
  (2 other events, 15.4 us)

commit v5 on v4

--- a/solution.py
+++ b/solution.py
@@ -19,11 +19,11 @@
 
 
 def pair_swap(block):
-    return lax.ppermute(block, "grp", [(i, i ^ 4) for i in range(lax.axis_size("grp"))])
-
-
-EIGHTS = [[0, 1, 2, 3, 12, 13, 14, 15], [4, 5, 6, 7, 8, 9, 10, 11]]
-FOURS = [[4 * y + x for x in range(4)] for y in range(4)]
+    return lax.ppermute(block, "grp", [(i, i ^ 1) for i in range(lax.axis_size("grp"))])
+
+
+EIGHTS = [[4 * y + x for y in range(4) for x in pair] for pair in ((0, 3), (1, 2))]
+FOURS = [group[at:at + 4] for group in EIGHTS for at in (0, 4)]
 
 
 def gather_column(block):
@@ -120,8 +120,7 @@
 def back(odd, hidden, own, other, slots):
     parts, count, units = hidden.shape
     features = own.shape[1]
-    half, steps = units // 2, parts // 2
-    own, other = (w.reshape(2, own.shape[0] // 2, features) for w in (own, other))
+    steps = parts // 2
 
     def kernel(odd_ref, hidden_ref, own_ref, other_ref, out_ref, total):
         k = pl.program_id(0)
@@ -130,12 +129,9 @@
         def _():
             total[...] = jnp.zeros_like(total)
 
-        weights = [
-            jnp.concatenate([w[at, j * half:(j + 1) * half] for j in range(2) for at in range(2)], 0)
-            for w in (own_ref, other_ref)
-        ]
         rows = jnp.concatenate([hidden_ref[0], hidden_ref[1]], 1)
-        total[...] += jnp.dot(rows, jnp.concatenate(weights, 1), preferred_element_type=F32)
+        weights = jnp.concatenate([own_ref[...], other_ref[...]], 1)
+        total[...] += jnp.dot(rows, weights, preferred_element_type=F32)
 
         @pl.when(k == steps - 1)
         def _():
@@ -145,7 +141,7 @@
             out_ref[:, :, :features] = jnp.where(swap, high, low).astype(BF16).reshape(shape)
             out_ref[:, :, features:] = jnp.where(swap, low, high).astype(BF16).reshape(shape)
 
-    weight = pl.BlockSpec((2, 2 * half, features), lambda k: (0, k, 0))
+    weight = pl.BlockSpec((2 * units, features), lambda k: (k, 0))
     out = (count // slots, slots, 2 * features)
     return pl.pallas_call(
         kernel,
@@ -167,12 +163,13 @@
     top = expert_ids.shape[1]
     g = lax.axis_index("grp")
     p = lax.axis_index("ep")
-    odd = (g // 4 % 2).astype(jnp.int32).reshape(1)
+    odd = (g % 2).astype(jnp.int32).reshape(1)
 
     gate_own, up_own, down_own = w_gate[0], w_up[0], w_down[0]
     gate_other, up_other, down_other = pair_swap(gate_own), pair_swap(up_own), pair_swap(down_own)
 
     column = gather_column(with_facts(tokens, expert_ids, gate_weights))
+    column, gate_other = lax.optimization_barrier((column, gate_other))
     parts = column, core_swap(column)
     half = parts[0].shape[0]
     rows = 2 * half
@@ -206,18 +203,9 @@
     hidden, down_other = lax.optimization_barrier((hidden, down_other))
     hidden = lax.all_to_all(hidden, "grp", split_axis=0, concat_axis=0, tiled=True, axis_index_groups=FOURS)
 
-    features = down_own.shape[1]
     out = back(odd, hidden, down_own, down_other, slots)
     home = lax.all_to_all(out, "grp", split_axis=0, concat_axis=0, tiled=True, axis_index_groups=EIGHTS)
-    home = jnp.concatenate(
-        [
-            jnp.concatenate(
-                [home[4 * of + x, :, features * at:features * (at + 1)] for at in range(2) for x in range(4)], 1
-            )
-            for of in range(2)
-        ],
-        0,
-    )
+    home = jnp.concatenate([jnp.concatenate(list(home[at:at + 4]), 1) for at in (0, 4)], 0)
 
     def weight(at):
         summed = jnp.sum(jnp.where(match, facts[at][None], 0.0), axis=1)

time: 236 us -> 262 us (1.11)
  other arithmetic: 2.3 us -> 43.4 us
  waiting for transfers between devices: 101 us -> 82.6 us
  starting transfers between devices: 94.2 us -> 97.4 us
    concatenate x0 -> x1, other arithmetic: none -> 41.1 us  [shards(): home = jnp.concatenate([home, home], 0)]
    ppermute x3, waiting for transfers between devices: 54.7 us -> 20.7 us  [pair_swap(): lax.ppermute(block, 'grp', [(i, i ^ 1) for i in range(lax.axis_size('grp'...]
    all_to_all x1, waiting for transfers between devices: 2.35 us -> 24.1 us  [shards(): lax.all_to_all(fanned, 'grp', split_axis=0, concat_axis=0, tiled=True, ax...]
    ppermute x14, waiting for transfers between devices: 22.9 us -> 19.8 us  [around(): lax.ppermute(block, 'ep', [(i, (i + 2 * chips) % size) for i in range(siz...]
    all_to_all x1, waiting for transfers between devices: 16.5 us -> 13.6 us  [shards(): lax.all_to_all(out, 'grp', split_axis=0, concat_axis=0, tiled=True, axis_...]
  transfers between devices with their start and end apart: 21 -> 21, of which waited for: 15 -> 13; matrix products, arithmetic and copies ran while one was open for 1% -> 1% of each run, Pallas kernels for 3% -> 3%
where the time goes in v5:
time: 262 us; the launch traced here: 260 us
  starting transfers between devices  97.4 us (37%)
  waiting for transfers between devices  82.6 us (32%)
  other arithmetic  43.4 us (17%)
  blocking collectives  17.7 us (7%)
  Pallas kernels  12.3 us (5%)
  local copies, waits for them, and re-layouts  3.8 us (1%)
    ppermute x14, starting transfers between devices, around(): lax.ppermute(block, 'ep', [(i, (i + 2 * chips) % size) for i in range(siz...  67.8 us
    concatenate x1, other arithmetic, shards(): home = jnp.concatenate([home, home], 0)  41.1 us
    all_to_all x1, waiting for transfers between devices, shards(): lax.all_to_all(fanned, 'grp', split_axis=0, concat_axis=0, tiled=True, ax...  24.1 us
    ppermute x3, waiting for transfers between devices, pair_swap(): lax.ppermute(block, 'grp', [(i, i ^ 1) for i in range(lax.axis_size('grp'...  20.7 us
    ppermute x14, waiting for transfers between devices, around(): lax.ppermute(block, 'ep', [(i, (i + 2 * chips) % size) for i in range(siz...  19.8 us
    all_to_all x1, blocking collectives, shards(): lax.all_to_all(hidden, 'grp', split_axis=0, concat_axis=0, tiled=True, ax...  17.7 us
    all_to_all x1, waiting for transfers between devices, shards(): lax.all_to_all(out, 'grp', split_axis=0, concat_axis=0, tiled=True, axis_...  13.6 us
    ppermute x2, starting transfers between devices, core_swap(): lax.ppermute(block, 'ep', [(i, i ^ 1) for i in range(lax.axis_size('ep'))])  10.9 us
  transfers between devices with their start and end apart: 21, of which 13 were waited for; matrix products, arithmetic and copies ran while one was open for 1% of the time, Pallas kernels for 3%

profile of v5, /device:TPU:1, one launch (start us, length us, event | category | flops | bytes accessed | tf_op | source)
XLA Modules:
  0.0 259.9 jit_solution(10974158896113042288)
XLA Ops:
  1.6 11.0 %collective-permute-start = (bf16[8,4224]{1,0:T(8,128)(2,1)}, bf16[8,4224]{1,0:T(8,128)(2,1)S(1)}, u32[]{:S(2)}, u32[]{:S(2)}) collective-permute-start(bf16[8,4224]{1,0:T(8,128)(2,1)} %with_facts.1), channel_id=1, source_target_pairs={{0,10},{1,11},{2,12},{3,13},{4,14},{5,15},{6,16},{7,17},{8,18},{9,... | collective-permute-start | bytes 202760 | tf_op jit(solution)/shard_map/ppermute | solution.py:14
  12.6 5.9 %collective-permute-start.1 = (bf16[8,4224]{1,0:T(8,128)(2,1)}, bf16[8,4224]{1,0:T(8,128)(2,1)S(1)}, u32[]{:S(2)}, u32[]{:S(2)}) collective-permute-start(bf16[8,4224]{1,0:T(8,128)(2,1)} %with_facts.1), channel_id=1, source_target_pairs={{0,22},{1,23},{2,24},{3,25},{4,26},{5,27},{6,28},{7,29},{8,30},{9,... | collective-permute-start | bytes 202760 | tf_op jit(solution)/shard_map/ppermute | solution.py:14
  27.4 4.5 %collective-permute-start.3 = (bf16[24,4224]{1,0:T(8,128)(2,1)S(1)}, bf16[24,4224]{1,0:T(8,128)(2,1)S(1)}, u32[]{:S(2)}, u32[]{:S(2)}) collective-permute-start(bf16[24,4224]{1,0:T(8,128)(2,1)S(1)} %pad_maximum_fusion), channel_id=1, source_target_pairs={{0,30},{1,31},{2,0},{3,1},{4,2},{5,3},{6,4},{7,5},{8,6},{9,7},{10,... | collective-permute-start | bytes 608264 | tf_op jit(solution)/shard_map/ppermute | solution.py:14
  31.9 7.4 %collective-permute-start.6 = (bf16[8,4224]{1,0:T(8,128)(2,1)S(1)}, bf16[8,4224]{1,0:T(8,128)(2,1)S(1)}, u32[]{:S(2)}, u32[]{:S(2)}) collective-permute-start(bf16[8,4224]{1,0:T(8,128)(2,1)S(1)} %collective-permute-done.1), channel_id=1, source_target_pairs={{0,26},{1,27},{2,28},{3,29},{4,30},{5,31},{6,0},{7,1},{8,2},{9,3},... | collective-permute-start | bytes 202760 | tf_op jit(solution)/shard_map/ppermute | solution.py:14
  39.3 3.4 %collective-permute-start.4 = (bf16[24,4224]{1,0:T(8,128)(2,1)S(1)}, bf16[24,4224]{1,0:T(8,128)(2,1)S(1)}, u32[]{:S(2)}, u32[]{:S(2)}) collective-permute-start(bf16[24,4224]{1,0:T(8,128)(2,1)S(1)} %collective-permute-done.2), channel_id=1, source_target_pairs={{0,2},{1,3},{2,4},{3,5},{4,6},{5,7},{6,8},{7,9},{8,10},{9,11},{10,... | collective-permute-start | bytes 608264 | tf_op jit(solution)/shard_map/ppermute | solution.py:14
  42.7 3.1 %collective-permute-start.5 = (bf16[24,4224]{1,0:T(8,128)(2,1)S(1)}, bf16[24,4224]{1,0:T(8,128)(2,1)S(1)}, u32[]{:S(2)}, u32[]{:S(2)}) collective-permute-start(bf16[24,4224]{1,0:T(8,128)(2,1)S(1)} %collective-permute-done.3), channel_id=1, source_target_pairs={{0,30},{1,31},{2,0},{3,1},{4,2},{5,3},{6,4},{7,5},{8,6},{9,7},{10,... | collective-permute-start | bytes 608264 | tf_op jit(solution)/shard_map/ppermute | solution.py:14
  47.3 3.3 %collective-permute-done.5 = bf16[24,4224]{1,0:T(8,128)(2,1)S(1)} collective-permute-done((bf16[24,4224]{1,0:T(8,128)(2,1)S(1)}, bf16[24,4224]{1,0:T(8,128)(2,1)S(1)}, u32[]{:S(2)}, u32[]{:S(2)}) %collective-permute-start.5) | collective-permute-done | bytes 202784 | tf_op jit(solution)/shard_map/ppermute | solution.py:14
  50.7 5.1 %collective-permute-start.8 = (bf16[128,4224]{1,0:T(8,128)(2,1)S(1)}, bf16[128,4224]{1,0:T(8,128)(2,1)S(1)}, u32[]{:S(2)}, u32[]{:S(2)}) collective-permute-start(bf16[128,4224]{1,0:T(8,128)(2,1)S(1)} %constant_dynamic-update-slice_fusion), channel_id=1, source_target_pairs={{0,1},{1,0},{2,3},{3,2},{4,5},{5,4},{6,7},{7,6},{8,9},{9,8},{10,11... | collective-permute-start | bytes 3244040 | tf_op jit(solution)/shard_map/ppermute | solution.py:18
  62.1 6.5 %all-to-all-start = ((bf16[8,64,4096]{2,1,0:T(8,128)(2,1)}), bf16[8,64,4096]{2,1,0:T(8,128)(2,1)}, u32[]{:S(2)}, u32[]{:S(2)}) async-start(bf16[8,64,4096]{2,1,0:T(8,128)(2,1)} %bitcast.40), calls=%async_computation | async-start | bytes 8388608 | tf_op jit(solution)/shard_map/all_to_all | solution.py:199
  70.5 3.4 %collective-permute-start.10 = (bf16[1024,512]{1,0:T(8,128)(2,1)S(1)}, bf16[1024,512]{1,0:T(8,128)(2,1)S(1)}, u32[]{:S(2)}, u32[]{:S(2)}) collective-permute-start(bf16[1024,512]{1,0:T(8,128)(2,1)S(1)} %bitcast.47), channel_id=1, source_target_pairs={{0,32},{32,0},{64,96},{96,64},{128,160},{160,128},{192,224},{224,1... | collective-permute-start | bytes 3145736 | tf_op jit(solution)/shard_map/ppermute | solution.py:22
  73.9 20.7 %collective-permute-done.9.up_other = bf16[4096,128]{1,0:T(8,128)(2,1)} collective-permute-done((bf16[4096,128]{1,0:T(8,128)(2,1)S(1)}, bf16[4096,128]{1,0:T(8,128)(2,1)}, u32[]{:S(2)}, u32[]{:S(2)}) %collective-permute-start.9) | collective-permute-done | bytes 1048608 | tf_op jit(solution)/shard_map/ppermute | solution.py:22
  94.7 24.1 %all-to-all-done = bf16[8,64,4096]{2,1,0:T(8,128)(2,1)} async-done(((bf16[8,64,4096]{2,1,0:T(8,128)(2,1)}), bf16[8,64,4096]{2,1,0:T(8,128)(2,1)}, u32[]{:S(2)}, u32[]{:S(2)}) %all-to-all-start) | async-done | bytes 4194336 | tf_op jit(solution)/shard_map/all_to_all | solution.py:199
  118.8 6.6 %front.1 = bf16[4,512,256]{2,1,0:T(8,128)(2,1)} custom-call(s32[1]{0:T(128)} %bitcast.4.odd_ref, bf16[512,4096]{1,0:T(8,128)(2,1)} %bitcast.7.rows_ref, bf16[4096,128]{1,0:T(8,128)(2,1)} %bitcast.43, bf16[4096,128]{1,0:T(8,128)(2,1)} %copy-done.2, bf16[4096,128]{1,0:T(8,128)(2,1)} %bitcast.44, bf16[4096,128]{1,0:T(8,128)(2,1)} %collective-permute-done.9.up_other), custom_call_target="tpu_custom_call" | custom-call | tf_op jit(solution)/shard_map/front/pallas_call | solution.py:105
  125.4 17.7 %all_to_all.15.hidden_ref = bf16[4,512,256]{2,1,0:T(8,128)(2,1)} all-to-all(bf16[4,512,256]{2,1,0:T(8,128)(2,1)} %front.1), channel_id=1, replica_groups={{0,96,128,224},{256,352,384,480},{32,64,160,192},{288,320,416,448},{1,9..., dimensions={0} | all-to-all | bytes 2097152 | tf_op jit(solution)/shard_map/all_to_all | solution.py:204
  143.1 4.1 %back.1 = bf16[8,64,1024]{2,1,0:T(8,128)(2,1)} custom-call(s32[1]{0:T(128)} %bitcast.4.odd_ref, bf16[4,512,256]{2,1,0:T(8,128)(2,1)} %all_to_all.15.hidden_ref, bf16[1024,512]{1,0:T(8,128)(2,1)} %bitcast.46, bf16[1024,512]{1,0:T(8,128)(2,1)} %copy-done.3), custom_call_target="tpu_custom_call" | custom-call | tf_op jit(solution)/shard_map/back/pallas_call | solution.py:146
  147.2 3.7 %all-to-all-start.2 = ((bf16[8,64,1024]{2,1,0:T(8,128)(2,1)}), bf16[8,64,1024]{2,1,0:T(8,128)(2,1)S(1)}, u32[]{:S(2)}, u32[]{:S(2)}) async-start(bf16[8,64,1024]{2,1,0:T(8,128)(2,1)} %back.1), calls=%async_computation.2 | async-start | bytes 2097152 | tf_op jit(solution)/shard_map/all_to_all | solution.py:207
  151.2 13.6 %all-to-all-done.2 = bf16[8,64,1024]{2,1,0:T(8,128)(2,1)S(1)} async-done(((bf16[8,64,1024]{2,1,0:T(8,128)(2,1)}), bf16[8,64,1024]{2,1,0:T(8,128)(2,1)S(1)}, u32[]{:S(2)}, u32[]{:S(2)}) %all-to-all-start.2) | async-done | bytes 1048608 | tf_op jit(solution)/shard_map/all_to_all | solution.py:207
  164.8 41.1 %maximum_maximum_fusion = bf16[256,4096]{1,0:T(8,128)(2,1)S(1)} fusion(bf16[64,1024]{1,0:T(8,128)(2,1)S(1)} %get-tuple-element.20, bf16[64,1024]{1,0:T(8,128)(2,1)S(1)} %get-tuple-element.21, bf16[64,1024]{1,0:T(8,128)(2,1)S(1)} %get-tuple-element.22, bf16[64,1024]{1,0:T(8,128)(2,1)S(1)} %get-tuple-element.23, bf16[64,1024]{1,0:T(8,128)(2,1)S(1)} %get-tuple-element.24, ...), kind=kLoop, calls=%fused_computation.3 | loop fusion | flops 33554432 | bytes 3145728 | tf_op jit(solution)/shard_map/concatenate | solution.py:216
  206.4 5.7 %collective-permute-start.11 = (bf16[128,4096]{1,0:T(8,128)(2,1)S(1)}, bf16[128,4096]{1,0:T(8,128)(2,1)S(1)}, u32[]{:S(2)}, u32[]{:S(2)}) collective-permute-start(bf16[128,4096]{1,0:T(8,128)(2,1)S(1)} %convolution_convert_fusion), channel_id=1, source_target_pairs={{0,1},{1,0},{2,3},{3,2},{4,5},{5,4},{6,7},{7,6},{8,9},{9,8},{10,11... | collective-permute-start | bytes 3145736 | tf_op jit(solution)/shard_map/ppermute | solution.py:18
  215.0 3.6 %collective-permute-start.15 = (bf16[24,4096]{1,0:T(8,128)(2,1)S(1)}, bf16[24,4096]{1,0:T(8,128)(2,1)S(1)}, u32[]{:S(2)}, u32[]{:S(2)}) collective-permute-start(bf16[24,4096]{1,0:T(8,128)(2,1)S(1)} %get-tuple-element.16), channel_id=1, source_target_pairs={{0,2},{1,3},{2,4},{3,5},{4,6},{5,7},{6,8},{7,9},{8,10},{9,11},{10,... | collective-permute-start | bytes 589832 | tf_op jit(solution)/shard_map/ppermute | solution.py:14
  221.5 4.9 %collective-permute-start.13 = (bf16[24,4096]{1,0:T(8,128)(2,1)S(1)}, bf16[24,4096]{1,0:T(8,128)(2,1)S(1)}, u32[]{:S(2)}, u32[]{:S(2)}) collective-permute-start(bf16[24,4096]{1,0:T(8,128)(2,1)S(1)} %get-tuple-element.18), channel_id=1, source_target_pairs={{0,4},{1,5},{2,6},{3,7},{4,8},{5,9},{6,10},{7,11},{8,12},{9,13},{1... | collective-permute-start | bytes 589832 | tf_op jit(solution)/shard_map/ppermute | solution.py:14
  229.0 4.9 %collective-permute-start.17 = (bf16[8,4096]{1,0:T(8,128)(2,1)S(1)}, bf16[8,4096]{1,0:T(8,128)(2,1)S(1)}, u32[]{:S(2)}, u32[]{:S(2)}) collective-permute-start(bf16[8,4096]{1,0:T(8,128)(2,1)S(1)} %slice.119), channel_id=1, source_target_pairs={{0,6},{1,7},{2,8},{3,9},{4,10},{5,11},{6,12},{7,13},{8,14},{9,15},... | collective-permute-start | bytes 196616 | tf_op jit(solution)/shard_map/ppermute | solution.py:14
  239.9 8.6 %collective-permute-start.18 = (bf16[8,4096]{1,0:T(8,128)(2,1)S(1)}, bf16[8,4096]{1,0:T(8,128)(2,1)S(1)}, u32[]{:S(2)}, u32[]{:S(2)}) collective-permute-start(bf16[8,4096]{1,0:T(8,128)(2,1)S(1)} %fusion.7), channel_id=1, source_target_pairs={{0,10},{1,11},{2,12},{3,13},{4,14},{5,15},{6,16},{7,17},{8,18},{9,... | collective-permute-start | bytes 196616 | tf_op jit(solution)/shard_map/ppermute | solution.py:14
  251.3 7.7 %collective-permute-done.16 = bf16[8,4096]{1,0:T(8,128)(2,1)S(1)} collective-permute-done((bf16[8,4096]{1,0:T(8,128)(2,1)S(1)}, bf16[8,4096]{1,0:T(8,128)(2,1)S(1)}, u32[]{:S(2)}, u32[]{:S(2)}) %collective-permute-start.16) | collective-permute-done | bytes 65568 | tf_op jit(solution)/shard_map/ppermute | solution.py:14
  (69 shorter events, 38.7 us)
Async XLA Ops:
  1.6 20.9 %collective-permute-start = (bf16[8,4224]{1,0:T(8,128)(2,1)}, bf16[8,4224]{1,0:T(8,128)(2,1)S(1)}, u32[]{:S(2)}, u32[]{:S(2)}) collective-permute-start(bf16[8,4224]{1,0:T(8,128)(2,1)} %with_facts.1), channel_id=1, source_target_pairs={{0,10},{1,11},{2,12},{3,13},{4,14},{5,15},{6,16},{7,17},{8,18},{9,... | collective-permute-start | bytes 202760 | tf_op jit(solution)/shard_map/ppermute | solution.py:14
  12.6 11.3 %collective-permute-start.1 = (bf16[8,4224]{1,0:T(8,128)(2,1)}, bf16[8,4224]{1,0:T(8,128)(2,1)S(1)}, u32[]{:S(2)}, u32[]{:S(2)}) collective-permute-start(bf16[8,4224]{1,0:T(8,128)(2,1)} %with_facts.1), channel_id=1, source_target_pairs={{0,22},{1,23},{2,24},{3,25},{4,26},{5,27},{6,28},{7,29},{8,30},{9,... | collective-permute-start | bytes 202760 | tf_op jit(solution)/shard_map/ppermute | solution.py:14
  18.5 32.2 %collective-permute-start.7 = (bf16[4096,128]{1,0:T(8,128)(2,1)}, bf16[4096,128]{1,0:T(8,128)(2,1)S(1)}, u32[]{:S(2)}, u32[]{:S(2)}) collective-permute-start(bf16[4096,128]{1,0:T(8,128)(2,1)} %bitcast.42), channel_id=1, source_target_pairs={{0,32},{32,0},{64,96},{96,64},{128,160},{160,128},{192,224},{224,1... | collective-permute-start | bytes 3145736 | tf_op jit(solution)/shard_map/ppermute | solution.py:22
  24.8 14.5 %collective-permute-start.2 = (bf16[24,4224]{1,0:T(8,128)(2,1)S(1)}, bf16[24,4224]{1,0:T(8,128)(2,1)S(1)}, u32[]{:S(2)}, u32[]{:S(2)}) collective-permute-start(bf16[24,4224]{1,0:T(8,128)(2,1)S(1)} %pad_maximum_fusion), channel_id=1, source_target_pairs={{0,2},{1,3},{2,4},{3,5},{4,6},{5,7},{6,8},{7,9},{8,10},{9,11},{10,... | collective-permute-start | bytes 608264 | tf_op jit(solution)/shard_map/ppermute | solution.py:14
  27.4 15.3 %collective-permute-start.3 = (bf16[24,4224]{1,0:T(8,128)(2,1)S(1)}, bf16[24,4224]{1,0:T(8,128)(2,1)S(1)}, u32[]{:S(2)}, u32[]{:S(2)}) collective-permute-start(bf16[24,4224]{1,0:T(8,128)(2,1)S(1)} %pad_maximum_fusion), channel_id=1, source_target_pairs={{0,30},{1,31},{2,0},{3,1},{4,2},{5,3},{6,4},{7,5},{8,6},{9,7},{10,... | collective-permute-start | bytes 608264 | tf_op jit(solution)/shard_map/ppermute | solution.py:14
  31.9 18.8 %collective-permute-start.6 = (bf16[8,4224]{1,0:T(8,128)(2,1)S(1)}, bf16[8,4224]{1,0:T(8,128)(2,1)S(1)}, u32[]{:S(2)}, u32[]{:S(2)}) collective-permute-start(bf16[8,4224]{1,0:T(8,128)(2,1)S(1)} %collective-permute-done.1), channel_id=1, source_target_pairs={{0,26},{1,27},{2,28},{3,29},{4,30},{5,31},{6,0},{7,1},{8,2},{9,3},... | collective-permute-start | bytes 202760 | tf_op jit(solution)/shard_map/ppermute | solution.py:14
  39.3 8.0 %collective-permute-start.4 = (bf16[24,4224]{1,0:T(8,128)(2,1)S(1)}, bf16[24,4224]{1,0:T(8,128)(2,1)S(1)}, u32[]{:S(2)}, u32[]{:S(2)}) collective-permute-start(bf16[24,4224]{1,0:T(8,128)(2,1)S(1)} %collective-permute-done.2), channel_id=1, source_target_pairs={{0,2},{1,3},{2,4},{3,5},{4,6},{5,7},{6,8},{7,9},{8,10},{9,11},{10,... | collective-permute-start | bytes 608264 | tf_op jit(solution)/shard_map/ppermute | solution.py:14
  42.7 7.9 %collective-permute-start.5 = (bf16[24,4224]{1,0:T(8,128)(2,1)S(1)}, bf16[24,4224]{1,0:T(8,128)(2,1)S(1)}, u32[]{:S(2)}, u32[]{:S(2)}) collective-permute-start(bf16[24,4224]{1,0:T(8,128)(2,1)S(1)} %collective-permute-done.3), channel_id=1, source_target_pairs={{0,30},{1,31},{2,0},{3,1},{4,2},{5,3},{6,4},{7,5},{8,6},{9,7},{10,... | collective-permute-start | bytes 608264 | tf_op jit(solution)/shard_map/ppermute | solution.py:14
  50.7 7.5 %collective-permute-start.8 = (bf16[128,4224]{1,0:T(8,128)(2,1)S(1)}, bf16[128,4224]{1,0:T(8,128)(2,1)S(1)}, u32[]{:S(2)}, u32[]{:S(2)}) collective-permute-start(bf16[128,4224]{1,0:T(8,128)(2,1)S(1)} %constant_dynamic-update-slice_fusion), channel_id=1, source_target_pairs={{0,1},{1,0},{2,3},{3,2},{4,5},{5,4},{6,7},{7,6},{8,9},{9,8},{10,11... | collective-permute-start | bytes 3244040 | tf_op jit(solution)/shard_map/ppermute | solution.py:18
  62.1 56.7 %all-to-all-start = ((bf16[8,64,4096]{2,1,0:T(8,128)(2,1)}), bf16[8,64,4096]{2,1,0:T(8,128)(2,1)}, u32[]{:S(2)}, u32[]{:S(2)}) async-start(bf16[8,64,4096]{2,1,0:T(8,128)(2,1)} %bitcast.40), calls=%async_computation | async-start | bytes 8388608 | tf_op jit(solution)/shard_map/all_to_all | solution.py:199
  68.6 26.0 %collective-permute-start.9 = (bf16[4096,128]{1,0:T(8,128)(2,1)S(1)}, bf16[4096,128]{1,0:T(8,128)(2,1)}, u32[]{:S(2)}, u32[]{:S(2)}) collective-permute-start(bf16[4096,128]{1,0:T(8,128)(2,1)S(1)} %bitcast.45), channel_id=1, source_target_pairs={{0,32},{32,0},{64,96},{96,64},{128,160},{160,128},{192,224},{224,1... | collective-permute-start | bytes 3145736 | tf_op jit(solution)/shard_map/ppermute | solution.py:22
  70.5 54.9 %collective-permute-start.10 = (bf16[1024,512]{1,0:T(8,128)(2,1)S(1)}, bf16[1024,512]{1,0:T(8,128)(2,1)S(1)}, u32[]{:S(2)}, u32[]{:S(2)}) collective-permute-start(bf16[1024,512]{1,0:T(8,128)(2,1)S(1)} %bitcast.47), channel_id=1, source_target_pairs={{0,32},{32,0},{64,96},{96,64},{128,160},{160,128},{192,224},{224,1... | collective-permute-start | bytes 3145736 | tf_op jit(solution)/shard_map/ppermute | solution.py:22
  125.4 17.7 %copy-start.3 = (bf16[1024,512]{1,0:T(8,128)(2,1)}, bf16[1024,512]{1,0:T(8,128)(2,1)S(1)}, u32[]{:S(2)}) copy-start(bf16[1024,512]{1,0:T(8,128)(2,1)S(1)} %collective-permute-done.10.other_ref) | copy-start | bytes 3145732
  147.2 17.5 %all-to-all-start.2 = ((bf16[8,64,1024]{2,1,0:T(8,128)(2,1)}), bf16[8,64,1024]{2,1,0:T(8,128)(2,1)S(1)}, u32[]{:S(2)}, u32[]{:S(2)}) async-start(bf16[8,64,1024]{2,1,0:T(8,128)(2,1)} %back.1), calls=%async_computation.2 | async-start | bytes 2097152 | tf_op jit(solution)/shard_map/all_to_all | solution.py:207
  206.4 8.0 %collective-permute-start.11 = (bf16[128,4096]{1,0:T(8,128)(2,1)S(1)}, bf16[128,4096]{1,0:T(8,128)(2,1)S(1)}, u32[]{:S(2)}, u32[]{:S(2)}) collective-permute-start(bf16[128,4096]{1,0:T(8,128)(2,1)S(1)} %convolution_convert_fusion), channel_id=1, source_target_pairs={{0,1},{1,0},{2,3},{3,2},{4,5},{5,4},{6,7},{7,6},{8,9},{9,8},{10,11... | collective-permute-start | bytes 3145736 | tf_op jit(solution)/shard_map/ppermute | solution.py:18
  214.9 44.0 %copy-start.4 = (bf16[8,4096]{1,0:T(8,128)(2,1)S(1)}, bf16[8,4096]{1,0:T(8,128)(2,1)}, u32[]{:S(2)}) copy-start(bf16[8,4096]{1,0:T(8,128)(2,1)} %tokens_ref.1) | copy-start | bytes 196612
  215.0 44.2 %copy-start.5 = (f32[4096]{0:T(1024)S(1)}, f32[4096]{0:T(1024)}, u32[]{:S(2)}) copy-start(f32[4096]{0:T(1024)} %param.13) | copy-start | bytes 49156
  215.0 18.8 %collective-permute-start.15 = (bf16[24,4096]{1,0:T(8,128)(2,1)S(1)}, bf16[24,4096]{1,0:T(8,128)(2,1)S(1)}, u32[]{:S(2)}, u32[]{:S(2)}) collective-permute-start(bf16[24,4096]{1,0:T(8,128)(2,1)S(1)} %get-tuple-element.16), channel_id=1, source_target_pairs={{0,2},{1,3},{2,4},{3,5},{4,6},{5,7},{6,8},{7,9},{8,10},{9,11},{10,... | collective-permute-start | bytes 589832 | tf_op jit(solution)/shard_map/ppermute | solution.py:14
  218.7 15.2 %collective-permute-start.14 = (bf16[24,4096]{1,0:T(8,128)(2,1)S(1)}, bf16[24,4096]{1,0:T(8,128)(2,1)S(1)}, u32[]{:S(2)}, u32[]{:S(2)}) collective-permute-start(bf16[24,4096]{1,0:T(8,128)(2,1)S(1)} %get-tuple-element.17), channel_id=1, source_target_pairs={{0,30},{1,31},{2,0},{3,1},{4,2},{5,3},{6,4},{7,5},{8,6},{9,7},{10,... | collective-permute-start | bytes 589832 | tf_op jit(solution)/shard_map/ppermute | solution.py:14
  221.5 14.9 %collective-permute-start.13 = (bf16[24,4096]{1,0:T(8,128)(2,1)S(1)}, bf16[24,4096]{1,0:T(8,128)(2,1)S(1)}, u32[]{:S(2)}, u32[]{:S(2)}) collective-permute-start(bf16[24,4096]{1,0:T(8,128)(2,1)S(1)} %get-tuple-element.18), channel_id=1, source_target_pairs={{0,4},{1,5},{2,6},{3,7},{4,8},{5,9},{6,10},{7,11},{8,12},{9,13},{1... | collective-permute-start | bytes 589832 | tf_op jit(solution)/shard_map/ppermute | solution.py:14
  226.5 12.8 %collective-permute-start.12 = (bf16[24,4096]{1,0:T(8,128)(2,1)S(1)}, bf16[24,4096]{1,0:T(8,128)(2,1)S(1)}, u32[]{:S(2)}, u32[]{:S(2)}) collective-permute-start(bf16[24,4096]{1,0:T(8,128)(2,1)S(1)} %get-tuple-element.15), channel_id=1, source_target_pairs={{0,28},{1,29},{2,30},{3,31},{4,0},{5,1},{6,2},{7,3},{8,4},{9,5},{1... | collective-permute-start | bytes 589832 | tf_op jit(solution)/shard_map/ppermute | solution.py:14
  229.0 10.9 %collective-permute-start.17 = (bf16[8,4096]{1,0:T(8,128)(2,1)S(1)}, bf16[8,4096]{1,0:T(8,128)(2,1)S(1)}, u32[]{:S(2)}, u32[]{:S(2)}) collective-permute-start(bf16[8,4096]{1,0:T(8,128)(2,1)S(1)} %slice.119), channel_id=1, source_target_pairs={{0,6},{1,7},{2,8},{3,9},{4,10},{5,11},{6,12},{7,13},{8,14},{9,15},... | collective-permute-start | bytes 196616 | tf_op jit(solution)/shard_map/ppermute | solution.py:14
  239.9 11.4 %collective-permute-start.18 = (bf16[8,4096]{1,0:T(8,128)(2,1)S(1)}, bf16[8,4096]{1,0:T(8,128)(2,1)S(1)}, u32[]{:S(2)}, u32[]{:S(2)}) collective-permute-start(bf16[8,4096]{1,0:T(8,128)(2,1)S(1)} %fusion.7), channel_id=1, source_target_pairs={{0,10},{1,11},{2,12},{3,13},{4,14},{5,15},{6,16},{7,17},{8,18},{9,... | collective-permute-start | bytes 196616 | tf_op jit(solution)/shard_map/ppermute | solution.py:14
  248.4 10.6 %collective-permute-start.16 = (bf16[8,4096]{1,0:T(8,128)(2,1)S(1)}, bf16[8,4096]{1,0:T(8,128)(2,1)S(1)}, u32[]{:S(2)}, u32[]{:S(2)}) collective-permute-start(bf16[8,4096]{1,0:T(8,128)(2,1)S(1)} %slice.174), channel_id=1, source_target_pairs={{0,22},{1,23},{2,24},{3,25},{4,26},{5,27},{6,28},{7,29},{8,30},{9,... | collective-permute-start | bytes 196616 | tf_op jit(solution)/shard_map/ppermute | solution.py:14
  (3 other events, 23.8 us)

commit v6 on v5

--- a/solution.py
+++ b/solution.py
@@ -205,7 +205,16 @@
 
     out = back(odd, hidden, down_own, down_other, slots)
     home = lax.all_to_all(out, "grp", split_axis=0, concat_axis=0, tiled=True, axis_index_groups=EIGHTS)
-    home = jnp.concatenate([jnp.concatenate(list(home[at:at + 4]), 1) for at in (0, 4)], 0)
+    half_width = home.shape[2] // 2
+    home = jnp.concatenate(
+        [
+            jnp.concatenate(
+                [home[of + j, :, half_width * at:half_width * (at + 1)] for j in range(4) for at in range(2)], 1
+            )
+            for of in (0, 4)
+        ],
+        0,
+    )
 
     def weight(at):
         summed = jnp.sum(jnp.where(match, facts[at][None], 0.0), axis=1)

time: 262 us -> 221 us (0.84)
  other arithmetic: 43.4 us -> 2.3 us
    concatenate x1 -> x0, other arithmetic: 41.1 us -> none  [shards(): home = jnp.concatenate([home, home], 0)]
where the time goes in v6:
time: 221 us; the launch traced here: 219 us
  starting transfers between devices  97.2 us (44%)
  waiting for transfers between devices  82.8 us (37%)
  blocking collectives  17.7 us (8%)
  Pallas kernels  12.3 us (6%)
  local copies, waits for them, and re-layouts  3.82 us (2%)
  other arithmetic  2.3 us (1%)
  matrix products  2.21 us (1%)
    ppermute x14, starting transfers between devices, around(): lax.ppermute(block, 'ep', [(i, (i + 2 * chips) % size) for i in range(siz...  67.8 us
    all_to_all x1, waiting for transfers between devices, shards(): lax.all_to_all(fanned, 'grp', split_axis=0, concat_axis=0, tiled=True, ax...  24.1 us
    ppermute x3, waiting for transfers between devices, pair_swap(): lax.ppermute(block, 'grp', [(i, i ^ 1) for i in range(lax.axis_size('grp'...  20.7 us
    ppermute x14, waiting for transfers between devices, around(): lax.ppermute(block, 'ep', [(i, (i + 2 * chips) % size) for i in range(siz...  19.8 us
    all_to_all x1, blocking collectives, shards(): lax.all_to_all(hidden, 'grp', split_axis=0, concat_axis=0, tiled=True, ax...  17.7 us
    all_to_all x1, waiting for transfers between devices, shards(): lax.all_to_all(out, 'grp', split_axis=0, concat_axis=0, tiled=True, axis_...  13.8 us
    ppermute x2, starting transfers between devices, core_swap(): lax.ppermute(block, 'ep', [(i, i ^ 1) for i in range(lax.axis_size('ep'))])  10.9 us
    ppermute x3, starting transfers between devices, pair_swap(): lax.ppermute(block, 'grp', [(i, i ^ 1) for i in range(lax.axis_size('grp'...  8.41 us
  transfers between devices with their start and end apart: 21, of which 13 were waited for; matrix products, arithmetic and copies ran while one was open for 1% of the time, Pallas kernels for 3%

profile of v6, /device:TPU:1, one launch (start us, length us, event | category | flops | bytes accessed | tf_op | source)
XLA Modules:
  0.0 218.8 jit_solution(15178628366759798315)
XLA Ops:
  1.6 11.0 %collective-permute-start = (bf16[8,4224]{1,0:T(8,128)(2,1)}, bf16[8,4224]{1,0:T(8,128)(2,1)S(1)}, u32[]{:S(2)}, u32[]{:S(2)}) collective-permute-start(bf16[8,4224]{1,0:T(8,128)(2,1)} %with_facts.1), channel_id=1, source_target_pairs={{0,10},{1,11},{2,12},{3,13},{4,14},{5,15},{6,16},{7,17},{8,18},{9,... | collective-permute-start | bytes 202760 | tf_op jit(solution)/shard_map/ppermute | solution.py:14
  12.6 5.9 %collective-permute-start.1 = (bf16[8,4224]{1,0:T(8,128)(2,1)}, bf16[8,4224]{1,0:T(8,128)(2,1)S(1)}, u32[]{:S(2)}, u32[]{:S(2)}) collective-permute-start(bf16[8,4224]{1,0:T(8,128)(2,1)} %with_facts.1), channel_id=1, source_target_pairs={{0,22},{1,23},{2,24},{3,25},{4,26},{5,27},{6,28},{7,29},{8,30},{9,... | collective-permute-start | bytes 202760 | tf_op jit(solution)/shard_map/ppermute | solution.py:14
  18.5 3.1 %collective-permute-start.7 = (bf16[4096,128]{1,0:T(8,128)(2,1)}, bf16[4096,128]{1,0:T(8,128)(2,1)S(1)}, u32[]{:S(2)}, u32[]{:S(2)}) collective-permute-start(bf16[4096,128]{1,0:T(8,128)(2,1)} %bitcast.88), channel_id=1, source_target_pairs={{0,32},{32,0},{64,96},{96,64},{128,160},{160,128},{192,224},{224,1... | collective-permute-start | bytes 3145736 | tf_op jit(solution)/shard_map/ppermute | solution.py:22
  27.4 4.5 %collective-permute-start.3 = (bf16[24,4224]{1,0:T(8,128)(2,1)S(1)}, bf16[24,4224]{1,0:T(8,128)(2,1)S(1)}, u32[]{:S(2)}, u32[]{:S(2)}) collective-permute-start(bf16[24,4224]{1,0:T(8,128)(2,1)S(1)} %pad_maximum_fusion.5), channel_id=1, source_target_pairs={{0,30},{1,31},{2,0},{3,1},{4,2},{5,3},{6,4},{7,5},{8,6},{9,7},{10,... | collective-permute-start | bytes 608264 | tf_op jit(solution)/shard_map/ppermute | solution.py:14
  31.9 7.4 %collective-permute-start.6 = (bf16[8,4224]{1,0:T(8,128)(2,1)S(1)}, bf16[8,4224]{1,0:T(8,128)(2,1)S(1)}, u32[]{:S(2)}, u32[]{:S(2)}) collective-permute-start(bf16[8,4224]{1,0:T(8,128)(2,1)S(1)} %collective-permute-done.1), channel_id=1, source_target_pairs={{0,26},{1,27},{2,28},{3,29},{4,30},{5,31},{6,0},{7,1},{8,2},{9,3},... | collective-permute-start | bytes 202760 | tf_op jit(solution)/shard_map/ppermute | solution.py:14
  39.3 3.4 %collective-permute-start.4 = (bf16[24,4224]{1,0:T(8,128)(2,1)S(1)}, bf16[24,4224]{1,0:T(8,128)(2,1)S(1)}, u32[]{:S(2)}, u32[]{:S(2)}) collective-permute-start(bf16[24,4224]{1,0:T(8,128)(2,1)S(1)} %collective-permute-done.2), channel_id=1, source_target_pairs={{0,2},{1,3},{2,4},{3,5},{4,6},{5,7},{6,8},{7,9},{8,10},{9,11},{10,... | collective-permute-start | bytes 608264 | tf_op jit(solution)/shard_map/ppermute | solution.py:14
  42.7 3.1 %collective-permute-start.5 = (bf16[24,4224]{1,0:T(8,128)(2,1)S(1)}, bf16[24,4224]{1,0:T(8,128)(2,1)S(1)}, u32[]{:S(2)}, u32[]{:S(2)}) collective-permute-start(bf16[24,4224]{1,0:T(8,128)(2,1)S(1)} %collective-permute-done.3), channel_id=1, source_target_pairs={{0,30},{1,31},{2,0},{3,1},{4,2},{5,3},{6,4},{7,5},{8,6},{9,7},{10,... | collective-permute-start | bytes 608264 | tf_op jit(solution)/shard_map/ppermute | solution.py:14
  47.3 3.3 %collective-permute-done.5 = bf16[24,4224]{1,0:T(8,128)(2,1)S(1)} collective-permute-done((bf16[24,4224]{1,0:T(8,128)(2,1)S(1)}, bf16[24,4224]{1,0:T(8,128)(2,1)S(1)}, u32[]{:S(2)}, u32[]{:S(2)}) %collective-permute-start.5) | collective-permute-done | bytes 202784 | tf_op jit(solution)/shard_map/ppermute | solution.py:14
  50.7 5.1 %collective-permute-start.8 = (bf16[128,4224]{1,0:T(8,128)(2,1)S(1)}, bf16[128,4224]{1,0:T(8,128)(2,1)S(1)}, u32[]{:S(2)}, u32[]{:S(2)}) collective-permute-start(bf16[128,4224]{1,0:T(8,128)(2,1)S(1)} %constant_dynamic-update-slice_fusion), channel_id=1, source_target_pairs={{0,1},{1,0},{2,3},{3,2},{4,5},{5,4},{6,7},{7,6},{8,9},{9,8},{10,11... | collective-permute-start | bytes 3244040 | tf_op jit(solution)/shard_map/ppermute | solution.py:18
  62.1 6.5 %all-to-all-start = ((bf16[8,64,4096]{2,1,0:T(8,128)(2,1)}), bf16[8,64,4096]{2,1,0:T(8,128)(2,1)}, u32[]{:S(2)}, u32[]{:S(2)}) async-start(bf16[8,64,4096]{2,1,0:T(8,128)(2,1)} %bitcast.86), calls=%async_computation | async-start | bytes 8388608 | tf_op jit(solution)/shard_map/all_to_all | solution.py:199
  70.6 3.4 %collective-permute-start.10 = (bf16[1024,512]{1,0:T(8,128)(2,1)S(1)}, bf16[1024,512]{1,0:T(8,128)(2,1)S(1)}, u32[]{:S(2)}, u32[]{:S(2)}) collective-permute-start(bf16[1024,512]{1,0:T(8,128)(2,1)S(1)} %bitcast.93), channel_id=1, source_target_pairs={{0,32},{32,0},{64,96},{96,64},{128,160},{160,128},{192,224},{224,1... | collective-permute-start | bytes 3145736 | tf_op jit(solution)/shard_map/ppermute | solution.py:22
  74.0 20.7 %collective-permute-done.9.up_other = bf16[4096,128]{1,0:T(8,128)(2,1)} collective-permute-done((bf16[4096,128]{1,0:T(8,128)(2,1)S(1)}, bf16[4096,128]{1,0:T(8,128)(2,1)}, u32[]{:S(2)}, u32[]{:S(2)}) %collective-permute-start.9) | collective-permute-done | bytes 1048608 | tf_op jit(solution)/shard_map/ppermute | solution.py:22
  94.7 24.1 %all-to-all-done = bf16[8,64,4096]{2,1,0:T(8,128)(2,1)} async-done(((bf16[8,64,4096]{2,1,0:T(8,128)(2,1)}), bf16[8,64,4096]{2,1,0:T(8,128)(2,1)}, u32[]{:S(2)}, u32[]{:S(2)}) %all-to-all-start) | async-done | bytes 4194336 | tf_op jit(solution)/shard_map/all_to_all | solution.py:199
  118.8 6.6 %front.1 = bf16[4,512,256]{2,1,0:T(8,128)(2,1)} custom-call(s32[1]{0:T(128)} %bitcast.4.odd_ref, bf16[512,4096]{1,0:T(8,128)(2,1)} %bitcast.7.rows_ref, bf16[4096,128]{1,0:T(8,128)(2,1)} %bitcast.89, bf16[4096,128]{1,0:T(8,128)(2,1)} %copy-done.2, bf16[4096,128]{1,0:T(8,128)(2,1)} %bitcast.90, bf16[4096,128]{1,0:T(8,128)(2,1)} %collective-permute-done.9.up_other), custom_call_target="tpu_custom_call" | custom-call | tf_op jit(solution)/shard_map/front/pallas_call | solution.py:105
  125.5 17.7 %all_to_all.15.hidden_ref = bf16[4,512,256]{2,1,0:T(8,128)(2,1)} all-to-all(bf16[4,512,256]{2,1,0:T(8,128)(2,1)} %front.1), channel_id=1, replica_groups={{0,96,128,224},{256,352,384,480},{32,64,160,192},{288,320,416,448},{1,9..., dimensions={0} | all-to-all | bytes 2097152 | tf_op jit(solution)/shard_map/all_to_all | solution.py:204
  143.2 4.1 %back.1 = bf16[8,64,1024]{2,1,0:T(8,128)(2,1)} custom-call(s32[1]{0:T(128)} %bitcast.4.odd_ref, bf16[4,512,256]{2,1,0:T(8,128)(2,1)} %all_to_all.15.hidden_ref, bf16[1024,512]{1,0:T(8,128)(2,1)} %bitcast.92, bf16[1024,512]{1,0:T(8,128)(2,1)} %copy-done.3), custom_call_target="tpu_custom_call" | custom-call | tf_op jit(solution)/shard_map/back/pallas_call | solution.py:146
  147.3 3.6 %all-to-all-start.2 = ((bf16[8,64,1024]{2,1,0:T(8,128)(2,1)}), bf16[8,64,1024]{2,1,0:T(8,128)(2,1)S(1)}, u32[]{:S(2)}, u32[]{:S(2)}) async-start(bf16[8,64,1024]{2,1,0:T(8,128)(2,1)} %back.1), calls=%async_computation.2 | async-start | bytes 2097152 | tf_op jit(solution)/shard_map/all_to_all | solution.py:207
  151.0 13.8 %all-to-all-done.2 = bf16[8,64,1024]{2,1,0:T(8,128)(2,1)S(1)} async-done(((bf16[8,64,1024]{2,1,0:T(8,128)(2,1)}), bf16[8,64,1024]{2,1,0:T(8,128)(2,1)S(1)}, u32[]{:S(2)}, u32[]{:S(2)}) %all-to-all-start.2) | async-done | bytes 1048608 | tf_op jit(solution)/shard_map/all_to_all | solution.py:207
  165.4 5.7 %collective-permute-start.11 = (bf16[128,4096]{1,0:T(8,128)(2,1)S(1)}, bf16[128,4096]{1,0:T(8,128)(2,1)S(1)}, u32[]{:S(2)}, u32[]{:S(2)}) collective-permute-start(bf16[128,4096]{1,0:T(8,128)(2,1)S(1)} %convolution_convert_fusion), channel_id=1, source_target_pairs={{0,1},{1,0},{2,3},{3,2},{4,5},{5,4},{6,7},{7,6},{8,9},{9,8},{10,11... | collective-permute-start | bytes 3145736 | tf_op jit(solution)/shard_map/ppermute | solution.py:18
  174.0 3.6 %collective-permute-start.15 = (bf16[24,4096]{1,0:T(8,128)(2,1)S(1)}, bf16[24,4096]{1,0:T(8,128)(2,1)S(1)}, u32[]{:S(2)}, u32[]{:S(2)}) collective-permute-start(bf16[24,4096]{1,0:T(8,128)(2,1)S(1)} %get-tuple-element.16), channel_id=1, source_target_pairs={{0,2},{1,3},{2,4},{3,5},{4,6},{5,7},{6,8},{7,9},{8,10},{9,11},{10,... | collective-permute-start | bytes 589832 | tf_op jit(solution)/shard_map/ppermute | solution.py:14
  180.5 4.9 %collective-permute-start.13 = (bf16[24,4096]{1,0:T(8,128)(2,1)S(1)}, bf16[24,4096]{1,0:T(8,128)(2,1)S(1)}, u32[]{:S(2)}, u32[]{:S(2)}) collective-permute-start(bf16[24,4096]{1,0:T(8,128)(2,1)S(1)} %get-tuple-element.18), channel_id=1, source_target_pairs={{0,4},{1,5},{2,6},{3,7},{4,8},{5,9},{6,10},{7,11},{8,12},{9,13},{1... | collective-permute-start | bytes 589832 | tf_op jit(solution)/shard_map/ppermute | solution.py:14
  187.9 4.9 %collective-permute-start.17 = (bf16[8,4096]{1,0:T(8,128)(2,1)S(1)}, bf16[8,4096]{1,0:T(8,128)(2,1)S(1)}, u32[]{:S(2)}, u32[]{:S(2)}) collective-permute-start(bf16[8,4096]{1,0:T(8,128)(2,1)S(1)} %slice.189), channel_id=1, source_target_pairs={{0,6},{1,7},{2,8},{3,9},{4,10},{5,11},{6,12},{7,13},{8,14},{9,15},... | collective-permute-start | bytes 196616 | tf_op jit(solution)/shard_map/ppermute | solution.py:14
  198.8 8.6 %collective-permute-start.18 = (bf16[8,4096]{1,0:T(8,128)(2,1)S(1)}, bf16[8,4096]{1,0:T(8,128)(2,1)S(1)}, u32[]{:S(2)}, u32[]{:S(2)}) collective-permute-start(bf16[8,4096]{1,0:T(8,128)(2,1)S(1)} %fusion.8), channel_id=1, source_target_pairs={{0,10},{1,11},{2,12},{3,13},{4,14},{5,15},{6,16},{7,17},{8,18},{9,... | collective-permute-start | bytes 196616 | tf_op jit(solution)/shard_map/ppermute | solution.py:14
  210.3 7.6 %collective-permute-done.16 = bf16[8,4096]{1,0:T(8,128)(2,1)S(1)} collective-permute-done((bf16[8,4096]{1,0:T(8,128)(2,1)S(1)}, bf16[8,4096]{1,0:T(8,128)(2,1)S(1)}, u32[]{:S(2)}, u32[]{:S(2)}) %collective-permute-start.16) | collective-permute-done | bytes 65568 | tf_op jit(solution)/shard_map/ppermute | solution.py:14
  (75 shorter events, 35.6 us)
Async XLA Ops:
  1.6 20.9 %collective-permute-start = (bf16[8,4224]{1,0:T(8,128)(2,1)}, bf16[8,4224]{1,0:T(8,128)(2,1)S(1)}, u32[]{:S(2)}, u32[]{:S(2)}) collective-permute-start(bf16[8,4224]{1,0:T(8,128)(2,1)} %with_facts.1), channel_id=1, source_target_pairs={{0,10},{1,11},{2,12},{3,13},{4,14},{5,15},{6,16},{7,17},{8,18},{9,... | collective-permute-start | bytes 202760 | tf_op jit(solution)/shard_map/ppermute | solution.py:14
  12.6 11.3 %collective-permute-start.1 = (bf16[8,4224]{1,0:T(8,128)(2,1)}, bf16[8,4224]{1,0:T(8,128)(2,1)S(1)}, u32[]{:S(2)}, u32[]{:S(2)}) collective-permute-start(bf16[8,4224]{1,0:T(8,128)(2,1)} %with_facts.1), channel_id=1, source_target_pairs={{0,22},{1,23},{2,24},{3,25},{4,26},{5,27},{6,28},{7,29},{8,30},{9,... | collective-permute-start | bytes 202760 | tf_op jit(solution)/shard_map/ppermute | solution.py:14
  18.5 32.2 %collective-permute-start.7 = (bf16[4096,128]{1,0:T(8,128)(2,1)}, bf16[4096,128]{1,0:T(8,128)(2,1)S(1)}, u32[]{:S(2)}, u32[]{:S(2)}) collective-permute-start(bf16[4096,128]{1,0:T(8,128)(2,1)} %bitcast.88), channel_id=1, source_target_pairs={{0,32},{32,0},{64,96},{96,64},{128,160},{160,128},{192,224},{224,1... | collective-permute-start | bytes 3145736 | tf_op jit(solution)/shard_map/ppermute | solution.py:22
  24.8 14.5 %collective-permute-start.2 = (bf16[24,4224]{1,0:T(8,128)(2,1)S(1)}, bf16[24,4224]{1,0:T(8,128)(2,1)S(1)}, u32[]{:S(2)}, u32[]{:S(2)}) collective-permute-start(bf16[24,4224]{1,0:T(8,128)(2,1)S(1)} %pad_maximum_fusion.5), channel_id=1, source_target_pairs={{0,2},{1,3},{2,4},{3,5},{4,6},{5,7},{6,8},{7,9},{8,10},{9,11},{10,... | collective-permute-start | bytes 608264 | tf_op jit(solution)/shard_map/ppermute | solution.py:14
  27.4 15.3 %collective-permute-start.3 = (bf16[24,4224]{1,0:T(8,128)(2,1)S(1)}, bf16[24,4224]{1,0:T(8,128)(2,1)S(1)}, u32[]{:S(2)}, u32[]{:S(2)}) collective-permute-start(bf16[24,4224]{1,0:T(8,128)(2,1)S(1)} %pad_maximum_fusion.5), channel_id=1, source_target_pairs={{0,30},{1,31},{2,0},{3,1},{4,2},{5,3},{6,4},{7,5},{8,6},{9,7},{10,... | collective-permute-start | bytes 608264 | tf_op jit(solution)/shard_map/ppermute | solution.py:14
  31.9 18.8 %collective-permute-start.6 = (bf16[8,4224]{1,0:T(8,128)(2,1)S(1)}, bf16[8,4224]{1,0:T(8,128)(2,1)S(1)}, u32[]{:S(2)}, u32[]{:S(2)}) collective-permute-start(bf16[8,4224]{1,0:T(8,128)(2,1)S(1)} %collective-permute-done.1), channel_id=1, source_target_pairs={{0,26},{1,27},{2,28},{3,29},{4,30},{5,31},{6,0},{7,1},{8,2},{9,3},... | collective-permute-start | bytes 202760 | tf_op jit(solution)/shard_map/ppermute | solution.py:14
  39.3 8.0 %collective-permute-start.4 = (bf16[24,4224]{1,0:T(8,128)(2,1)S(1)}, bf16[24,4224]{1,0:T(8,128)(2,1)S(1)}, u32[]{:S(2)}, u32[]{:S(2)}) collective-permute-start(bf16[24,4224]{1,0:T(8,128)(2,1)S(1)} %collective-permute-done.2), channel_id=1, source_target_pairs={{0,2},{1,3},{2,4},{3,5},{4,6},{5,7},{6,8},{7,9},{8,10},{9,11},{10,... | collective-permute-start | bytes 608264 | tf_op jit(solution)/shard_map/ppermute | solution.py:14
  42.7 7.9 %collective-permute-start.5 = (bf16[24,4224]{1,0:T(8,128)(2,1)S(1)}, bf16[24,4224]{1,0:T(8,128)(2,1)S(1)}, u32[]{:S(2)}, u32[]{:S(2)}) collective-permute-start(bf16[24,4224]{1,0:T(8,128)(2,1)S(1)} %collective-permute-done.3), channel_id=1, source_target_pairs={{0,30},{1,31},{2,0},{3,1},{4,2},{5,3},{6,4},{7,5},{8,6},{9,7},{10,... | collective-permute-start | bytes 608264 | tf_op jit(solution)/shard_map/ppermute | solution.py:14
  50.7 7.5 %collective-permute-start.8 = (bf16[128,4224]{1,0:T(8,128)(2,1)S(1)}, bf16[128,4224]{1,0:T(8,128)(2,1)S(1)}, u32[]{:S(2)}, u32[]{:S(2)}) collective-permute-start(bf16[128,4224]{1,0:T(8,128)(2,1)S(1)} %constant_dynamic-update-slice_fusion), channel_id=1, source_target_pairs={{0,1},{1,0},{2,3},{3,2},{4,5},{5,4},{6,7},{7,6},{8,9},{9,8},{10,11... | collective-permute-start | bytes 3244040 | tf_op jit(solution)/shard_map/ppermute | solution.py:18
  62.1 56.7 %all-to-all-start = ((bf16[8,64,4096]{2,1,0:T(8,128)(2,1)}), bf16[8,64,4096]{2,1,0:T(8,128)(2,1)}, u32[]{:S(2)}, u32[]{:S(2)}) async-start(bf16[8,64,4096]{2,1,0:T(8,128)(2,1)} %bitcast.86), calls=%async_computation | async-start | bytes 8388608 | tf_op jit(solution)/shard_map/all_to_all | solution.py:199
  68.6 26.0 %collective-permute-start.9 = (bf16[4096,128]{1,0:T(8,128)(2,1)S(1)}, bf16[4096,128]{1,0:T(8,128)(2,1)}, u32[]{:S(2)}, u32[]{:S(2)}) collective-permute-start(bf16[4096,128]{1,0:T(8,128)(2,1)S(1)} %bitcast.91), channel_id=1, source_target_pairs={{0,32},{32,0},{64,96},{96,64},{128,160},{160,128},{192,224},{224,1... | collective-permute-start | bytes 3145736 | tf_op jit(solution)/shard_map/ppermute | solution.py:22
  70.6 54.9 %collective-permute-start.10 = (bf16[1024,512]{1,0:T(8,128)(2,1)S(1)}, bf16[1024,512]{1,0:T(8,128)(2,1)S(1)}, u32[]{:S(2)}, u32[]{:S(2)}) collective-permute-start(bf16[1024,512]{1,0:T(8,128)(2,1)S(1)} %bitcast.93), channel_id=1, source_target_pairs={{0,32},{32,0},{64,96},{96,64},{128,160},{160,128},{192,224},{224,1... | collective-permute-start | bytes 3145736 | tf_op jit(solution)/shard_map/ppermute | solution.py:22
  125.5 17.7 %copy-start.3 = (bf16[1024,512]{1,0:T(8,128)(2,1)}, bf16[1024,512]{1,0:T(8,128)(2,1)S(1)}, u32[]{:S(2)}) copy-start(bf16[1024,512]{1,0:T(8,128)(2,1)S(1)} %collective-permute-done.10.other_ref) | copy-start | bytes 3145732
  147.3 17.5 %all-to-all-start.2 = ((bf16[8,64,1024]{2,1,0:T(8,128)(2,1)}), bf16[8,64,1024]{2,1,0:T(8,128)(2,1)S(1)}, u32[]{:S(2)}, u32[]{:S(2)}) async-start(bf16[8,64,1024]{2,1,0:T(8,128)(2,1)} %back.1), calls=%async_computation.2 | async-start | bytes 2097152 | tf_op jit(solution)/shard_map/all_to_all | solution.py:207
  165.4 8.0 %collective-permute-start.11 = (bf16[128,4096]{1,0:T(8,128)(2,1)S(1)}, bf16[128,4096]{1,0:T(8,128)(2,1)S(1)}, u32[]{:S(2)}, u32[]{:S(2)}) collective-permute-start(bf16[128,4096]{1,0:T(8,128)(2,1)S(1)} %convolution_convert_fusion), channel_id=1, source_target_pairs={{0,1},{1,0},{2,3},{3,2},{4,5},{5,4},{6,7},{7,6},{8,9},{9,8},{10,11... | collective-permute-start | bytes 3145736 | tf_op jit(solution)/shard_map/ppermute | solution.py:18
  173.9 44.0 %copy-start.4 = (bf16[8,4096]{1,0:T(8,128)(2,1)S(1)}, bf16[8,4096]{1,0:T(8,128)(2,1)}, u32[]{:S(2)}) copy-start(bf16[8,4096]{1,0:T(8,128)(2,1)} %tokens_ref.1) | copy-start | bytes 196612
  173.9 44.2 %copy-start.5 = (f32[4096]{0:T(1024)S(1)}, f32[4096]{0:T(1024)}, u32[]{:S(2)}) copy-start(f32[4096]{0:T(1024)} %param.13) | copy-start | bytes 49156
  174.0 18.9 %collective-permute-start.15 = (bf16[24,4096]{1,0:T(8,128)(2,1)S(1)}, bf16[24,4096]{1,0:T(8,128)(2,1)S(1)}, u32[]{:S(2)}, u32[]{:S(2)}) collective-permute-start(bf16[24,4096]{1,0:T(8,128)(2,1)S(1)} %get-tuple-element.16), channel_id=1, source_target_pairs={{0,2},{1,3},{2,4},{3,5},{4,6},{5,7},{6,8},{7,9},{8,10},{9,11},{10,... | collective-permute-start | bytes 589832 | tf_op jit(solution)/shard_map/ppermute | solution.py:14
  177.7 15.2 %collective-permute-start.14 = (bf16[24,4096]{1,0:T(8,128)(2,1)S(1)}, bf16[24,4096]{1,0:T(8,128)(2,1)S(1)}, u32[]{:S(2)}, u32[]{:S(2)}) collective-permute-start(bf16[24,4096]{1,0:T(8,128)(2,1)S(1)} %get-tuple-element.17), channel_id=1, source_target_pairs={{0,30},{1,31},{2,0},{3,1},{4,2},{5,3},{6,4},{7,5},{8,6},{9,7},{10,... | collective-permute-start | bytes 589832 | tf_op jit(solution)/shard_map/ppermute | solution.py:14
  180.5 15.0 %collective-permute-start.13 = (bf16[24,4096]{1,0:T(8,128)(2,1)S(1)}, bf16[24,4096]{1,0:T(8,128)(2,1)S(1)}, u32[]{:S(2)}, u32[]{:S(2)}) collective-permute-start(bf16[24,4096]{1,0:T(8,128)(2,1)S(1)} %get-tuple-element.18), channel_id=1, source_target_pairs={{0,4},{1,5},{2,6},{3,7},{4,8},{5,9},{6,10},{7,11},{8,12},{9,13},{1... | collective-permute-start | bytes 589832 | tf_op jit(solution)/shard_map/ppermute | solution.py:14
  185.5 12.8 %collective-permute-start.12 = (bf16[24,4096]{1,0:T(8,128)(2,1)S(1)}, bf16[24,4096]{1,0:T(8,128)(2,1)S(1)}, u32[]{:S(2)}, u32[]{:S(2)}) collective-permute-start(bf16[24,4096]{1,0:T(8,128)(2,1)S(1)} %get-tuple-element.15), channel_id=1, source_target_pairs={{0,28},{1,29},{2,30},{3,31},{4,0},{5,1},{6,2},{7,3},{8,4},{9,5},{1... | collective-permute-start | bytes 589832 | tf_op jit(solution)/shard_map/ppermute | solution.py:14
  187.9 10.9 %collective-permute-start.17 = (bf16[8,4096]{1,0:T(8,128)(2,1)S(1)}, bf16[8,4096]{1,0:T(8,128)(2,1)S(1)}, u32[]{:S(2)}, u32[]{:S(2)}) collective-permute-start(bf16[8,4096]{1,0:T(8,128)(2,1)S(1)} %slice.189), channel_id=1, source_target_pairs={{0,6},{1,7},{2,8},{3,9},{4,10},{5,11},{6,12},{7,13},{8,14},{9,15},... | collective-permute-start | bytes 196616 | tf_op jit(solution)/shard_map/ppermute | solution.py:14
  198.8 11.5 %collective-permute-start.18 = (bf16[8,4096]{1,0:T(8,128)(2,1)S(1)}, bf16[8,4096]{1,0:T(8,128)(2,1)S(1)}, u32[]{:S(2)}, u32[]{:S(2)}) collective-permute-start(bf16[8,4096]{1,0:T(8,128)(2,1)S(1)} %fusion.8), channel_id=1, source_target_pairs={{0,10},{1,11},{2,12},{3,13},{4,14},{5,15},{6,16},{7,17},{8,18},{9,... | collective-permute-start | bytes 196616 | tf_op jit(solution)/shard_map/ppermute | solution.py:14
  207.4 10.5 %collective-permute-start.16 = (bf16[8,4096]{1,0:T(8,128)(2,1)S(1)}, bf16[8,4096]{1,0:T(8,128)(2,1)S(1)}, u32[]{:S(2)}, u32[]{:S(2)}) collective-permute-start(bf16[8,4096]{1,0:T(8,128)(2,1)S(1)} %slice.290), channel_id=1, source_target_pairs={{0,22},{1,23},{2,24},{3,25},{4,26},{5,27},{6,28},{7,29},{8,30},{9,... | collective-permute-start | bytes 196616 | tf_op jit(solution)/shard_map/ppermute | solution.py:14
  (3 other events, 23.8 us)

commit v7 on v6

--- a/solution.py
+++ b/solution.py
@@ -77,7 +77,7 @@
 
 def front(odd, rows, gates, ups):
     count, width = rows.shape
-    units, block = gates[0].shape[1], 1024
+    units, block = gates[0].shape[1], 2048
     steps = width // block
 
     def kernel(odd_ref, rows_ref, gate_own, gate_other, up_own, up_other, out_ref, total):
@@ -113,6 +113,7 @@
         out_specs=whole((4, count, 2 * units)),
         out_shape=jax.ShapeDtypeStruct((4, count, 2 * units), BF16),
         scratch_shapes=[pltpu.VMEM((count, 4 * units), F32)],
+        compiler_params=pltpu.CompilerParams(vmem_limit_bytes=32 * 2**20),
         name="front",
     )(odd, rows, *gates, *ups)
 
@@ -166,10 +167,9 @@
     odd = (g % 2).astype(jnp.int32).reshape(1)
 
     gate_own, up_own, down_own = w_gate[0], w_up[0], w_down[0]
-    gate_other, up_other, down_other = pair_swap(gate_own), pair_swap(up_own), pair_swap(down_own)
+    gate_other, up_other = pair_swap(gate_own), pair_swap(up_own)
 
     column = gather_column(with_facts(tokens, expert_ids, gate_weights))
-    column, gate_other = lax.optimization_barrier((column, gate_other))
     parts = column, core_swap(column)
     half = parts[0].shape[0]
     rows = 2 * half
@@ -197,10 +197,11 @@
     fanned = jnp.broadcast_to(chosen, (2, 4, slots, width)).reshape(8, slots, width)
 
     arrived = lax.all_to_all(fanned, "grp", split_axis=0, concat_axis=0, tiled=True, axis_index_groups=EIGHTS)
+    arrived, down_own = lax.optimization_barrier((arrived, down_own))
+    down_other = pair_swap(down_own)
     arrived = arrived.reshape(8 * slots, width)
 
     hidden = front(odd, arrived, (gate_own, gate_other), (up_own, up_other))
-    hidden, down_other = lax.optimization_barrier((hidden, down_other))
     hidden = lax.all_to_all(hidden, "grp", split_axis=0, concat_axis=0, tiled=True, axis_index_groups=FOURS)
 
     out = back(odd, hidden, down_own, down_other, slots)

time: 221 us -> 222 us (level)
  waiting for transfers between devices: 82.8 us -> 89.3 us
    all_to_all x1, waiting for transfers between devices: 24.1 us -> 44.9 us  [shards(): lax.all_to_all(fanned, 'grp', split_axis=0, concat_axis=0, tiled=True, ax...]
    ppermute x3, waiting for transfers between devices: 20.7 us -> 2.33 us  [pair_swap(): lax.ppermute(block, 'grp', [(i, i ^ 1) for i in range(lax.axis_size('grp'...]
    ppermute x14, waiting for transfers between devices: 19.8 us -> 22.9 us  [around(): lax.ppermute(block, 'ep', [(i, (i + 2 * chips) % size) for i in range(siz...]
  transfers between devices with their start and end apart: 21 -> 21, of which waited for: 13 -> 13; matrix products, arithmetic and copies ran while one was open for 1% -> 1% of each run, Pallas kernels for 3% -> 2%
where the time goes in v7:
time: 222 us; the launch traced here: 221 us
  starting transfers between devices  96 us (43%)
  waiting for transfers between devices  89.3 us (40%)
  blocking collectives  16.5 us (7%)
  Pallas kernels  10.2 us (5%)
  local copies, waits for them, and re-layouts  3.84 us (2%)
  other arithmetic  2.3 us (1%)
    ppermute x14, starting transfers between devices, around(): lax.ppermute(block, 'ep', [(i, (i + 2 * chips) % size) for i in range(siz...  67.8 us
    all_to_all x1, waiting for transfers between devices, shards(): lax.all_to_all(fanned, 'grp', split_axis=0, concat_axis=0, tiled=True, ax...  44.9 us
    ppermute x14, waiting for transfers between devices, around(): lax.ppermute(block, 'ep', [(i, (i + 2 * chips) % size) for i in range(siz...  22.9 us
    all_to_all x1, blocking collectives, shards(): lax.all_to_all(hidden, 'grp', split_axis=0, concat_axis=0, tiled=True, ax...  16.5 us
    all_to_all x1, waiting for transfers between devices, shards(): lax.all_to_all(out, 'grp', split_axis=0, concat_axis=0, tiled=True, axis_...  14.8 us
    ppermute x2, starting transfers between devices, core_swap(): lax.ppermute(block, 'ep', [(i, i ^ 1) for i in range(lax.axis_size('ep'))])  9.89 us
    ppermute x3, starting transfers between devices, pair_swap(): lax.ppermute(block, 'grp', [(i, i ^ 1) for i in range(lax.axis_size('grp'...  7.2 us
    all_to_all x1, starting transfers between devices, shards(): lax.all_to_all(fanned, 'grp', split_axis=0, concat_axis=0, tiled=True, ax...  6.52 us
  transfers between devices with their start and end apart: 21, of which 13 were waited for; matrix products, arithmetic and copies ran while one was open for 1% of the time, Pallas kernels for 2%

profile of v7, /device:TPU:1, one launch (start us, length us, event | category | flops | bytes accessed | tf_op | source)
XLA Modules:
  0.0 220.8 jit_solution(10505057489115388771)
XLA Ops:
  1.6 11.0 %collective-permute-start = (bf16[8,4224]{1,0:T(8,128)(2,1)}, bf16[8,4224]{1,0:T(8,128)(2,1)S(1)}, u32[]{:S(2)}, u32[]{:S(2)}) collective-permute-start(bf16[8,4224]{1,0:T(8,128)(2,1)} %with_facts.1), channel_id=1, source_target_pairs={{0,10},{1,11},{2,12},{3,13},{4,14},{5,15},{6,16},{7,17},{8,18},{9,... | collective-permute-start | bytes 202760 | tf_op jit(solution)/shard_map/ppermute | solution.py:14
  12.6 5.9 %collective-permute-start.1 = (bf16[8,4224]{1,0:T(8,128)(2,1)}, bf16[8,4224]{1,0:T(8,128)(2,1)S(1)}, u32[]{:S(2)}, u32[]{:S(2)}) collective-permute-start(bf16[8,4224]{1,0:T(8,128)(2,1)} %with_facts.1), channel_id=1, source_target_pairs={{0,22},{1,23},{2,24},{3,25},{4,26},{5,27},{6,28},{7,29},{8,30},{9,... | collective-permute-start | bytes 202760 | tf_op jit(solution)/shard_map/ppermute | solution.py:14
  19.4 4.6 %collective-permute-done.1 = bf16[8,4224]{1,0:T(8,128)(2,1)S(1)} collective-permute-done((bf16[8,4224]{1,0:T(8,128)(2,1)}, bf16[8,4224]{1,0:T(8,128)(2,1)S(1)}, u32[]{:S(2)}, u32[]{:S(2)}) %collective-permute-start.1) | collective-permute-done | bytes 67616 | tf_op jit(solution)/shard_map/ppermute | solution.py:14
  27.4 4.5 %collective-permute-start.3 = (bf16[24,4224]{1,0:T(8,128)(2,1)S(1)}, bf16[24,4224]{1,0:T(8,128)(2,1)S(1)}, u32[]{:S(2)}, u32[]{:S(2)}) collective-permute-start(bf16[24,4224]{1,0:T(8,128)(2,1)S(1)} %pad_maximum_fusion.5), channel_id=1, source_target_pairs={{0,30},{1,31},{2,0},{3,1},{4,2},{5,3},{6,4},{7,5},{8,6},{9,7},{10,... | collective-permute-start | bytes 608264 | tf_op jit(solution)/shard_map/ppermute | solution.py:14
  31.9 7.4 %collective-permute-start.6 = (bf16[8,4224]{1,0:T(8,128)(2,1)S(1)}, bf16[8,4224]{1,0:T(8,128)(2,1)S(1)}, u32[]{:S(2)}, u32[]{:S(2)}) collective-permute-start(bf16[8,4224]{1,0:T(8,128)(2,1)S(1)} %collective-permute-done.1), channel_id=1, source_target_pairs={{0,26},{1,27},{2,28},{3,29},{4,30},{5,31},{6,0},{7,1},{8,2},{9,3},... | collective-permute-start | bytes 202760 | tf_op jit(solution)/shard_map/ppermute | solution.py:14
  39.3 3.4 %collective-permute-start.4 = (bf16[24,4224]{1,0:T(8,128)(2,1)S(1)}, bf16[24,4224]{1,0:T(8,128)(2,1)S(1)}, u32[]{:S(2)}, u32[]{:S(2)}) collective-permute-start(bf16[24,4224]{1,0:T(8,128)(2,1)S(1)} %collective-permute-done.2), channel_id=1, source_target_pairs={{0,2},{1,3},{2,4},{3,5},{4,6},{5,7},{6,8},{7,9},{8,10},{9,11},{10,... | collective-permute-start | bytes 608264 | tf_op jit(solution)/shard_map/ppermute | solution.py:14
  42.7 3.1 %collective-permute-start.5 = (bf16[24,4224]{1,0:T(8,128)(2,1)S(1)}, bf16[24,4224]{1,0:T(8,128)(2,1)S(1)}, u32[]{:S(2)}, u32[]{:S(2)}) collective-permute-start(bf16[24,4224]{1,0:T(8,128)(2,1)S(1)} %collective-permute-done.3), channel_id=1, source_target_pairs={{0,30},{1,31},{2,0},{3,1},{4,2},{5,3},{6,4},{7,5},{8,6},{9,7},{10,... | collective-permute-start | bytes 608264 | tf_op jit(solution)/shard_map/ppermute | solution.py:14
  47.3 3.3 %collective-permute-done.5 = bf16[24,4224]{1,0:T(8,128)(2,1)S(1)} collective-permute-done((bf16[24,4224]{1,0:T(8,128)(2,1)S(1)}, bf16[24,4224]{1,0:T(8,128)(2,1)S(1)}, u32[]{:S(2)}, u32[]{:S(2)}) %collective-permute-start.5) | collective-permute-done | bytes 202784 | tf_op jit(solution)/shard_map/ppermute | solution.py:14
  50.7 5.1 %collective-permute-start.7 = (bf16[128,4224]{1,0:T(8,128)(2,1)S(1)}, bf16[128,4224]{1,0:T(8,128)(2,1)S(1)}, u32[]{:S(2)}, u32[]{:S(2)}) collective-permute-start(bf16[128,4224]{1,0:T(8,128)(2,1)S(1)} %constant_dynamic-update-slice_fusion), channel_id=1, source_target_pairs={{0,1},{1,0},{2,3},{3,2},{4,5},{5,4},{6,7},{7,6},{8,9},{9,8},{10,11... | collective-permute-start | bytes 3244040 | tf_op jit(solution)/shard_map/ppermute | solution.py:18
  62.1 6.5 %all-to-all-start = ((bf16[8,64,4096]{2,1,0:T(8,128)(2,1)}), bf16[8,64,4096]{2,1,0:T(8,128)(2,1)}, u32[]{:S(2)}, u32[]{:S(2)}) async-start(bf16[8,64,4096]{2,1,0:T(8,128)(2,1)} %bitcast.90), calls=%async_computation | async-start | bytes 8388608 | tf_op jit(solution)/shard_map/all_to_all | solution.py:199
  70.5 3.4 %collective-permute-start.9 = (bf16[4096,128]{1,0:T(8,128)(2,1)S(1)}, bf16[4096,128]{1,0:T(8,128)(2,1)}, u32[]{:S(2)}, u32[]{:S(2)}) collective-permute-start(bf16[4096,128]{1,0:T(8,128)(2,1)S(1)} %bitcast.88), channel_id=1, source_target_pairs={{0,32},{32,0},{64,96},{96,64},{128,160},{160,128},{192,224},{224,1... | collective-permute-start | bytes 3145736 | tf_op jit(solution)/shard_map/ppermute | solution.py:22
  73.9 44.9 %all-to-all-done = bf16[8,64,4096]{2,1,0:T(8,128)(2,1)} async-done(((bf16[8,64,4096]{2,1,0:T(8,128)(2,1)}), bf16[8,64,4096]{2,1,0:T(8,128)(2,1)}, u32[]{:S(2)}, u32[]{:S(2)}) %all-to-all-start) | async-done | bytes 4194336 | tf_op jit(solution)/shard_map/all_to_all | solution.py:199
  120.8 4.5 %front.1 = bf16[4,512,256]{2,1,0:T(8,128)(2,1)S(1)} custom-call(s32[1]{0:T(128)} %bitcast.3.odd_ref, bf16[512,4096]{1,0:T(8,128)(2,1)} %bitcast.7.rows_ref, bf16[4096,128]{1,0:T(8,128)(2,1)S(1)} %bitcast.87, bf16[4096,128]{1,0:T(8,128)(2,1)S(1)} %collective-permute-done.8.gate_other, bf16[4096,128]{1,0:T(8,128)(2,1)S(1)} %bitcast.89, ...), custom_call_target="tpu_custom_call" | custom-call | tf_op jit(solution)/shard_map/front/pallas_call | solution.py:105
  125.3 16.5 %all_to_all.15.hidden_ref = bf16[4,512,256]{2,1,0:T(8,128)(2,1)} all-to-all(bf16[4,512,256]{2,1,0:T(8,128)(2,1)S(1)} %front.1), channel_id=1, replica_groups={{0,96,128,224},{256,352,384,480},{32,64,160,192},{288,320,416,448},{1,9..., dimensions={0} | all-to-all | bytes 2097152 | tf_op jit(solution)/shard_map/all_to_all | solution.py:205
  144.1 4.1 %back.1 = bf16[8,64,1024]{2,1,0:T(8,128)(2,1)} custom-call(s32[1]{0:T(128)} %bitcast.3.odd_ref, bf16[4,512,256]{2,1,0:T(8,128)(2,1)} %all_to_all.15.hidden_ref, bf16[1024,512]{1,0:T(8,128)(2,1)} %bitcast.93, bf16[1024,512]{1,0:T(8,128)(2,1)} %collective-permute-done.10.other_ref), custom_call_target="tpu_custom_call" | custom-call | tf_op jit(solution)/shard_map/back/pallas_call | solution.py:147
  148.2 4.5 %all-to-all-start.2 = ((bf16[8,64,1024]{2,1,0:T(8,128)(2,1)}), bf16[8,64,1024]{2,1,0:T(8,128)(2,1)S(1)}, u32[]{:S(2)}, u32[]{:S(2)}) async-start(bf16[8,64,1024]{2,1,0:T(8,128)(2,1)} %back.1), calls=%async_computation.2 | async-start | bytes 2097152 | tf_op jit(solution)/shard_map/all_to_all | solution.py:208
  152.9 14.8 %all-to-all-done.2 = bf16[8,64,1024]{2,1,0:T(8,128)(2,1)S(1)} async-done(((bf16[8,64,1024]{2,1,0:T(8,128)(2,1)}), bf16[8,64,1024]{2,1,0:T(8,128)(2,1)S(1)}, u32[]{:S(2)}, u32[]{:S(2)}) %all-to-all-start.2) | async-done | bytes 1048608 | tf_op jit(solution)/shard_map/all_to_all | solution.py:208
  168.4 4.7 %collective-permute-start.11 = (bf16[128,4096]{1,0:T(8,128)(2,1)S(1)}, bf16[128,4096]{1,0:T(8,128)(2,1)S(1)}, u32[]{:S(2)}, u32[]{:S(2)}) collective-permute-start(bf16[128,4096]{1,0:T(8,128)(2,1)S(1)} %convolution_convert_fusion), channel_id=1, source_target_pairs={{0,1},{1,0},{2,3},{3,2},{4,5},{5,4},{6,7},{7,6},{8,9},{9,8},{10,11... | collective-permute-start | bytes 3145736 | tf_op jit(solution)/shard_map/ppermute | solution.py:18
  176.0 3.6 %collective-permute-start.15 = (bf16[24,4096]{1,0:T(8,128)(2,1)S(1)}, bf16[24,4096]{1,0:T(8,128)(2,1)S(1)}, u32[]{:S(2)}, u32[]{:S(2)}) collective-permute-start(bf16[24,4096]{1,0:T(8,128)(2,1)S(1)} %get-tuple-element.12), channel_id=1, source_target_pairs={{0,2},{1,3},{2,4},{3,5},{4,6},{5,7},{6,8},{7,9},{8,10},{9,11},{10,... | collective-permute-start | bytes 589832 | tf_op jit(solution)/shard_map/ppermute | solution.py:14
  179.6 2.8 %collective-permute-start.14 = (bf16[24,4096]{1,0:T(8,128)(2,1)S(1)}, bf16[24,4096]{1,0:T(8,128)(2,1)S(1)}, u32[]{:S(2)}, u32[]{:S(2)}) collective-permute-start(bf16[24,4096]{1,0:T(8,128)(2,1)S(1)} %get-tuple-element.13), channel_id=1, source_target_pairs={{0,30},{1,31},{2,0},{3,1},{4,2},{5,3},{6,4},{7,5},{8,6},{9,7},{10,... | collective-permute-start | bytes 589832 | tf_op jit(solution)/shard_map/ppermute | solution.py:14
  182.5 4.9 %collective-permute-start.13 = (bf16[24,4096]{1,0:T(8,128)(2,1)S(1)}, bf16[24,4096]{1,0:T(8,128)(2,1)S(1)}, u32[]{:S(2)}, u32[]{:S(2)}) collective-permute-start(bf16[24,4096]{1,0:T(8,128)(2,1)S(1)} %get-tuple-element.14), channel_id=1, source_target_pairs={{0,4},{1,5},{2,6},{3,7},{4,8},{5,9},{6,10},{7,11},{8,12},{9,13},{1... | collective-permute-start | bytes 589832 | tf_op jit(solution)/shard_map/ppermute | solution.py:14
  189.9 4.9 %collective-permute-start.17 = (bf16[8,4096]{1,0:T(8,128)(2,1)S(1)}, bf16[8,4096]{1,0:T(8,128)(2,1)S(1)}, u32[]{:S(2)}, u32[]{:S(2)}) collective-permute-start(bf16[8,4096]{1,0:T(8,128)(2,1)S(1)} %slice.191), channel_id=1, source_target_pairs={{0,6},{1,7},{2,8},{3,9},{4,10},{5,11},{6,12},{7,13},{8,14},{9,15},... | collective-permute-start | bytes 196616 | tf_op jit(solution)/shard_map/ppermute | solution.py:14
  200.8 8.5 %collective-permute-start.18 = (bf16[8,4096]{1,0:T(8,128)(2,1)S(1)}, bf16[8,4096]{1,0:T(8,128)(2,1)S(1)}, u32[]{:S(2)}, u32[]{:S(2)}) collective-permute-start(bf16[8,4096]{1,0:T(8,128)(2,1)S(1)} %fusion.8), channel_id=1, source_target_pairs={{0,10},{1,11},{2,12},{3,13},{4,14},{5,15},{6,16},{7,17},{8,18},{9,... | collective-permute-start | bytes 196616 | tf_op jit(solution)/shard_map/ppermute | solution.py:14
  212.4 7.6 %collective-permute-done.16 = bf16[8,4096]{1,0:T(8,128)(2,1)S(1)} collective-permute-done((bf16[8,4096]{1,0:T(8,128)(2,1)S(1)}, bf16[8,4096]{1,0:T(8,128)(2,1)S(1)}, u32[]{:S(2)}, u32[]{:S(2)}) %collective-permute-start.16) | collective-permute-done | bytes 65568 | tf_op jit(solution)/shard_map/ppermute | solution.py:14
  (71 shorter events, 35.7 us)
Async XLA Ops:
  1.6 17.8 %collective-permute-start = (bf16[8,4224]{1,0:T(8,128)(2,1)}, bf16[8,4224]{1,0:T(8,128)(2,1)S(1)}, u32[]{:S(2)}, u32[]{:S(2)}) collective-permute-start(bf16[8,4224]{1,0:T(8,128)(2,1)} %with_facts.1), channel_id=1, source_target_pairs={{0,10},{1,11},{2,12},{3,13},{4,14},{5,15},{6,16},{7,17},{8,18},{9,... | collective-permute-start | bytes 202760 | tf_op jit(solution)/shard_map/ppermute | solution.py:14
  12.6 11.3 %collective-permute-start.1 = (bf16[8,4224]{1,0:T(8,128)(2,1)}, bf16[8,4224]{1,0:T(8,128)(2,1)S(1)}, u32[]{:S(2)}, u32[]{:S(2)}) collective-permute-start(bf16[8,4224]{1,0:T(8,128)(2,1)} %with_facts.1), channel_id=1, source_target_pairs={{0,22},{1,23},{2,24},{3,25},{4,26},{5,27},{6,28},{7,29},{8,30},{9,... | collective-permute-start | bytes 202760 | tf_op jit(solution)/shard_map/ppermute | solution.py:14
  24.8 14.5 %collective-permute-start.2 = (bf16[24,4224]{1,0:T(8,128)(2,1)S(1)}, bf16[24,4224]{1,0:T(8,128)(2,1)S(1)}, u32[]{:S(2)}, u32[]{:S(2)}) collective-permute-start(bf16[24,4224]{1,0:T(8,128)(2,1)S(1)} %pad_maximum_fusion.5), channel_id=1, source_target_pairs={{0,2},{1,3},{2,4},{3,5},{4,6},{5,7},{6,8},{7,9},{8,10},{9,11},{10,... | collective-permute-start | bytes 608264 | tf_op jit(solution)/shard_map/ppermute | solution.py:14
  27.4 15.3 %collective-permute-start.3 = (bf16[24,4224]{1,0:T(8,128)(2,1)S(1)}, bf16[24,4224]{1,0:T(8,128)(2,1)S(1)}, u32[]{:S(2)}, u32[]{:S(2)}) collective-permute-start(bf16[24,4224]{1,0:T(8,128)(2,1)S(1)} %pad_maximum_fusion.5), channel_id=1, source_target_pairs={{0,30},{1,31},{2,0},{3,1},{4,2},{5,3},{6,4},{7,5},{8,6},{9,7},{10,... | collective-permute-start | bytes 608264 | tf_op jit(solution)/shard_map/ppermute | solution.py:14
  31.9 18.8 %collective-permute-start.6 = (bf16[8,4224]{1,0:T(8,128)(2,1)S(1)}, bf16[8,4224]{1,0:T(8,128)(2,1)S(1)}, u32[]{:S(2)}, u32[]{:S(2)}) collective-permute-start(bf16[8,4224]{1,0:T(8,128)(2,1)S(1)} %collective-permute-done.1), channel_id=1, source_target_pairs={{0,26},{1,27},{2,28},{3,29},{4,30},{5,31},{6,0},{7,1},{8,2},{9,3},... | collective-permute-start | bytes 202760 | tf_op jit(solution)/shard_map/ppermute | solution.py:14
  39.3 8.0 %collective-permute-start.4 = (bf16[24,4224]{1,0:T(8,128)(2,1)S(1)}, bf16[24,4224]{1,0:T(8,128)(2,1)S(1)}, u32[]{:S(2)}, u32[]{:S(2)}) collective-permute-start(bf16[24,4224]{1,0:T(8,128)(2,1)S(1)} %collective-permute-done.2), channel_id=1, source_target_pairs={{0,2},{1,3},{2,4},{3,5},{4,6},{5,7},{6,8},{7,9},{8,10},{9,11},{10,... | collective-permute-start | bytes 608264 | tf_op jit(solution)/shard_map/ppermute | solution.py:14
  42.7 7.9 %collective-permute-start.5 = (bf16[24,4224]{1,0:T(8,128)(2,1)S(1)}, bf16[24,4224]{1,0:T(8,128)(2,1)S(1)}, u32[]{:S(2)}, u32[]{:S(2)}) collective-permute-start(bf16[24,4224]{1,0:T(8,128)(2,1)S(1)} %collective-permute-done.3), channel_id=1, source_target_pairs={{0,30},{1,31},{2,0},{3,1},{4,2},{5,3},{6,4},{7,5},{8,6},{9,7},{10,... | collective-permute-start | bytes 608264 | tf_op jit(solution)/shard_map/ppermute | solution.py:14
  50.7 7.5 %collective-permute-start.7 = (bf16[128,4224]{1,0:T(8,128)(2,1)S(1)}, bf16[128,4224]{1,0:T(8,128)(2,1)S(1)}, u32[]{:S(2)}, u32[]{:S(2)}) collective-permute-start(bf16[128,4224]{1,0:T(8,128)(2,1)S(1)} %constant_dynamic-update-slice_fusion), channel_id=1, source_target_pairs={{0,1},{1,0},{2,3},{3,2},{4,5},{5,4},{6,7},{7,6},{8,9},{9,8},{10,11... | collective-permute-start | bytes 3244040 | tf_op jit(solution)/shard_map/ppermute | solution.py:18
  62.1 8.5 %copy-start.1 = (bf16[1,4096,128]{2,1,0:T(8,128)(2,1)S(1)}, bf16[1,4096,128]{2,1,0:T(8,128)(2,1)}, u32[]{:S(2)}) copy-start(bf16[1,4096,128]{2,1,0:T(8,128)(2,1)} %param.11) | copy-start | bytes 3145732
  62.1 56.7 %all-to-all-start = ((bf16[8,64,4096]{2,1,0:T(8,128)(2,1)}), bf16[8,64,4096]{2,1,0:T(8,128)(2,1)}, u32[]{:S(2)}, u32[]{:S(2)}) async-start(bf16[8,64,4096]{2,1,0:T(8,128)(2,1)} %bitcast.90), calls=%async_computation | async-start | bytes 8388608 | tf_op jit(solution)/shard_map/all_to_all | solution.py:199
  68.6 52.1 %collective-permute-start.8 = (bf16[4096,128]{1,0:T(8,128)(2,1)S(1)}, bf16[4096,128]{1,0:T(8,128)(2,1)S(1)}, u32[]{:S(2)}, u32[]{:S(2)}) collective-permute-start(bf16[4096,128]{1,0:T(8,128)(2,1)S(1)} %bitcast.86), channel_id=1, source_target_pairs={{0,32},{32,0},{64,96},{96,64},{128,160},{160,128},{192,224},{224,1... | collective-permute-start | bytes 3145736 | tf_op jit(solution)/shard_map/ppermute | solution.py:22
  70.5 50.2 %collective-permute-start.9 = (bf16[4096,128]{1,0:T(8,128)(2,1)S(1)}, bf16[4096,128]{1,0:T(8,128)(2,1)}, u32[]{:S(2)}, u32[]{:S(2)}) collective-permute-start(bf16[4096,128]{1,0:T(8,128)(2,1)S(1)} %bitcast.88), channel_id=1, source_target_pairs={{0,32},{32,0},{64,96},{96,64},{128,160},{160,128},{192,224},{224,1... | collective-permute-start | bytes 3145736 | tf_op jit(solution)/shard_map/ppermute | solution.py:22
  118.8 25.3 %collective-permute-start.10 = (bf16[1024,512]{1,0:T(8,128)(2,1)}, bf16[1024,512]{1,0:T(8,128)(2,1)}, u32[]{:S(2)}, u32[]{:S(2)}) collective-permute-start(bf16[1024,512]{1,0:T(8,128)(2,1)} %bitcast.92), channel_id=1, source_target_pairs={{0,32},{32,0},{64,96},{96,64},{128,160},{160,128},{192,224},{224,1... | collective-permute-start | bytes 3145736 | tf_op jit(solution)/shard_map/ppermute | solution.py:22
  148.2 19.6 %all-to-all-start.2 = ((bf16[8,64,1024]{2,1,0:T(8,128)(2,1)}), bf16[8,64,1024]{2,1,0:T(8,128)(2,1)S(1)}, u32[]{:S(2)}, u32[]{:S(2)}) async-start(bf16[8,64,1024]{2,1,0:T(8,128)(2,1)} %back.1), calls=%async_computation.2 | async-start | bytes 2097152 | tf_op jit(solution)/shard_map/all_to_all | solution.py:208
  168.4 7.0 %collective-permute-start.11 = (bf16[128,4096]{1,0:T(8,128)(2,1)S(1)}, bf16[128,4096]{1,0:T(8,128)(2,1)S(1)}, u32[]{:S(2)}, u32[]{:S(2)}) collective-permute-start(bf16[128,4096]{1,0:T(8,128)(2,1)S(1)} %convolution_convert_fusion), channel_id=1, source_target_pairs={{0,1},{1,0},{2,3},{3,2},{4,5},{5,4},{6,7},{7,6},{8,9},{9,8},{10,11... | collective-permute-start | bytes 3145736 | tf_op jit(solution)/shard_map/ppermute | solution.py:18
  175.9 44.0 %copy-start.2 = (bf16[8,4096]{1,0:T(8,128)(2,1)S(1)}, bf16[8,4096]{1,0:T(8,128)(2,1)}, u32[]{:S(2)}) copy-start(bf16[8,4096]{1,0:T(8,128)(2,1)} %tokens_ref.1) | copy-start | bytes 196612
  175.9 44.2 %copy-start.3 = (f32[4096]{0:T(1024)S(1)}, f32[4096]{0:T(1024)}, u32[]{:S(2)}) copy-start(f32[4096]{0:T(1024)} %param.13) | copy-start | bytes 49156
  176.0 18.8 %collective-permute-start.15 = (bf16[24,4096]{1,0:T(8,128)(2,1)S(1)}, bf16[24,4096]{1,0:T(8,128)(2,1)S(1)}, u32[]{:S(2)}, u32[]{:S(2)}) collective-permute-start(bf16[24,4096]{1,0:T(8,128)(2,1)S(1)} %get-tuple-element.12), channel_id=1, source_target_pairs={{0,2},{1,3},{2,4},{3,5},{4,6},{5,7},{6,8},{7,9},{8,10},{9,11},{10,... | collective-permute-start | bytes 589832 | tf_op jit(solution)/shard_map/ppermute | solution.py:14
  179.6 15.2 %collective-permute-start.14 = (bf16[24,4096]{1,0:T(8,128)(2,1)S(1)}, bf16[24,4096]{1,0:T(8,128)(2,1)S(1)}, u32[]{:S(2)}, u32[]{:S(2)}) collective-permute-start(bf16[24,4096]{1,0:T(8,128)(2,1)S(1)} %get-tuple-element.13), channel_id=1, source_target_pairs={{0,30},{1,31},{2,0},{3,1},{4,2},{5,3},{6,4},{7,5},{8,6},{9,7},{10,... | collective-permute-start | bytes 589832 | tf_op jit(solution)/shard_map/ppermute | solution.py:14
  182.5 14.9 %collective-permute-start.13 = (bf16[24,4096]{1,0:T(8,128)(2,1)S(1)}, bf16[24,4096]{1,0:T(8,128)(2,1)S(1)}, u32[]{:S(2)}, u32[]{:S(2)}) collective-permute-start(bf16[24,4096]{1,0:T(8,128)(2,1)S(1)} %get-tuple-element.14), channel_id=1, source_target_pairs={{0,4},{1,5},{2,6},{3,7},{4,8},{5,9},{6,10},{7,11},{8,12},{9,13},{1... | collective-permute-start | bytes 589832 | tf_op jit(solution)/shard_map/ppermute | solution.py:14
  187.4 12.8 %collective-permute-start.12 = (bf16[24,4096]{1,0:T(8,128)(2,1)S(1)}, bf16[24,4096]{1,0:T(8,128)(2,1)S(1)}, u32[]{:S(2)}, u32[]{:S(2)}) collective-permute-start(bf16[24,4096]{1,0:T(8,128)(2,1)S(1)} %get-tuple-element.11), channel_id=1, source_target_pairs={{0,28},{1,29},{2,30},{3,31},{4,0},{5,1},{6,2},{7,3},{8,4},{9,5},{1... | collective-permute-start | bytes 589832 | tf_op jit(solution)/shard_map/ppermute | solution.py:14
  189.9 10.9 %collective-permute-start.17 = (bf16[8,4096]{1,0:T(8,128)(2,1)S(1)}, bf16[8,4096]{1,0:T(8,128)(2,1)S(1)}, u32[]{:S(2)}, u32[]{:S(2)}) collective-permute-start(bf16[8,4096]{1,0:T(8,128)(2,1)S(1)} %slice.191), channel_id=1, source_target_pairs={{0,6},{1,7},{2,8},{3,9},{4,10},{5,11},{6,12},{7,13},{8,14},{9,15},... | collective-permute-start | bytes 196616 | tf_op jit(solution)/shard_map/ppermute | solution.py:14
  200.8 11.5 %collective-permute-start.18 = (bf16[8,4096]{1,0:T(8,128)(2,1)S(1)}, bf16[8,4096]{1,0:T(8,128)(2,1)S(1)}, u32[]{:S(2)}, u32[]{:S(2)}) collective-permute-start(bf16[8,4096]{1,0:T(8,128)(2,1)S(1)} %fusion.8), channel_id=1, source_target_pairs={{0,10},{1,11},{2,12},{3,13},{4,14},{5,15},{6,16},{7,17},{8,18},{9,... | collective-permute-start | bytes 196616 | tf_op jit(solution)/shard_map/ppermute | solution.py:14
  209.4 10.6 %collective-permute-start.16 = (bf16[8,4096]{1,0:T(8,128)(2,1)S(1)}, bf16[8,4096]{1,0:T(8,128)(2,1)S(1)}, u32[]{:S(2)}, u32[]{:S(2)}) collective-permute-start(bf16[8,4096]{1,0:T(8,128)(2,1)S(1)} %slice.292), channel_id=1, source_target_pairs={{0,22},{1,23},{2,24},{3,25},{4,26},{5,27},{6,28},{7,29},{8,30},{9,... | collective-permute-start | bytes 196616 | tf_op jit(solution)/shard_map/ppermute | solution.py:14
  (1 other events, 6.5 us)

commit v8 on v6

--- a/solution.py
+++ b/solution.py
@@ -77,7 +77,7 @@
 
 def front(odd, rows, gates, ups):
     count, width = rows.shape
-    units, block = gates[0].shape[1], 1024
+    units, block = gates[0].shape[1], 2048
     steps = width // block
 
     def kernel(odd_ref, rows_ref, gate_own, gate_other, up_own, up_other, out_ref, total):
@@ -113,6 +113,7 @@
         out_specs=whole((4, count, 2 * units)),
         out_shape=jax.ShapeDtypeStruct((4, count, 2 * units), BF16),
         scratch_shapes=[pltpu.VMEM((count, 4 * units), F32)],
+        compiler_params=pltpu.CompilerParams(vmem_limit_bytes=32 * 2**20),
         name="front",
     )(odd, rows, *gates, *ups)
 

time: 221 us -> 218 us (0.986)
  transfers between devices with their start and end apart: 21 -> 21, of which waited for: 13 -> 13; matrix products, arithmetic and copies ran while one was open for 1% -> 1% of each run, Pallas kernels for 3% -> 2%
where the time goes in v8:
time: 218 us; the launch traced here: 216 us
  starting transfers between devices  97.1 us (45%)
  waiting for transfers between devices  83.4 us (38%)
  blocking collectives  16.5 us (8%)
  Pallas kernels  10.2 us (5%)
  local copies, waits for them, and re-layouts  3.83 us (2%)
  other arithmetic  2.3 us (1%)
  matrix products  2.21 us (1%)
    ppermute x14, starting transfers between devices, around(): lax.ppermute(block, 'ep', [(i, (i + 2 * chips) % size) for i in range(siz...  67.8 us
    all_to_all x1, waiting for transfers between devices, shards(): lax.all_to_all(fanned, 'grp', split_axis=0, concat_axis=0, tiled=True, ax...  24.1 us
    ppermute x3, waiting for transfers between devices, pair_swap(): lax.ppermute(block, 'grp', [(i, i ^ 1) for i in range(lax.axis_size('grp'...  20.7 us
    ppermute x14, waiting for transfers between devices, around(): lax.ppermute(block, 'ep', [(i, (i + 2 * chips) % size) for i in range(siz...  19.8 us
    all_to_all x1, blocking collectives, shards(): lax.all_to_all(hidden, 'grp', split_axis=0, concat_axis=0, tiled=True, ax...  16.5 us
    all_to_all x1, waiting for transfers between devices, shards(): lax.all_to_all(out, 'grp', split_axis=0, concat_axis=0, tiled=True, axis_...  14.4 us
    ppermute x2, starting transfers between devices, core_swap(): lax.ppermute(block, 'ep', [(i, i ^ 1) for i in range(lax.axis_size('ep'))])  10.4 us
    ppermute x3, starting transfers between devices, pair_swap(): lax.ppermute(block, 'grp', [(i, i ^ 1) for i in range(lax.axis_size('grp'...  8.41 us
  transfers between devices with their start and end apart: 21, of which 13 were waited for; matrix products, arithmetic and copies ran while one was open for 1% of the time, Pallas kernels for 2%

profile of v8, /device:TPU:1, one launch (start us, length us, event | category | flops | bytes accessed | tf_op | source)
XLA Modules:
  0.0 216.0 jit_solution(15127200823655447067)
XLA Ops:
  1.6 11.0 %collective-permute-start = (bf16[8,4224]{1,0:T(8,128)(2,1)}, bf16[8,4224]{1,0:T(8,128)(2,1)S(1)}, u32[]{:S(2)}, u32[]{:S(2)}) collective-permute-start(bf16[8,4224]{1,0:T(8,128)(2,1)} %with_facts.1), channel_id=1, source_target_pairs={{0,10},{1,11},{2,12},{3,13},{4,14},{5,15},{6,16},{7,17},{8,18},{9,... | collective-permute-start | bytes 202760 | tf_op jit(solution)/shard_map/ppermute | solution.py:14
  12.6 5.9 %collective-permute-start.1 = (bf16[8,4224]{1,0:T(8,128)(2,1)}, bf16[8,4224]{1,0:T(8,128)(2,1)S(1)}, u32[]{:S(2)}, u32[]{:S(2)}) collective-permute-start(bf16[8,4224]{1,0:T(8,128)(2,1)} %with_facts.1), channel_id=1, source_target_pairs={{0,22},{1,23},{2,24},{3,25},{4,26},{5,27},{6,28},{7,29},{8,30},{9,... | collective-permute-start | bytes 202760 | tf_op jit(solution)/shard_map/ppermute | solution.py:14
  18.5 3.1 %collective-permute-start.7 = (bf16[4096,128]{1,0:T(8,128)(2,1)}, bf16[4096,128]{1,0:T(8,128)(2,1)S(1)}, u32[]{:S(2)}, u32[]{:S(2)}) collective-permute-start(bf16[4096,128]{1,0:T(8,128)(2,1)} %bitcast.86), channel_id=1, source_target_pairs={{0,32},{32,0},{64,96},{96,64},{128,160},{160,128},{192,224},{224,1... | collective-permute-start | bytes 3145736 | tf_op jit(solution)/shard_map/ppermute | solution.py:22
  27.4 4.5 %collective-permute-start.3 = (bf16[24,4224]{1,0:T(8,128)(2,1)S(1)}, bf16[24,4224]{1,0:T(8,128)(2,1)S(1)}, u32[]{:S(2)}, u32[]{:S(2)}) collective-permute-start(bf16[24,4224]{1,0:T(8,128)(2,1)S(1)} %pad_maximum_fusion.5), channel_id=1, source_target_pairs={{0,30},{1,31},{2,0},{3,1},{4,2},{5,3},{6,4},{7,5},{8,6},{9,7},{10,... | collective-permute-start | bytes 608264 | tf_op jit(solution)/shard_map/ppermute | solution.py:14
  31.9 7.4 %collective-permute-start.6 = (bf16[8,4224]{1,0:T(8,128)(2,1)S(1)}, bf16[8,4224]{1,0:T(8,128)(2,1)S(1)}, u32[]{:S(2)}, u32[]{:S(2)}) collective-permute-start(bf16[8,4224]{1,0:T(8,128)(2,1)S(1)} %collective-permute-done.1), channel_id=1, source_target_pairs={{0,26},{1,27},{2,28},{3,29},{4,30},{5,31},{6,0},{7,1},{8,2},{9,3},... | collective-permute-start | bytes 202760 | tf_op jit(solution)/shard_map/ppermute | solution.py:14
  39.3 3.4 %collective-permute-start.4 = (bf16[24,4224]{1,0:T(8,128)(2,1)S(1)}, bf16[24,4224]{1,0:T(8,128)(2,1)S(1)}, u32[]{:S(2)}, u32[]{:S(2)}) collective-permute-start(bf16[24,4224]{1,0:T(8,128)(2,1)S(1)} %collective-permute-done.2), channel_id=1, source_target_pairs={{0,2},{1,3},{2,4},{3,5},{4,6},{5,7},{6,8},{7,9},{8,10},{9,11},{10,... | collective-permute-start | bytes 608264 | tf_op jit(solution)/shard_map/ppermute | solution.py:14
  42.7 3.1 %collective-permute-start.5 = (bf16[24,4224]{1,0:T(8,128)(2,1)S(1)}, bf16[24,4224]{1,0:T(8,128)(2,1)S(1)}, u32[]{:S(2)}, u32[]{:S(2)}) collective-permute-start(bf16[24,4224]{1,0:T(8,128)(2,1)S(1)} %collective-permute-done.3), channel_id=1, source_target_pairs={{0,30},{1,31},{2,0},{3,1},{4,2},{5,3},{6,4},{7,5},{8,6},{9,7},{10,... | collective-permute-start | bytes 608264 | tf_op jit(solution)/shard_map/ppermute | solution.py:14
  47.3 3.3 %collective-permute-done.5 = bf16[24,4224]{1,0:T(8,128)(2,1)S(1)} collective-permute-done((bf16[24,4224]{1,0:T(8,128)(2,1)S(1)}, bf16[24,4224]{1,0:T(8,128)(2,1)S(1)}, u32[]{:S(2)}, u32[]{:S(2)}) %collective-permute-start.5) | collective-permute-done | bytes 202784 | tf_op jit(solution)/shard_map/ppermute | solution.py:14
  50.7 5.1 %collective-permute-start.8 = (bf16[128,4224]{1,0:T(8,128)(2,1)S(1)}, bf16[128,4224]{1,0:T(8,128)(2,1)S(1)}, u32[]{:S(2)}, u32[]{:S(2)}) collective-permute-start(bf16[128,4224]{1,0:T(8,128)(2,1)S(1)} %constant_dynamic-update-slice_fusion), channel_id=1, source_target_pairs={{0,1},{1,0},{2,3},{3,2},{4,5},{5,4},{6,7},{7,6},{8,9},{9,8},{10,11... | collective-permute-start | bytes 3244040 | tf_op jit(solution)/shard_map/ppermute | solution.py:18
  62.1 6.5 %all-to-all-start = ((bf16[8,64,4096]{2,1,0:T(8,128)(2,1)}), bf16[8,64,4096]{2,1,0:T(8,128)(2,1)}, u32[]{:S(2)}, u32[]{:S(2)}) async-start(bf16[8,64,4096]{2,1,0:T(8,128)(2,1)} %bitcast.90), calls=%async_computation | async-start | bytes 8388608 | tf_op jit(solution)/shard_map/all_to_all | solution.py:200
  70.6 3.4 %collective-permute-start.10 = (bf16[1024,512]{1,0:T(8,128)(2,1)}, bf16[1024,512]{1,0:T(8,128)(2,1)}, u32[]{:S(2)}, u32[]{:S(2)}) collective-permute-start(bf16[1024,512]{1,0:T(8,128)(2,1)} %bitcast.92), channel_id=1, source_target_pairs={{0,32},{32,0},{64,96},{96,64},{128,160},{160,128},{192,224},{224,1... | collective-permute-start | bytes 3145736 | tf_op jit(solution)/shard_map/ppermute | solution.py:22
  73.9 20.7 %collective-permute-done.9.up_other = bf16[4096,128]{1,0:T(8,128)(2,1)} collective-permute-done((bf16[4096,128]{1,0:T(8,128)(2,1)S(1)}, bf16[4096,128]{1,0:T(8,128)(2,1)}, u32[]{:S(2)}, u32[]{:S(2)}) %collective-permute-start.9) | collective-permute-done | bytes 1048608 | tf_op jit(solution)/shard_map/ppermute | solution.py:22
  94.7 24.1 %all-to-all-done = bf16[8,64,4096]{2,1,0:T(8,128)(2,1)} async-done(((bf16[8,64,4096]{2,1,0:T(8,128)(2,1)}), bf16[8,64,4096]{2,1,0:T(8,128)(2,1)}, u32[]{:S(2)}, u32[]{:S(2)}) %all-to-all-start) | async-done | bytes 4194336 | tf_op jit(solution)/shard_map/all_to_all | solution.py:200
  118.8 4.5 %front.1 = bf16[4,512,256]{2,1,0:T(8,128)(2,1)S(1)} custom-call(s32[1]{0:T(128)} %bitcast.4.odd_ref, bf16[512,4096]{1,0:T(8,128)(2,1)} %bitcast.7.rows_ref, bf16[4096,128]{1,0:T(8,128)(2,1)S(1)} %bitcast.87, bf16[4096,128]{1,0:T(8,128)(2,1)S(1)} %collective-permute-done.7.gate_other, bf16[4096,128]{1,0:T(8,128)(2,1)S(1)} %bitcast.89, ...), custom_call_target="tpu_custom_call" | custom-call | tf_op jit(solution)/shard_map/front/pallas_call | solution.py:105
  123.3 16.5 %all_to_all.15.hidden_ref = bf16[4,512,256]{2,1,0:T(8,128)(2,1)} all-to-all(bf16[4,512,256]{2,1,0:T(8,128)(2,1)S(1)} %front.1), channel_id=1, replica_groups={{0,96,128,224},{256,352,384,480},{32,64,160,192},{288,320,416,448},{1,9..., dimensions={0} | all-to-all | bytes 2097152 | tf_op jit(solution)/shard_map/all_to_all | solution.py:205
  139.9 4.1 %back.1 = bf16[8,64,1024]{2,1,0:T(8,128)(2,1)} custom-call(s32[1]{0:T(128)} %bitcast.4.odd_ref, bf16[4,512,256]{2,1,0:T(8,128)(2,1)} %all_to_all.15.hidden_ref, bf16[1024,512]{1,0:T(8,128)(2,1)} %bitcast.93, bf16[1024,512]{1,0:T(8,128)(2,1)} %collective-permute-done.10.other_ref), custom_call_target="tpu_custom_call" | custom-call | tf_op jit(solution)/shard_map/back/pallas_call | solution.py:147
  143.9 4.0 %all-to-all-start.2 = ((bf16[8,64,1024]{2,1,0:T(8,128)(2,1)}), bf16[8,64,1024]{2,1,0:T(8,128)(2,1)S(1)}, u32[]{:S(2)}, u32[]{:S(2)}) async-start(bf16[8,64,1024]{2,1,0:T(8,128)(2,1)} %back.1), calls=%async_computation.2 | async-start | bytes 2097152 | tf_op jit(solution)/shard_map/all_to_all | solution.py:208
  148.1 14.4 %all-to-all-done.2 = bf16[8,64,1024]{2,1,0:T(8,128)(2,1)S(1)} async-done(((bf16[8,64,1024]{2,1,0:T(8,128)(2,1)}), bf16[8,64,1024]{2,1,0:T(8,128)(2,1)S(1)}, u32[]{:S(2)}, u32[]{:S(2)}) %all-to-all-start.2) | async-done | bytes 1048608 | tf_op jit(solution)/shard_map/all_to_all | solution.py:208
  163.1 5.2 %collective-permute-start.11 = (bf16[128,4096]{1,0:T(8,128)(2,1)S(1)}, bf16[128,4096]{1,0:T(8,128)(2,1)S(1)}, u32[]{:S(2)}, u32[]{:S(2)}) collective-permute-start(bf16[128,4096]{1,0:T(8,128)(2,1)S(1)} %convolution_convert_fusion), channel_id=1, source_target_pairs={{0,1},{1,0},{2,3},{3,2},{4,5},{5,4},{6,7},{7,6},{8,9},{9,8},{10,11... | collective-permute-start | bytes 3145736 | tf_op jit(solution)/shard_map/ppermute | solution.py:18
  171.2 3.6 %collective-permute-start.15 = (bf16[24,4096]{1,0:T(8,128)(2,1)S(1)}, bf16[24,4096]{1,0:T(8,128)(2,1)S(1)}, u32[]{:S(2)}, u32[]{:S(2)}) collective-permute-start(bf16[24,4096]{1,0:T(8,128)(2,1)S(1)} %get-tuple-element.16), channel_id=1, source_target_pairs={{0,2},{1,3},{2,4},{3,5},{4,6},{5,7},{6,8},{7,9},{8,10},{9,11},{10,... | collective-permute-start | bytes 589832 | tf_op jit(solution)/shard_map/ppermute | solution.py:14
  177.7 4.9 %collective-permute-start.13 = (bf16[24,4096]{1,0:T(8,128)(2,1)S(1)}, bf16[24,4096]{1,0:T(8,128)(2,1)S(1)}, u32[]{:S(2)}, u32[]{:S(2)}) collective-permute-start(bf16[24,4096]{1,0:T(8,128)(2,1)S(1)} %get-tuple-element.18), channel_id=1, source_target_pairs={{0,4},{1,5},{2,6},{3,7},{4,8},{5,9},{6,10},{7,11},{8,12},{9,13},{1... | collective-permute-start | bytes 589832 | tf_op jit(solution)/shard_map/ppermute | solution.py:14
  185.1 4.9 %collective-permute-start.17 = (bf16[8,4096]{1,0:T(8,128)(2,1)S(1)}, bf16[8,4096]{1,0:T(8,128)(2,1)S(1)}, u32[]{:S(2)}, u32[]{:S(2)}) collective-permute-start(bf16[8,4096]{1,0:T(8,128)(2,1)S(1)} %slice.189), channel_id=1, source_target_pairs={{0,6},{1,7},{2,8},{3,9},{4,10},{5,11},{6,12},{7,13},{8,14},{9,15},... | collective-permute-start | bytes 196616 | tf_op jit(solution)/shard_map/ppermute | solution.py:14
  196.0 8.6 %collective-permute-start.18 = (bf16[8,4096]{1,0:T(8,128)(2,1)S(1)}, bf16[8,4096]{1,0:T(8,128)(2,1)S(1)}, u32[]{:S(2)}, u32[]{:S(2)}) collective-permute-start(bf16[8,4096]{1,0:T(8,128)(2,1)S(1)} %fusion.8), channel_id=1, source_target_pairs={{0,10},{1,11},{2,12},{3,13},{4,14},{5,15},{6,16},{7,17},{8,18},{9,... | collective-permute-start | bytes 196616 | tf_op jit(solution)/shard_map/ppermute | solution.py:14
  207.8 7.4 %collective-permute-done.16 = bf16[8,4096]{1,0:T(8,128)(2,1)S(1)} collective-permute-done((bf16[8,4096]{1,0:T(8,128)(2,1)S(1)}, bf16[8,4096]{1,0:T(8,128)(2,1)S(1)}, u32[]{:S(2)}, u32[]{:S(2)}) %collective-permute-start.16) | collective-permute-done | bytes 65568 | tf_op jit(solution)/shard_map/ppermute | solution.py:14
  (71 shorter events, 35.9 us)
Async XLA Ops:
  1.6 20.9 %collective-permute-start = (bf16[8,4224]{1,0:T(8,128)(2,1)}, bf16[8,4224]{1,0:T(8,128)(2,1)S(1)}, u32[]{:S(2)}, u32[]{:S(2)}) collective-permute-start(bf16[8,4224]{1,0:T(8,128)(2,1)} %with_facts.1), channel_id=1, source_target_pairs={{0,10},{1,11},{2,12},{3,13},{4,14},{5,15},{6,16},{7,17},{8,18},{9,... | collective-permute-start | bytes 202760 | tf_op jit(solution)/shard_map/ppermute | solution.py:14
  12.6 11.3 %collective-permute-start.1 = (bf16[8,4224]{1,0:T(8,128)(2,1)}, bf16[8,4224]{1,0:T(8,128)(2,1)S(1)}, u32[]{:S(2)}, u32[]{:S(2)}) collective-permute-start(bf16[8,4224]{1,0:T(8,128)(2,1)} %with_facts.1), channel_id=1, source_target_pairs={{0,22},{1,23},{2,24},{3,25},{4,26},{5,27},{6,28},{7,29},{8,30},{9,... | collective-permute-start | bytes 202760 | tf_op jit(solution)/shard_map/ppermute | solution.py:14
  18.5 32.2 %collective-permute-start.7 = (bf16[4096,128]{1,0:T(8,128)(2,1)}, bf16[4096,128]{1,0:T(8,128)(2,1)S(1)}, u32[]{:S(2)}, u32[]{:S(2)}) collective-permute-start(bf16[4096,128]{1,0:T(8,128)(2,1)} %bitcast.86), channel_id=1, source_target_pairs={{0,32},{32,0},{64,96},{96,64},{128,160},{160,128},{192,224},{224,1... | collective-permute-start | bytes 3145736 | tf_op jit(solution)/shard_map/ppermute | solution.py:22
  24.8 14.5 %collective-permute-start.2 = (bf16[24,4224]{1,0:T(8,128)(2,1)S(1)}, bf16[24,4224]{1,0:T(8,128)(2,1)S(1)}, u32[]{:S(2)}, u32[]{:S(2)}) collective-permute-start(bf16[24,4224]{1,0:T(8,128)(2,1)S(1)} %pad_maximum_fusion.5), channel_id=1, source_target_pairs={{0,2},{1,3},{2,4},{3,5},{4,6},{5,7},{6,8},{7,9},{8,10},{9,11},{10,... | collective-permute-start | bytes 608264 | tf_op jit(solution)/shard_map/ppermute | solution.py:14
  27.4 15.3 %collective-permute-start.3 = (bf16[24,4224]{1,0:T(8,128)(2,1)S(1)}, bf16[24,4224]{1,0:T(8,128)(2,1)S(1)}, u32[]{:S(2)}, u32[]{:S(2)}) collective-permute-start(bf16[24,4224]{1,0:T(8,128)(2,1)S(1)} %pad_maximum_fusion.5), channel_id=1, source_target_pairs={{0,30},{1,31},{2,0},{3,1},{4,2},{5,3},{6,4},{7,5},{8,6},{9,7},{10,... | collective-permute-start | bytes 608264 | tf_op jit(solution)/shard_map/ppermute | solution.py:14
  31.9 18.8 %collective-permute-start.6 = (bf16[8,4224]{1,0:T(8,128)(2,1)S(1)}, bf16[8,4224]{1,0:T(8,128)(2,1)S(1)}, u32[]{:S(2)}, u32[]{:S(2)}) collective-permute-start(bf16[8,4224]{1,0:T(8,128)(2,1)S(1)} %collective-permute-done.1), channel_id=1, source_target_pairs={{0,26},{1,27},{2,28},{3,29},{4,30},{5,31},{6,0},{7,1},{8,2},{9,3},... | collective-permute-start | bytes 202760 | tf_op jit(solution)/shard_map/ppermute | solution.py:14
  39.3 8.0 %collective-permute-start.4 = (bf16[24,4224]{1,0:T(8,128)(2,1)S(1)}, bf16[24,4224]{1,0:T(8,128)(2,1)S(1)}, u32[]{:S(2)}, u32[]{:S(2)}) collective-permute-start(bf16[24,4224]{1,0:T(8,128)(2,1)S(1)} %collective-permute-done.2), channel_id=1, source_target_pairs={{0,2},{1,3},{2,4},{3,5},{4,6},{5,7},{6,8},{7,9},{8,10},{9,11},{10,... | collective-permute-start | bytes 608264 | tf_op jit(solution)/shard_map/ppermute | solution.py:14
  42.7 7.9 %collective-permute-start.5 = (bf16[24,4224]{1,0:T(8,128)(2,1)S(1)}, bf16[24,4224]{1,0:T(8,128)(2,1)S(1)}, u32[]{:S(2)}, u32[]{:S(2)}) collective-permute-start(bf16[24,4224]{1,0:T(8,128)(2,1)S(1)} %collective-permute-done.3), channel_id=1, source_target_pairs={{0,30},{1,31},{2,0},{3,1},{4,2},{5,3},{6,4},{7,5},{8,6},{9,7},{10,... | collective-permute-start | bytes 608264 | tf_op jit(solution)/shard_map/ppermute | solution.py:14
  50.7 7.5 %collective-permute-start.8 = (bf16[128,4224]{1,0:T(8,128)(2,1)S(1)}, bf16[128,4224]{1,0:T(8,128)(2,1)S(1)}, u32[]{:S(2)}, u32[]{:S(2)}) collective-permute-start(bf16[128,4224]{1,0:T(8,128)(2,1)S(1)} %constant_dynamic-update-slice_fusion), channel_id=1, source_target_pairs={{0,1},{1,0},{2,3},{3,2},{4,5},{5,4},{6,7},{7,6},{8,9},{9,8},{10,11... | collective-permute-start | bytes 3244040 | tf_op jit(solution)/shard_map/ppermute | solution.py:18
  62.1 56.7 %copy-start = (bf16[1,4096,128]{2,1,0:T(8,128)(2,1)S(1)}, bf16[1,4096,128]{2,1,0:T(8,128)(2,1)}, u32[]{:S(2)}) copy-start(bf16[1,4096,128]{2,1,0:T(8,128)(2,1)} %param.10) | copy-start | bytes 3145732
  62.1 56.7 %all-to-all-start = ((bf16[8,64,4096]{2,1,0:T(8,128)(2,1)}), bf16[8,64,4096]{2,1,0:T(8,128)(2,1)}, u32[]{:S(2)}, u32[]{:S(2)}) async-start(bf16[8,64,4096]{2,1,0:T(8,128)(2,1)} %bitcast.90), calls=%async_computation | async-start | bytes 8388608 | tf_op jit(solution)/shard_map/all_to_all | solution.py:200
  68.6 26.1 %collective-permute-start.9 = (bf16[4096,128]{1,0:T(8,128)(2,1)S(1)}, bf16[4096,128]{1,0:T(8,128)(2,1)}, u32[]{:S(2)}, u32[]{:S(2)}) collective-permute-start(bf16[4096,128]{1,0:T(8,128)(2,1)S(1)} %bitcast.88), channel_id=1, source_target_pairs={{0,32},{32,0},{64,96},{96,64},{128,160},{160,128},{192,224},{224,1... | collective-permute-start | bytes 3145736 | tf_op jit(solution)/shard_map/ppermute | solution.py:22
  70.6 52.8 %collective-permute-start.10 = (bf16[1024,512]{1,0:T(8,128)(2,1)}, bf16[1024,512]{1,0:T(8,128)(2,1)}, u32[]{:S(2)}, u32[]{:S(2)}) collective-permute-start(bf16[1024,512]{1,0:T(8,128)(2,1)} %bitcast.92), channel_id=1, source_target_pairs={{0,32},{32,0},{64,96},{96,64},{128,160},{160,128},{192,224},{224,1... | collective-permute-start | bytes 3145736 | tf_op jit(solution)/shard_map/ppermute | solution.py:22
  143.9 18.6 %all-to-all-start.2 = ((bf16[8,64,1024]{2,1,0:T(8,128)(2,1)}), bf16[8,64,1024]{2,1,0:T(8,128)(2,1)S(1)}, u32[]{:S(2)}, u32[]{:S(2)}) async-start(bf16[8,64,1024]{2,1,0:T(8,128)(2,1)} %back.1), calls=%async_computation.2 | async-start | bytes 2097152 | tf_op jit(solution)/shard_map/all_to_all | solution.py:208
  163.1 7.5 %collective-permute-start.11 = (bf16[128,4096]{1,0:T(8,128)(2,1)S(1)}, bf16[128,4096]{1,0:T(8,128)(2,1)S(1)}, u32[]{:S(2)}, u32[]{:S(2)}) collective-permute-start(bf16[128,4096]{1,0:T(8,128)(2,1)S(1)} %convolution_convert_fusion), channel_id=1, source_target_pairs={{0,1},{1,0},{2,3},{3,2},{4,5},{5,4},{6,7},{7,6},{8,9},{9,8},{10,11... | collective-permute-start | bytes 3145736 | tf_op jit(solution)/shard_map/ppermute | solution.py:18
  171.1 44.0 %copy-start.2 = (bf16[8,4096]{1,0:T(8,128)(2,1)S(1)}, bf16[8,4096]{1,0:T(8,128)(2,1)}, u32[]{:S(2)}) copy-start(bf16[8,4096]{1,0:T(8,128)(2,1)} %tokens_ref.1) | copy-start | bytes 196612
  171.1 44.2 %copy-start.3 = (f32[4096]{0:T(1024)S(1)}, f32[4096]{0:T(1024)}, u32[]{:S(2)}) copy-start(f32[4096]{0:T(1024)} %param.13) | copy-start | bytes 49156
  171.2 18.8 %collective-permute-start.15 = (bf16[24,4096]{1,0:T(8,128)(2,1)S(1)}, bf16[24,4096]{1,0:T(8,128)(2,1)S(1)}, u32[]{:S(2)}, u32[]{:S(2)}) collective-permute-start(bf16[24,4096]{1,0:T(8,128)(2,1)S(1)} %get-tuple-element.16), channel_id=1, source_target_pairs={{0,2},{1,3},{2,4},{3,5},{4,6},{5,7},{6,8},{7,9},{8,10},{9,11},{10,... | collective-permute-start | bytes 589832 | tf_op jit(solution)/shard_map/ppermute | solution.py:14
  174.8 15.2 %collective-permute-start.14 = (bf16[24,4096]{1,0:T(8,128)(2,1)S(1)}, bf16[24,4096]{1,0:T(8,128)(2,1)S(1)}, u32[]{:S(2)}, u32[]{:S(2)}) collective-permute-start(bf16[24,4096]{1,0:T(8,128)(2,1)S(1)} %get-tuple-element.17), channel_id=1, source_target_pairs={{0,30},{1,31},{2,0},{3,1},{4,2},{5,3},{6,4},{7,5},{8,6},{9,7},{10,... | collective-permute-start | bytes 589832 | tf_op jit(solution)/shard_map/ppermute | solution.py:14
  177.7 14.9 %collective-permute-start.13 = (bf16[24,4096]{1,0:T(8,128)(2,1)S(1)}, bf16[24,4096]{1,0:T(8,128)(2,1)S(1)}, u32[]{:S(2)}, u32[]{:S(2)}) collective-permute-start(bf16[24,4096]{1,0:T(8,128)(2,1)S(1)} %get-tuple-element.18), channel_id=1, source_target_pairs={{0,4},{1,5},{2,6},{3,7},{4,8},{5,9},{6,10},{7,11},{8,12},{9,13},{1... | collective-permute-start | bytes 589832 | tf_op jit(solution)/shard_map/ppermute | solution.py:14
  182.7 12.8 %collective-permute-start.12 = (bf16[24,4096]{1,0:T(8,128)(2,1)S(1)}, bf16[24,4096]{1,0:T(8,128)(2,1)S(1)}, u32[]{:S(2)}, u32[]{:S(2)}) collective-permute-start(bf16[24,4096]{1,0:T(8,128)(2,1)S(1)} %get-tuple-element.15), channel_id=1, source_target_pairs={{0,28},{1,29},{2,30},{3,31},{4,0},{5,1},{6,2},{7,3},{8,4},{9,5},{1... | collective-permute-start | bytes 589832 | tf_op jit(solution)/shard_map/ppermute | solution.py:14
  185.1 10.9 %collective-permute-start.17 = (bf16[8,4096]{1,0:T(8,128)(2,1)S(1)}, bf16[8,4096]{1,0:T(8,128)(2,1)S(1)}, u32[]{:S(2)}, u32[]{:S(2)}) collective-permute-start(bf16[8,4096]{1,0:T(8,128)(2,1)S(1)} %slice.189), channel_id=1, source_target_pairs={{0,6},{1,7},{2,8},{3,9},{4,10},{5,11},{6,12},{7,13},{8,14},{9,15},... | collective-permute-start | bytes 196616 | tf_op jit(solution)/shard_map/ppermute | solution.py:14
  196.0 11.7 %collective-permute-start.18 = (bf16[8,4096]{1,0:T(8,128)(2,1)S(1)}, bf16[8,4096]{1,0:T(8,128)(2,1)S(1)}, u32[]{:S(2)}, u32[]{:S(2)}) collective-permute-start(bf16[8,4096]{1,0:T(8,128)(2,1)S(1)} %fusion.8), channel_id=1, source_target_pairs={{0,10},{1,11},{2,12},{3,13},{4,14},{5,15},{6,16},{7,17},{8,18},{9,... | collective-permute-start | bytes 196616 | tf_op jit(solution)/shard_map/ppermute | solution.py:14
  204.6 10.6 %collective-permute-start.16 = (bf16[8,4096]{1,0:T(8,128)(2,1)S(1)}, bf16[8,4096]{1,0:T(8,128)(2,1)S(1)}, u32[]{:S(2)}, u32[]{:S(2)}) collective-permute-start(bf16[8,4096]{1,0:T(8,128)(2,1)S(1)} %slice.290), channel_id=1, source_target_pairs={{0,22},{1,23},{2,24},{3,25},{4,26},{5,27},{6,28},{7,29},{8,30},{9,... | collective-permute-start | bytes 196616 | tf_op jit(solution)/shard_map/ppermute | solution.py:14
  (1 other events, 6.5 us)
